TPU v7x, 128 devices: a whole 4x4x4 slice. The times are simulated.
128 devices in a mesh: depth: 16 (over x, y), tile: 8 (over z, core).
Axes of the slice: x: 4, y: 4, z: 4, core: 2. Of those that a mesh axis runs over, the one named last changes fastest.
Arguments:
- measured: float32 [64, 2048, 1024], P('depth', 'tile'), may hold values from 0.1 to 3
- estimate: float32 [64, 2048, 1024], P('depth', 'tile'), may hold values from 0.5 to 2
- extinction: float32 [64, 2048, 1024], P('depth', 'tile'), may hold values from 0.002 to 0.05
- psf_rows: float32 [16, 65], replicated, may hold values from 0.05 to 1
- psf_cols: float32 [16, 65], replicated, may hold values from 0.05 to 1
- stratum: int32 [64], P('depth'), may hold values from 0 to 15
- seam_flags: int32 [7], replicated, may hold values 0 or 1
Outputs:
- updated: float32 [64, 2048, 1024], P('depth', 'tile')
- projection: float32 [2048, 1024], P('tile')
All inputs are finite; a program needn't handle non-finite values.
Results may differ from a plain program's by a relative error of at most 0.000073.
Values sent between devices are 32-bit elements; how exact they have to be, the bound alone decides.
No kernel may reach another device: no remote copies, remote signals or barrier semaphores. Data moves between devices by JAX's collectives and lax.ppermute only.
A program may use at most 128 MiB of HBM per device.

v0:
```python
import jax
import jax.numpy as jnp
from jax import lax
from jax.sharding import PartitionSpec as P


def carried_in(part, axis, combine, identity):
    place = lax.axis_index(axis)
    gathered = lax.all_gather(part, axis)
    state = jnp.zeros_like(part) + jnp.asarray(identity, part.dtype)

    def one(hop, state):
        return combine(state, lax.dynamic_index_in_dim(gathered, hop, 0, False))

    return lax.fori_loop(0, place, one, state)


def with_halo(cells, sides, width):
    for axis, dim in sides:
        count = lax.axis_size(axis)
        ends = count - 1
        head = lax.slice_in_dim(cells, 0, width, axis=dim)
        tail = lax.slice_in_dim(cells, cells.shape[dim] - width, cells.shape[dim], axis=dim)
        cells = jnp.concatenate(
            [
                lax.ppermute(tail, axis, [(i, (i + 1) % count) for i in range(ends)]),
                cells,
                lax.ppermute(head, axis, [((i + 1) % count, i) for i in range(ends)]),
            ],
            axis=dim,
        )
    return cells


def band_matrix(kernel, offsets):
    length = kernel.shape[0]
    result = jnp.zeros(offsets.shape, jnp.float32)
    for index in range(length):
        result = jnp.where(offsets == index, kernel[index], result)
    return result


def banded(kernel, row_count, col_count):
    offsets = (
        jnp.arange(col_count, dtype=jnp.int32)[None, :]
        - jnp.arange(row_count, dtype=jnp.int32)[:, None]
    )
    return band_matrix(kernel, offsets)


def lateral_apply(data, kernel, half_width):
    row_total, col_total = data.shape
    block_width = min(128, col_total)
    block_count = col_total // block_width
    padded = jnp.pad(data, ((0, 0), (block_width, block_width)))
    blocks = padded.reshape(row_total, block_count + 2, block_width)
    windows = jnp.concatenate(
        [blocks[:, :block_count], blocks[:, 1 : block_count + 1], blocks[:, 2:]], axis=2
    )
    sources = jnp.arange(3 * block_width, dtype=jnp.int32)[:, None]
    targets = jnp.arange(block_width, dtype=jnp.int32)[None, :]
    offsets = sources - targets - block_width + half_width
    matrix = band_matrix(kernel, offsets)
    result_blocks = jnp.einsum("rnk,kc->rnc", windows, matrix, precision=lax.Precision.HIGHEST)
    return result_blocks.reshape(row_total, col_total)


def combine(earlier, later):
    return earlier + later


def on_device(measured, estimate, extinction, psf_rows, psf_cols, stratum, seam_flags):
    planes, row_count, col_count = measured.shape
    half_width = (psf_rows.shape[1] - 1) // 2
    highest = lax.Precision.HIGHEST
    running = jnp.zeros(extinction.shape[1:], jnp.float32)
    prefixes = []
    for plane in range(planes):
        prefixes.append(running)
        running = running + extinction[plane]
    above = carried_in(running, "depth", combine, jnp.zeros_like(running))
    optical = above[None] + jnp.stack(prefixes)
    weighted = jnp.exp(-optical) * estimate
    strata = psf_rows.shape[0]
    picker = (stratum[:, None] == jnp.arange(strata, dtype=jnp.int32)[None, :]).astype(jnp.float32)
    vertical = jnp.dot(
        picker, psf_rows / jnp.sum(psf_rows, axis=1, keepdims=True), precision=highest
    )
    lateral = jnp.dot(
        picker, psf_cols / jnp.sum(psf_cols, axis=1, keepdims=True), precision=highest
    )
    padded = jnp.concatenate(
        [jnp.zeros((1,), jnp.float32), seam_flags.astype(jnp.float32), jnp.zeros((1,), jnp.float32)]
    )
    flags = lax.dynamic_slice_in_dim(padded, lax.axis_index("tile"), 2)

    def rim_scale(width):
        column = jnp.concatenate(
            [
                flags[0] * jnp.ones((width,), jnp.float32),
                jnp.ones((row_count,), jnp.float32),
                flags[1] * jnp.ones((width,), jnp.float32),
            ]
        )
        return column[None, :, None]

    quotients = []
    extended = with_halo(weighted, (("tile", 1),), half_width) * rim_scale(half_width)
    for plane in range(planes):
        band_rows = banded(vertical[plane], row_count, row_count + 2 * half_width)
        mixed = jnp.dot(band_rows, extended[plane], precision=highest)
        blurred = lateral_apply(mixed, lateral[plane], half_width)
        quotients.append(measured[plane] / blurred)
    quotient = with_halo(jnp.stack(quotients), (("tile", 1),), half_width) * rim_scale(half_width)
    results = []
    for plane in range(planes):
        band_back = banded(vertical[plane][::-1], row_count, row_count + 2 * half_width)
        mixed = jnp.dot(band_back, quotient[plane], precision=highest)
        spread = lateral_apply(mixed, lateral[plane][::-1], half_width)
        results.append(estimate[plane] * spread)
    updated = jnp.stack(results)
    projection = lax.pmax(jnp.max(updated, axis=0), "depth")
    return (updated, projection)


def solution(mesh):
    return jax.shard_map(
        on_device,
        mesh=mesh,
        in_specs=(
            P("depth", "tile", None),
            P("depth", "tile", None),
            P("depth", "tile", None),
            P(),
            P(),
            P("depth"),
            P(),
        ),
        out_specs=(P("depth", "tile", None), P("tile", None)),
        check_vma=False,
    )
```

profile of v0, /device:TPU:0, one launch (start us, length us, event | category | flops | bytes accessed | tf_op | source)
XLA Modules:
  0.0 1073.7 jit_solution(105203936941761167)
XLA Ops:
  7.3 4.1 slice_add_fusion
  30.4 94.8 %all-gather.2.cloned.1.call-done = f32[16,256,1024]{2,1,0:T(8,128)} async-done(((f32[1,256,1024]{2,1,0:T(8,128)}), f32[16,256,1024]{2,1,0:T(8,128)}) %all-gather.2.cloned.1.call-update) | async-done | bytes 16777232 | tf_op jit(solution)/shard_map/all_gather | solution.py:9
  125.3 3.6 fusion.2
  130.3 3.2 collective-permute-start
  138.9 43.6 %fusion.58 = f32[256,1024]{0,1:T(8,128)S(1)} fusion(f32[4,320,1024]{2,1,0:T(8,128)S(1)} %maximum_multiply_fusion, f32[]{:T(128)} %bitcast.65, f32[]{:T(128)} %bitcast.64, f32[]{:T(128)} %bitcast.63, f32[]{:T(128)} %bitcast.62, f32[]{:T(128)} %bitcast.61, f32[]{:T(128)} %bitcast.60, f32[]{:T(128)} %bitcast.59, f32[]{:T(128)} %bitcast.58, f32[]{:T(128)} %bitcast.57, ...), kind=kOutput, calls=%fused_computation.71 | convolution fusion | flops 1017364480 | bytes 2359556
  185.9 46.2 %fusion.3 = f32[256,8,128]{0,2,1:T(8,128)} fusion(f32[256,8,128]{2,0,1:T(8,128)S(1)} %copy-done.10, f32[256,8,128]{2,0,1:T(8,128)} %copy.122, f32[256,8,128]{2,0,1:T(8,128)S(1)} %copy.121, f32[]{:T(128)} %bitcast.134, f32[]{:T(128)} %bitcast.133, f32[]{:T(128)} %bitcast.132, f32[]{:T(128)} %bitcast.131, f32[]{:T(128)} %bitcast.130, f32[]{:T(128)} %bitcast.129, ...), kind=kOutput, calls=%fused_computation.8 | convolution fusion | flops 1216020480 | bytes 4194564 | tf_op jit(solution)/shard_map/rnk,kc->rnc/dot_general | solution.py:64
  232.2 1.6 copy.85
  233.7 44.7 %fusion.57 = f32[256,1024]{0,1:T(8,128)S(1)} fusion(f32[4,320,1024]{2,1,0:T(8,128)} %copy-done, f32[]{:T(128)} %bitcast.201, f32[]{:T(128)} %bitcast.200, f32[]{:T(128)} %bitcast.199, f32[]{:T(128)} %bitcast.198, f32[]{:T(128)} %bitcast.197, f32[]{:T(128)} %bitcast.196, f32[]{:T(128)} %bitcast.195, f32[]{:T(128)} %bitcast.194, f32[]{:T(128)} %bitcast.193, ...), kind=kOutput, calls=%fused_computation.69 | convolution fusion | flops 1017364480 | bytes 2392576
  278.5 1.3 fusion.4939
  279.8 2.5 copy.126
  284.0 47.1 %fusion.9 = f32[256,8,128]{0,2,1:T(8,128)} fusion(f32[256,8,128]{2,0,1:T(8,128)} %copy.126, f32[256,8,128]{2,0,1:T(8,128)} %copy.125, f32[256,8,128]{2,0,1:T(8,128)S(1)} %copy.124, f32[]{:T(128)} %bitcast.268, f32[]{:T(128)} %bitcast.267, f32[]{:T(128)} %bitcast.266, f32[]{:T(128)} %bitcast.265, f32[]{:T(128)} %bitcast.264, f32[]{:T(128)} %bitcast.263, ...), kind=kOutput, calls=%fused_computation.14 | convolution fusion | flops 1216020480 | bytes 4194564 | tf_op jit(solution)/shard_map/rnk,kc->rnc/dot_general | solution.py:64
  331.1 1.6 copy.90
  332.6 45.3 %fusion.55 = f32[256,1024]{0,1:T(8,128)S(1)} fusion(f32[4,320,1024]{2,1,0:T(8,128)} %copy-done, f32[]{:T(128)} %bitcast.469, f32[]{:T(128)} %bitcast.468, f32[]{:T(128)} %bitcast.467, f32[]{:T(128)} %bitcast.466, f32[]{:T(128)} %bitcast.465, f32[]{:T(128)} %bitcast.464, f32[]{:T(128)} %bitcast.463, f32[]{:T(128)} %bitcast.462, f32[]{:T(128)} %bitcast.461, ...), kind=kOutput, calls=%fused_computation.65 | convolution fusion | flops 1017364480 | bytes 2392576
  378.1 1.7 fusion.4941
  379.8 2.5 copy.132
  382.3 2.5 copy.131
  386.2 47.1 %fusion.21 = f32[256,8,128]{0,2,1:T(8,128)} fusion(f32[256,8,128]{2,0,1:T(8,128)} %copy.132, f32[256,8,128]{2,0,1:T(8,128)} %copy.131, f32[256,8,128]{2,0,1:T(8,128)} %copy.130, f32[]{:T(128)} %bitcast.536, f32[]{:T(128)} %bitcast.535, f32[]{:T(128)} %bitcast.534, f32[]{:T(128)} %bitcast.533, f32[]{:T(128)} %bitcast.532, f32[]{:T(128)} %bitcast.531, ...), kind=kOutput, calls=%fused_computation.26 | convolution fusion | flops 1216020480 | bytes 4194564 | tf_op jit(solution)/shard_map/rnk,kc->rnc/dot_general | solution.py:64
  433.2 1.6 copy.100
  434.8 45.0 %fusion.56 = f32[256,1024]{0,1:T(8,128)S(1)} fusion(f32[4,320,1024]{2,1,0:T(8,128)} %copy-done, f32[]{:T(128)} %bitcast.335, f32[]{:T(128)} %bitcast.334, f32[]{:T(128)} %bitcast.333, f32[]{:T(128)} %bitcast.332, f32[]{:T(128)} %bitcast.331, f32[]{:T(128)} %bitcast.330, f32[]{:T(128)} %bitcast.329, f32[]{:T(128)} %bitcast.328, f32[]{:T(128)} %bitcast.327, ...), kind=kOutput, calls=%fused_computation.67 | convolution fusion | flops 1017364480 | bytes 2392576
  479.9 1.8 fusion.4940
  481.7 2.6 copy.129
  484.3 2.5 copy.128
  486.8 2.5 copy.127
  489.4 47.2 %fusion.15 = f32[256,8,128]{0,2,1:T(8,128)} fusion(f32[256,8,128]{2,0,1:T(8,128)} %copy.129, f32[256,8,128]{2,0,1:T(8,128)} %copy.128, f32[256,8,128]{2,0,1:T(8,128)} %copy.127, f32[]{:T(128)} %bitcast.402, f32[]{:T(128)} %bitcast.401, f32[]{:T(128)} %bitcast.400, f32[]{:T(128)} %bitcast.399, f32[]{:T(128)} %bitcast.398, f32[]{:T(128)} %bitcast.397, ...), kind=kOutput, calls=%fused_computation.20 | convolution fusion | flops 1216020480 | bytes 4194564 | tf_op jit(solution)/shard_map/rnk,kc->rnc/dot_general | solution.py:64
  536.5 2.5 copy.95
  539.1 3.5 slice_divide_fusion.3
  543.9 5.4 collective-permute-start.2
  549.3 1.5 collective-permute-done.2
  550.8 1.9 maximum_multiply_fusion.1
  552.6 43.6 %fusion.54 = f32[256,1024]{0,1:T(8,128)S(1)} fusion(f32[4,320,1024]{2,1,0:T(8,128)S(1)} %maximum_multiply_fusion.1, f32[]{:T(128)} %bitcast.65, f32[]{:T(128)} %bitcast.64, f32[]{:T(128)} %bitcast.63, f32[]{:T(128)} %bitcast.62, f32[]{:T(128)} %bitcast.61, f32[]{:T(128)} %bitcast.60, f32[]{:T(128)} %bitcast.59, f32[]{:T(128)} %bitcast.58, f32[]{:T(128)} %bitcast.57, ...), kind=kOutput, calls=%fused_computation.63 | convolution fusion | flops 1017364480 | bytes 2359556
  596.2 44.1 %fusion.53 = f32[256,1024]{0,1:T(8,128)} fusion(f32[4,320,1024]{2,1,0:T(8,128)S(1)} %maximum_multiply_fusion.1, f32[]{:T(128)} %bitcast.201, f32[]{:T(128)} %bitcast.200, f32[]{:T(128)} %bitcast.199, f32[]{:T(128)} %bitcast.198, f32[]{:T(128)} %bitcast.197, f32[]{:T(128)} %bitcast.196, f32[]{:T(128)} %bitcast.195, f32[]{:T(128)} %bitcast.194, ...), kind=kOutput, calls=%fused_computation.61 | convolution fusion | flops 1017364480 | bytes 2359556
  640.3 44.7 %fusion.52 = f32[256,1024]{0,1:T(8,128)} fusion(f32[4,320,1024]{2,1,0:T(8,128)S(1)} %maximum_multiply_fusion.1, f32[]{:T(128)} %bitcast.335, f32[]{:T(128)} %bitcast.334, f32[]{:T(128)} %bitcast.333, f32[]{:T(128)} %bitcast.332, f32[]{:T(128)} %bitcast.331, f32[]{:T(128)} %bitcast.330, f32[]{:T(128)} %bitcast.329, f32[]{:T(128)} %bitcast.328, ...), kind=kOutput, calls=%fused_computation.59 | convolution fusion | flops 1017364480 | bytes 2359556
  685.0 45.3 %fusion.51 = f32[256,1024]{0,1:T(8,128)} fusion(f32[4,320,1024]{2,1,0:T(8,128)S(1)} %maximum_multiply_fusion.1, f32[]{:T(128)} %bitcast.469, f32[]{:T(128)} %bitcast.468, f32[]{:T(128)} %bitcast.467, f32[]{:T(128)} %bitcast.466, f32[]{:T(128)} %bitcast.465, f32[]{:T(128)} %bitcast.464, f32[]{:T(128)} %bitcast.463, f32[]{:T(128)} %bitcast.462, ...), kind=kOutput, calls=%fused_computation.57 | convolution fusion | flops 1017364480 | bytes 2359556
  730.8 1.3 copy.135
  733.7 46.3 %fusion.27 = f32[256,8,128]{0,2,1:T(8,128)} fusion(f32[256,8,128]{2,0,1:T(8,128)S(1)} %copy-done.7, f32[256,8,128]{2,0,1:T(8,128)} %copy.134, f32[256,8,128]{2,0,1:T(8,128)S(1)} %copy.133, f32[]{:T(128)} %bitcast.134, f32[]{:T(128)} %bitcast.133, f32[]{:T(128)} %bitcast.132, f32[]{:T(128)} %bitcast.131, f32[]{:T(128)} %bitcast.130, f32[]{:T(128)} %bitcast.129, ...), kind=kOutput, calls=%fused_computation.32 | convolution fusion | flops 1216020480 | bytes 4194564 | tf_op jit(solution)/shard_map/rnk,kc->rnc/dot_general | solution.py:64
  780.1 2.5 copy.105
  786.0 46.9 %fusion.33 = f32[256,8,128]{0,2,1:T(8,128)} fusion(f32[256,8,128]{2,0,1:T(8,128)S(1)} %copy-done.8, f32[256,8,128]{2,0,1:T(8,128)} %copy.137, f32[256,8,128]{2,0,1:T(8,128)S(1)} %copy.136, f32[]{:T(128)} %bitcast.268, f32[]{:T(128)} %bitcast.267, f32[]{:T(128)} %bitcast.266, f32[]{:T(128)} %bitcast.265, f32[]{:T(128)} %bitcast.264, f32[]{:T(128)} %bitcast.263, ...), kind=kOutput, calls=%fused_computation.38 | convolution fusion | flops 1216020480 | bytes 4194564 | tf_op jit(solution)/shard_map/rnk,kc->rnc/dot_general | solution.py:64
  832.9 2.5 copy.110
  837.2 1.3 copy.140
  838.9 46.9 %fusion.39 = f32[256,8,128]{0,2,1:T(8,128)} fusion(f32[256,8,128]{2,0,1:T(8,128)S(1)} %copy-done.9, f32[256,8,128]{2,0,1:T(8,128)} %copy.140, f32[256,8,128]{2,0,1:T(8,128)S(1)} %copy.139, f32[]{:T(128)} %bitcast.402, f32[]{:T(128)} %bitcast.401, f32[]{:T(128)} %bitcast.400, f32[]{:T(128)} %bitcast.399, f32[]{:T(128)} %bitcast.398, f32[]{:T(128)} %bitcast.397, ...), kind=kOutput, calls=%fused_computation.44 | convolution fusion | flops 1216020480 | bytes 4194564 | tf_op jit(solution)/shard_map/rnk,kc->rnc/dot_general | solution.py:64
  885.8 2.5 copy.115
  890.1 1.4 copy.143
  892.7 47.0 %fusion.45 = f32[256,8,128]{0,2,1:T(8,128)} fusion(f32[256,8,128]{2,0,1:T(8,128)} %copy.144, f32[256,8,128]{2,0,1:T(8,128)} %copy.143, f32[256,8,128]{2,0,1:T(8,128)} %copy.142, f32[]{:T(128)} %bitcast.536, f32[]{:T(128)} %bitcast.535, f32[]{:T(128)} %bitcast.534, f32[]{:T(128)} %bitcast.533, f32[]{:T(128)} %bitcast.532, f32[]{:T(128)} %bitcast.531, ...), kind=kOutput, calls=%fused_computation.50 | convolution fusion | flops 1216020480 | bytes 4194564 | tf_op jit(solution)/shard_map/rnk,kc->rnc/dot_general | solution.py:64
  939.7 2.5 copy.120
  942.2 5.3 maximum_bitcast_fusion
  947.6 4.8 pad_maximum_fusion
  952.3 111.8 %all-reduce.10.cloned.1.call-done = f32[256,1024]{1,0:T(8,128)} async-done(((f32[256,1024]{1,0:T(8,128)}), f32[256,1024]{1,0:T(8,128)}) %all-reduce.10.cloned.1.call-update) | async-done | bytes 1048592 | tf_op jit(solution)/shard_map/pmax | solution.py:122
  1064.2 2.3 copy.160
  (113 shorter events, 44.3 us)
Async XLA Ops:
  7.2 4.2 copy-start.13
  7.2 4.3 copy-start.11
  7.2 4.4 copy-start.12
  7.2 5.3 copy-start.14
  7.2 118.0 %all-gather.2.cloned.1.call-start = ((), (), s32[]{:S(2)}) async-start(), calls=%async_computation | async-start | bytes 17825792 | tf_op jit(solution)/shard_map/all_gather | solution.py:9
  11.4 1052.8 %all-reduce.10.cloned.1.call-start = ((), (), s32[]{:S(2)}) async-start(), calls=%async_computation.1 | async-start | bytes 2097152 | tf_op jit(solution)/shard_map/pmax | solution.py:122
  129.0 8.8 collective-permute-start.1
  130.3 7.5 collective-permute-start
  138.9 43.6 %copy-start = (f32[4,320,1024]{2,1,0:T(8,128)}, f32[4,320,1024]{2,1,0:T(8,128)S(1)}, u32[]{:S(2)}) copy-start(f32[4,320,1024]{2,1,0:T(8,128)S(1)} %maximum_multiply_fusion) | copy-start | bytes 15728644
  184.3 1.6 copy-start.10
  542.6 6.7 collective-permute-start.3
  543.9 6.9 collective-permute-start.2
  732.1 1.6 copy-start.7
  733.7 48.9 %copy-start.6 = (f32[256,1024]{0,1:T(8,128)S(1)}, f32[256,1024]{0,1:T(8,128)}, u32[]{:S(2)}) copy-start(f32[256,1024]{0,1:T(8,128)} %fusion.53) | copy-start | bytes 3145732
  784.4 1.6 copy-start.8
  786.0 49.4 %copy-start.5 = (f32[256,1024]{0,1:T(8,128)S(1)}, f32[256,1024]{0,1:T(8,128)}, u32[]{:S(2)}) copy-start(f32[256,1024]{0,1:T(8,128)} %fusion.52) | copy-start | bytes 3145732
  837.2 1.7 copy-start.9
  838.8 49.5 %copy-start.4 = (f32[256,1024]{0,1:T(8,128)S(1)}, f32[256,1024]{0,1:T(8,128)}, u32[]{:S(2)}) copy-start(f32[256,1024]{0,1:T(8,128)} %fusion.51) | copy-start | bytes 3145732
  892.7 49.5 %copy-start.1 = (f32[1,256,1024]{2,1,0:T(8,128)S(1)}, f32[1,256,1024]{2,1,0:T(8,128)}, u32[]{:S(2)}) copy-start(f32[1,256,1024]{2,1,0:T(8,128)} %copy.105) | copy-start | bytes 3145732
  892.7 49.5 %copy-start.2 = (f32[1,256,1024]{2,1,0:T(8,128)S(1)}, f32[1,256,1024]{2,1,0:T(8,128)}, u32[]{:S(2)}) copy-start(f32[1,256,1024]{2,1,0:T(8,128)} %copy.110) | copy-start | bytes 3145732
  892.7 49.5 %copy-start.3 = (f32[1,256,1024]{2,1,0:T(8,128)S(1)}, f32[1,256,1024]{2,1,0:T(8,128)}, u32[]{:S(2)}) copy-start(f32[1,256,1024]{2,1,0:T(8,128)} %copy.115) | copy-start | bytes 3145732
Sparse Core Ops, SparseCore 0:
  11.5 113.6 all-gather.1
  947.7 116.4 all-reduce.9
where the time goes:
time: 1090 us; the launch traced here: 1070 us
  matrix products  731 us (67%)
  waiting for transfers between devices  208 us (19%)
  local copies, waits for them, and re-layouts  83.3 us (8%)
  other arithmetic  24.6 us (2%)
  between operations  15 us (1%)
  starting transfers between devices  11.3 us (1%)
    dot_general x8, matrix products, lateral_apply(): jnp.einsum('rnk,kc->rnc', windows, matrix, precision=lax.Precision.HIGHEST)  375 us
    unnamed x8, matrix products  356 us
    pmax x1, waiting for transfers between devices, on_device(): projection = lax.pmax(jnp.max(updated, axis=0), 'depth')  112 us
    all_gather x1, waiting for transfers between devices, carried_in(): gathered = lax.all_gather(part, axis)  94.8 us
    unnamed x55, local copies, waits for them, and re-layouts  36.3 us
  transfers between devices with their start and end apart: 6, of which 3 were waited for; matrix products, arithmetic and copies ran while one was open for 3% of the time, Pallas kernels for 0%

commit v1 on v0

v1 whole, which is shorter than its diff:
```python
import functools

import jax
import jax.numpy as jnp
from jax import lax
from jax.experimental import pallas as pl
from jax.experimental.pallas import tpu as pltpu
from jax.sharding import PartitionSpec as P

SIDE = 4
HALF = 32
TAPS = 65
BF = jnp.bfloat16
F32 = jnp.float32
VMEM_LIMIT = 56 * 1024 * 1024


def params(**kw):
    return pltpu.CompilerParams(vmem_limit_bytes=VMEM_LIMIT, **kw)


def whole():
    return pl.BlockSpec(memory_space=pltpu.VMEM)


def smem():
    return pl.BlockSpec(memory_space=pltpu.SMEM)


def place():
    depth = lax.axis_index("depth")
    tile = lax.axis_index("tile")
    x, y, core = depth // SIDE, depth % SIDE, tile % 2
    first = jnp.where(core == 0, y, x)
    second = jnp.where(core == 0, x, y)
    return first, second, core, tile


def turn(value, k):
    return lax.rem(value + (k + 2 * SIDE), SIDE)


def perm(stage, k, tiles):
    pairs = []
    for x in range(SIDE):
        for y in range(SIDE):
            for tile in range(tiles):
                along_y = (tile % 2 == 0) == (stage == 0)
                tx, ty = (x, (y + k) % SIDE) if along_y else ((x + k) % SIDE, y)
                pairs.append(((x * SIDE + y) * tiles + tile, (tx * SIDE + ty) * tiles + tile))
    return pairs


def exchange(stage, sign, parts):
    tiles = lax.axis_size("tile")
    got = [parts[0]] + [None] * (SIDE - 1)
    for k in (2, 1, 3):
        got[k] = lax.ppermute(parts[k], ("depth", "tile"), perm(stage, sign * k, tiles))
    return got


def split(value):
    high = value.astype(BF)
    return high, (value - high.astype(F32)).astype(BF)


def rows_at(index, size):
    return pl.ds(pl.multiple_of(index * size, size), size)


def sums_kernel(ext, est_top, est_bot, mea_top, mea_bot, up, down, o0, o1, o2, o3, acc):
    plane = pl.program_id(0)
    first, _, _, _ = place()
    rim = 2 * HALF
    rows = acc.shape[0]

    @pl.when(plane == 0)
    def _():
        acc[...] = jnp.zeros_like(acc)

    up[0, :rim] = jnp.exp(-acc[:rim]) * est_top[0]
    down[0, :rim] = jnp.exp(-acc[rows - rim :]) * est_bot[0]
    up[0, rim:] = mea_top[0]
    down[0, rim:] = mea_bot[0]
    acc[...] += ext[0]

    @pl.when(plane == pl.num_programs(0) - 1)
    def _():
        for k, out in enumerate((o0, o1, o2, o3)):
            out[...] = acc[rows_at(turn(first, k), rows // SIDE)]


def sums(extinction, estimate, measured):
    planes, rows, cols = extinction.shape
    rim, quarter = 2 * HALF, rows // SIDE
    last = rows // rim - 1
    plane_block = pl.BlockSpec((1, rim + HALF, cols), lambda p: (p, 0, 0))
    part = pl.BlockSpec((quarter, cols), lambda p: (0, 0))
    return pl.pallas_call(
        sums_kernel,
        grid=(planes,),
        in_specs=[
            pl.BlockSpec((1, rows, cols), lambda p: (p, 0, 0)),
            pl.BlockSpec((1, rim, cols), lambda p: (p, 0, 0)),
            pl.BlockSpec((1, rim, cols), lambda p: (p, last, 0)),
            pl.BlockSpec((1, HALF, cols), lambda p: (p, 0, 0)),
            pl.BlockSpec((1, HALF, cols), lambda p: (p, rows // HALF - 1, 0)),
        ],
        out_specs=[plane_block, plane_block] + [part] * SIDE,
        out_shape=[jax.ShapeDtypeStruct((planes, rim + HALF, cols), F32)] * 2
        + [jax.ShapeDtypeStruct((quarter, cols), F32)] * SIDE,
        scratch_shapes=[pltpu.VMEM((rows, cols), F32)],
        compiler_params=params(),
    )(extinction, estimate, estimate, measured, measured)


def local(kernel, shapes, args, scratch=(), specs=None):
    out = [jax.ShapeDtypeStruct(s, F32) for s in shapes]
    return pl.pallas_call(
        kernel,
        in_specs=specs or [whole()] * len(args),
        out_specs=[whole()] * len(out),
        out_shape=out,
        scratch_shapes=list(scratch),
        compiler_params=params(),
    )(*args)


def regroup_kernel(r0, r1, r2, r3, b0, b1, b2, b3):
    first, second, _, _ = place()
    rows = r0.shape[0] // SIDE
    for j, source in enumerate((r0, r1, r2, r3)):
        for k, out in enumerate((b0, b1, b2, b3)):
            out[turn(first, -j)] = source[rows_at(turn(second, k), rows)]


def scan_kernel(c0, c1, c2, c3, d0, d1, d2, d3, buf):
    _, second, core, _ = place()

    def slot(j, k):
        g = turn(second, -k)
        return jnp.where(core == 0, g * SIDE + j, j * SIDE + g)

    for k, source in enumerate((c0, c1, c2, c3)):
        for j in range(SIDE):
            buf[slot(j, k)] = source[j]
    total = jnp.zeros(buf.shape[1:], F32)
    for d in range(SIDE * SIDE):
        value = buf[d]
        buf[d] = total
        total = total + value
    for k, out in enumerate((d0, d1, d2, d3)):
        for j in range(SIDE):
            out[j] = buf[slot(j, k)]


def ungroup_kernel(e0, e1, e2, e3, h0, h1, h2, h3):
    first, second, _, _ = place()
    rows = e0.shape[1]
    for m, source in enumerate((e0, e1, e2, e3)):
        for k, out in enumerate((h0, h1, h2, h3)):
            out[rows_at(turn(second, m), rows)] = source[turn(first, -k)]


def place_kernel(sign, i0, i1, i2, i3, out):
    first, _, _, _ = place()
    rows = i0.shape[0]
    for k, source in enumerate((i0, i1, i2, i3)):
        out[rows_at(turn(first, sign * k), rows)] = source[...]


def above_of(parts):
    quarter, cols = parts[0].shape
    small = quarter // SIDE
    got = exchange(0, 1, parts)
    packed = local(regroup_kernel, [(SIDE, small, cols)] * SIDE, got)
    got = exchange(1, 1, packed)
    scanned = local(
        scan_kernel,
        [(SIDE, small, cols)] * SIDE,
        got,
        [pltpu.VMEM((SIDE * SIDE, small, cols), F32)],
    )
    got = exchange(1, -1, scanned)
    back = local(ungroup_kernel, [(quarter, cols)] * SIDE, got)
    got = exchange(0, -1, back)
    return local(functools.partial(place_kernel, 1), [(quarter * SIDE, cols)], got)[0]


def max_split_kernel(r0, r1, r2, r3, b0, b1, b2, b3):
    _, second, _, _ = place()
    rows = r0.shape[0] // SIDE
    for k, out in enumerate((b0, b1, b2, b3)):
        at = rows_at(turn(second, k), rows)
        out[...] = jnp.maximum(jnp.maximum(r0[at], r1[at]), jnp.maximum(r2[at], r3[at]))


def max_kernel(r0, r1, r2, r3, out):
    out[...] = jnp.maximum(jnp.maximum(r0[...], r1[...]), jnp.maximum(r2[...], r3[...]))


def join_kernel(stage, i0, i1, i2, i3, out):
    first, second, _, _ = place()
    rows = i0.shape[0]
    for k, source in enumerate((i0, i1, i2, i3)):
        out[rows_at(turn(second if stage else first, -k), rows)] = source[...]


def highest(parts):
    quarter, cols = parts[0].shape
    small = quarter // SIDE
    got = exchange(0, 1, parts)
    packed = local(max_split_kernel, [(small, cols)] * SIDE, got)
    got = exchange(1, 1, packed)
    top = local(max_kernel, [(small, cols)], got)[0]
    got = exchange(1, 1, [top] * SIDE)
    joined = local(functools.partial(join_kernel, 1), [(quarter, cols)], got)[0]
    got = exchange(0, 1, [joined] * SIDE)
    return local(functools.partial(join_kernel, 0), [(quarter * SIDE, cols)], got)[0]


def bands_kernel(stratum, taps, v_ref, l_ref):
    def toeplitz(row, count, shift):
        line = taps[0, row : row + 1]
        line = line / jnp.sum(line, axis=1, keepdims=True)
        wide = jnp.broadcast_to(line, (count, line.shape[1]))
        return pltpu.roll(wide, shift, 1, stride=1, stride_axis=0)

    for way in range(2):
        band = toeplitz(way, v_ref.shape[3], 0)
        v_ref[0, way, 0], v_ref[0, way, 1] = split(band)
        ring = toeplitz(3 - way, 256, 256 - HALF)
        k = lax.broadcasted_iota(jnp.int32, ring.shape, 0)
        n = lax.broadcasted_iota(jnp.int32, ring.shape, 1)
        zero = jnp.zeros_like(ring)
        main = jnp.where(jnp.abs(n - k) <= HALF, ring, zero)
        left = jnp.where(k - n > HALF, ring, zero)[128:]
        right = jnp.where(n - k > HALF, ring, zero)[:128]
        for at, part in ((0, left), (128, main), (384, right)):
            high, low = split(part)
            l_ref[0, way, 0, at : at + part.shape[0]] = high
            l_ref[0, way, 1, at : at + part.shape[0]] = low


def bands(psf_rows, psf_cols, stratum):
    planes = stratum.shape[0]
    taps = jnp.stack([psf_rows, psf_rows[:, ::-1], psf_cols, psf_cols[:, ::-1]], axis=1)
    taps = jnp.pad(taps, ((0, 0), (0, 0), (0, 256 - TAPS)))
    return pl.pallas_call(
        bands_kernel,
        grid_spec=pltpu.PrefetchScalarGridSpec(
            num_scalar_prefetch=1,
            grid=(planes,),
            in_specs=[pl.BlockSpec((1, 4, 256), lambda p, s: (s[p], 0, 0))],
            out_specs=[
                pl.BlockSpec((1, 2, 2, 192, 256), lambda p, s: (p, 0, 0, 0, 0)),
                pl.BlockSpec((1, 2, 2, 512, 256), lambda p, s: (p, 0, 0, 0, 0)),
            ],
        ),
        out_shape=[
            jax.ShapeDtypeStruct((planes, 2, 2, 192, 256), BF),
            jax.ShapeDtypeStruct((planes, 2, 2, 512, 256), BF),
        ],
        compiler_params=params(),
    )(stratum, taps)


def dot(a, b):
    return jnp.dot(a, b, preferred_element_type=F32)


def dot3(a_high, a_low, b_high, b_low):
    return dot(a_high, b_high) + (dot(a_high, b_low) + dot(a_low, b_high))


def step_kernel(
    seams, ext, est, mea, above, above_top, above_bot, rim_top, rim_bot, v_ref, l_ref,
    upd, o0, o1, o2, o3, optical, top, wh, wl, mh, ml, qh, ql, nh, nl,
):
    plane = pl.program_id(0)
    first, _, _, tile = place()
    rows, cols = optical.shape
    rim = 2 * HALF
    ends = lax.axis_size("tile") - 1
    join_top = jnp.where(tile > 0, seams[jnp.maximum(tile - 1, 0)], 0) == 1
    join_bot = jnp.where(tile < ends, seams[jnp.minimum(tile, ends - 1)], 0) == 1

    @pl.when(plane == 0)
    def _():
        optical[...] = above[...]
        for ref in (mh, ml, nh, nl):
            edge = jnp.zeros((ref.shape[0], 128), BF)
            ref[:, :128] = edge
            ref[:, ref.shape[1] - 128 :] = edge

    for joined, far, packed, at in (
        (join_top, above_top, rim_top, 0),
        (join_bot, above_bot, rim_bot, rows + rim),
    ):
        value = jnp.where(joined, jnp.exp(-far[...]) * packed[0, :rim], 0.0)
        wh[at : at + rim], wl[at : at + rim] = split(value)
    for r in range(0, rows, 64):
        depth = optical[r : r + 64]
        value = jnp.exp(-depth) * est[0, r : r + 64]
        wh[rim + r : rim + r + 64], wl[rim + r : rim + r + 64] = split(value)
        optical[r : r + 64] = depth + ext[0, r : r + 64]

    def vertical(way, sh, sl, dh, dl):
        total = dh.shape[0]
        for at in range(0, total, 192):
            m = min(192, total - at)
            depth = min(256, m + rim)
            th, tl = v_ref[0, way, 0, :m, :depth], v_ref[0, way, 1, :m, :depth]
            for c in range(0, cols, 256):
                result = dot3(th, tl, sh[at : at + depth, c : c + 256], sl[at : at + depth, c : c + 256])
                dh[at : at + m, 128 + c : 384 + c], dl[at : at + m, 128 + c : 384 + c] = split(result)

    vertical(0, wh, wl, mh, ml)
    lh, ll = l_ref.at[0, 0, 0], l_ref.at[0, 0, 1]
    for c in range(0, cols, 256):
        for a, b in ((0, 160), (160, 320)):
            blurred = dot3(mh[a:b, c : c + 512], ml[a:b, c : c + 512], lh[...], ll[...])
            s = slice(c, c + 256)
            if a == 0:
                halo = jnp.where(join_top, rim_top[0, rim:, s] / blurred[:HALF], 0.0)
                inner = mea[0, : b - HALF, s] / blurred[HALF:]
                qh[:HALF, s], ql[:HALF, s] = split(halo)
                qh[HALF:b, s], ql[HALF:b, s] = split(inner)
            else:
                halo = jnp.where(join_bot, rim_bot[0, rim:, s] / blurred[b - a - HALF :], 0.0)
                inner = mea[0, a - HALF :, s] / blurred[: b - a - HALF]
                qh[b - HALF :, s], ql[b - HALF :, s] = split(halo)
                qh[a : b - HALF, s], ql[a : b - HALF, s] = split(inner)

    vertical(1, qh, ql, nh, nl)
    lh, ll = l_ref.at[0, 1, 0], l_ref.at[0, 1, 1]
    for c in range(0, cols, 256):
        s = slice(c, c + 256)
        for a in range(0, rows, 128):
            t = slice(a, a + 128)
            spread = dot3(nh[t, c : c + 512], nl[t, c : c + 512], lh[...], ll[...])
            result = est[0, t, s] * spread
            upd[0, t, s] = result
            top[t, s] = jnp.maximum(jnp.where(plane == 0, result, top[t, s]), result)

    @pl.when(plane == pl.num_programs(0) - 1)
    def _():
        for k, out in enumerate((o0, o1, o2, o3)):
            out[...] = top[rows_at(turn(first, k), rows // SIDE)]


def step(seams, ext, est, mea, above, above_top, above_bot, rim_top, rim_bot, v, l):
    planes, rows, cols = ext.shape
    rim, quarter = 2 * HALF, rows // SIDE
    stack = pl.BlockSpec((1, rows, cols), lambda p: (p, 0, 0))
    pack = pl.BlockSpec((1, rim + HALF, cols), lambda p: (p, 0, 0))
    part = pl.BlockSpec((quarter, cols), lambda p: (0, 0))
    return pl.pallas_call(
        step_kernel,
        grid=(planes,),
        in_specs=[
            smem(), stack, stack, stack, whole(), whole(), whole(), pack, pack,
            pl.BlockSpec((1,) + v.shape[1:], lambda p: (p, 0, 0, 0, 0)),
            pl.BlockSpec((1,) + l.shape[1:], lambda p: (p, 0, 0, 0, 0)),
        ],
        out_specs=[stack] + [part] * SIDE,
        out_shape=[jax.ShapeDtypeStruct((planes, rows, cols), F32)]
        + [jax.ShapeDtypeStruct((quarter, cols), F32)] * SIDE,
        scratch_shapes=[
            pltpu.VMEM((rows, cols), F32),
            pltpu.VMEM((rows, cols), F32),
            pltpu.VMEM((rows + 2 * rim, cols), BF),
            pltpu.VMEM((rows + 2 * rim, cols), BF),
            pltpu.VMEM((rows + rim, cols + 256), BF),
            pltpu.VMEM((rows + rim, cols + 256), BF),
            pltpu.VMEM((rows + rim, cols), BF),
            pltpu.VMEM((rows + rim, cols), BF),
            pltpu.VMEM((rows, cols + 256), BF),
            pltpu.VMEM((rows, cols + 256), BF),
        ],
        compiler_params=params(),
    )(seams, ext, est, mea, above, above_top, above_bot, rim_top, rim_bot, v, l)


def on_device(measured, estimate, extinction, psf_rows, psf_cols, stratum, seam_flags):
    rows = measured.shape[1]
    rim = 2 * HALF
    tiles = lax.axis_size("tile")
    onward = [(i, i + 1) for i in range(tiles - 1)]
    backward = [(i + 1, i) for i in range(tiles - 1)]
    up, down, *parts = sums(extinction, estimate, measured)
    rim_top = lax.ppermute(down, "tile", onward)
    rim_bot = lax.ppermute(up, "tile", backward)
    v, l = bands(psf_rows, psf_cols, stratum)
    above = above_of(parts)
    above_top = lax.ppermute(above[rows - rim :], "tile", onward)
    above_bot = lax.ppermute(above[:rim], "tile", backward)
    updated, *tops = step(
        seam_flags, extinction, estimate, measured, above, above_top, above_bot, rim_top, rim_bot, v, l
    )
    return updated, highest(tops)


def solution(mesh):
    return jax.shard_map(
        on_device,
        mesh=mesh,
        in_specs=(
            P("depth", "tile", None),
            P("depth", "tile", None),
            P("depth", "tile", None),
            P(),
            P(),
            P("depth"),
            P(),
        ),
        out_specs=(P("depth", "tile", None), P("tile", None)),
        check_vma=False,
    )
```

time: 1090 us -> 158 us (0.14); the launches traced: 1070 us -> 156 us
  matrix products: 731 us -> 0 us
  waiting for transfers between devices: 208 us -> 56.4 us
  local copies, waits for them, and re-layouts: 83.3 us -> 9.62 us
  Pallas kernels: 0 us -> 45.4 us
  starting transfers between devices: 11.3 us -> 43.2 us
  other arithmetic: 24.6 us -> 0.69 us
  between operations: 15 us -> 0.79 us
    dot_general x10 -> x0, matrix products: 375 us -> none  [the longest x8 375 us: lateral_apply(): jnp.einsum('rnk,kc->rnc', windows, matrix, precision=lax.Precision.HIGHEST)]
    unnamed x8 -> x0, matrix products: 356 us -> none
    pmax x1 -> x0, waiting for transfers between devices: 112 us -> none  [on_device(): projection = lax.pmax(jnp.max(updated, axis=0), 'depth')]
    all_gather x1 -> x0, waiting for transfers between devices: 94.8 us -> none  [carried_in(): gathered = lax.all_gather(part, axis)]
    ppermute x4 -> x28, waiting for transfers between devices: 1.48 us -> 56.4 us  [the longest x24 56.4 us: exchange(): lax.ppermute(parts[k], ('depth', 'tile'), perm(stage, sign * k, tiles))]
    pallas_call x0 -> x11, Pallas kernels: none -> 45.4 us  [the longest x1 18 us: step(): pl.pallas_call(step_kernel, grid=(planes,), in_specs=[smem(), stack, stac...]
    ppermute x4 -> x28, starting transfers between devices: 11.2 us -> 43.2 us  [the longest x24 35.5 us: exchange(): lax.ppermute(parts[k], ('depth', 'tile'), perm(stage, sign * k, tiles))]
    unnamed x55 -> x58, local copies, waits for them, and re-layouts: 36.3 us -> 7.55 us
  transfers between devices with their start and end apart: 6 -> 28, of which waited for: 3 -> 20; matrix products, arithmetic and copies ran while one was open for 3% -> 2% of each run, Pallas kernels for 0% -> 9%
where the time goes in v1:
time: 158 us; the launch traced here: 156 us
  waiting for transfers between devices  56.4 us (36%)
  Pallas kernels  45.4 us (29%)
  starting transfers between devices  43.2 us (27%)
  local copies, waits for them, and re-layouts  9.62 us (6%)
    ppermute x24, waiting for transfers between devices, exchange(): lax.ppermute(parts[k], ('depth', 'tile'), perm(stage, sign * k, tiles))  56.4 us
    ppermute x24, starting transfers between devices, exchange(): lax.ppermute(parts[k], ('depth', 'tile'), perm(stage, sign * k, tiles))  35.5 us
    pallas_call x1, Pallas kernels, step(): pl.pallas_call(step_kernel, grid=(planes,), in_specs=[smem(), stack, stac...  18 us
    pallas_call x8, Pallas kernels, local(): pl.pallas_call(kernel, in_specs=specs or [whole()] * len(args), out_specs...  16.5 us
    unnamed x58, local copies, waits for them, and re-layouts  7.55 us
    pallas_call x1, Pallas kernels, sums(): pl.pallas_call(sums_kernel, grid=(planes,), in_specs=[pl.BlockSpec((1, ro...  5.81 us
    pallas_call x1, Pallas kernels, bands(): pl.pallas_call(bands_kernel, grid_spec=pltpu.PrefetchScalarGridSpec(num_s...  5.03 us
    ppermute x1, starting transfers between devices, on_device(): above_top = lax.ppermute(above[rows - rim:], 'tile', onward)  3.75 us
  transfers between devices with their start and end apart: 28, of which 20 were waited for; matrix products, arithmetic and copies ran while one was open for 2% of the time, Pallas kernels for 9%

profile of v1, /device:TPU:0, one launch (start us, length us, event | category | flops | bytes accessed | tf_op | source)
XLA Modules:
  0.0 156.0 jit_solution(8000358447992140759)
XLA Ops:
  0.6 5.8 %shard_map.86 = (f32[4,96,1024]{2,1,0:T(8,128)}, f32[4,96,1024]{2,1,0:T(8,128)}, f32[64,1024]{1,0:T(8,128)}, f32[64,1024]{1,0:T(8,128)}, f32[64,1024]{1,0:T(8,128)}, /*index=5*/f32[64,1024]{1,0:T(8,128)}) custom-call(f32[4,256,1024]{2,1,0:T(8,128)} %ext.3, f32[4,256,1024]{2,1,0:T(8,128)} %est.1, f32[4,256,1024]{2,1,0:T(8,128)} %est.1, f32[4,256,1024]{2,1,0:T(8,128)} %mea.1, ...), custom_call_target="tpu_custom_call" | custom-call | tf_op jit(solution)/shard_map/pallas_call | solution.py:99
  6.5 1.4 collective-permute-start.14
  7.9 1.3 collective-permute-start.15
  9.2 2.2 %collective-permute-start = (f32[64,1024]{1,0:T(8,128)}, f32[64,1024]{1,0:T(8,128)S(1)}, u32[]{:S(2)}, u32[]{:S(2)}) collective-permute-start(f32[64,1024]{1,0:T(8,128)} %get-tuple-element.32), channel_id=1, source_target_pairs={{0,8},{1,33},{2,10},{3,35},{4,12},{5,37},{6,14},{7,39},{8,16},{9,4... | collective-permute-start | bytes 786440 | tf_op jit(solution)/shard_map/ppermute | solution.py:58
  11.3 2.9 %collective-permute-start.1 = (f32[64,1024]{1,0:T(8,128)}, f32[64,1024]{1,0:T(8,128)S(1)}, u32[]{:S(2)}, u32[]{:S(2)}) collective-permute-start(f32[64,1024]{1,0:T(8,128)} %get-tuple-element.33), channel_id=1, source_target_pairs={{0,16},{1,65},{2,18},{3,67},{4,20},{5,69},{6,22},{7,71},{8,24},{9,... | collective-permute-start | bytes 786440 | tf_op jit(solution)/shard_map/ppermute | solution.py:58
  14.2 1.3 collective-permute-start.2
  15.6 1.7 %collective-permute-done.r1 = f32[64,1024]{1,0:T(8,128)S(1)} collective-permute-done((f32[64,1024]{1,0:T(8,128)}, f32[64,1024]{1,0:T(8,128)S(1)}, u32[]{:S(2)}, u32[]{:S(2)}) %collective-permute-start) | collective-permute-done | bytes 262176 | tf_op jit(solution)/shard_map/ppermute | solution.py:58
  17.3 4.3 %collective-permute-done.1.r2 = f32[64,1024]{1,0:T(8,128)S(1)} collective-permute-done((f32[64,1024]{1,0:T(8,128)}, f32[64,1024]{1,0:T(8,128)S(1)}, u32[]{:S(2)}, u32[]{:S(2)}) %collective-permute-start.1) | collective-permute-done | bytes 262176 | tf_op jit(solution)/shard_map/ppermute | solution.py:58
  22.5 2.2 %shard_map.87 = (f32[4,16,1024]{2,1,0:T(8,128)}, f32[4,16,1024]{2,1,0:T(8,128)}, f32[4,16,1024]{2,1,0:T(8,128)}, f32[4,16,1024]{2,1,0:T(8,128)}) custom-call(f32[64,1024]{1,0:T(8,128)} %get-tuple-element.31.r0, f32[64,1024]{1,0:T(8,128)} %copy-done.3, f32[64,1024]{1,0:T(8,128)} %copy-done.7, f32[64,1024]{1,0:T(8,128)} %copy-done.11), custom_call_target="tpu_custom_call" | custom-call | tf_op jit(solution)/shard_map/pallas_call | solution.py:119
  24.7 1.5 collective-permute-start.3
  26.2 2.7 %collective-permute-start.4 = (f32[4,16,1024]{2,1,0:T(8,128)}, f32[4,16,1024]{2,1,0:T(8,128)S(1)}, u32[]{:S(2)}, u32[]{:S(2)}) collective-permute-start(f32[4,16,1024]{2,1,0:T(8,128)} %get-tuple-element.37), channel_id=1, source_target_pairs={{0,64},{1,17},{2,66},{3,19},{4,68},{5,21},{6,70},{7,23},{8,72},{9,... | collective-permute-start | bytes 786440 | tf_op jit(solution)/shard_map/ppermute | solution.py:58
  28.9 1.4 collective-permute-start.5
  30.4 2.1 %collective-permute-done.3.c1 = f32[4,16,1024]{2,1,0:T(8,128)S(1)} collective-permute-done((f32[4,16,1024]{2,1,0:T(8,128)}, f32[4,16,1024]{2,1,0:T(8,128)S(1)}, u32[]{:S(2)}, u32[]{:S(2)}) %collective-permute-start.3) | collective-permute-done | bytes 262176 | tf_op jit(solution)/shard_map/ppermute | solution.py:58
  32.5 3.8 %collective-permute-done.4.c2 = f32[4,16,1024]{2,1,0:T(8,128)S(1)} collective-permute-done((f32[4,16,1024]{2,1,0:T(8,128)}, f32[4,16,1024]{2,1,0:T(8,128)S(1)}, u32[]{:S(2)}, u32[]{:S(2)}) %collective-permute-start.4) | collective-permute-done | bytes 262176 | tf_op jit(solution)/shard_map/ppermute | solution.py:58
  37.1 2.4 %shard_map.88 = (f32[4,16,1024]{2,1,0:T(8,128)}, f32[4,16,1024]{2,1,0:T(8,128)}, f32[4,16,1024]{2,1,0:T(8,128)}, f32[4,16,1024]{2,1,0:T(8,128)}) custom-call(f32[4,16,1024]{2,1,0:T(8,128)} %get-tuple-element.35.c0, f32[4,16,1024]{2,1,0:T(8,128)} %copy-done.4, f32[4,16,1024]{2,1,0:T(8,128)} %copy-done.8, f32[4,16,1024]{2,1,0:T(8,128)} %copy-done.12), custom_call_target="tpu_custom_call" | custom-call | tf_op jit(solution)/shard_map/pallas_call | solution.py:119
  39.5 2.4 %collective-permute-start.6 = (f32[4,16,1024]{2,1,0:T(8,128)}, f32[4,16,1024]{2,1,0:T(8,128)S(1)}, u32[]{:S(2)}, u32[]{:S(2)}) collective-permute-start(f32[4,16,1024]{2,1,0:T(8,128)} %get-tuple-element.40), channel_id=1, source_target_pairs={{0,96},{1,25},{2,98},{3,27},{4,100},{5,29},{6,102},{7,31},{8,104},... | collective-permute-start | bytes 786440 | tf_op jit(solution)/shard_map/ppermute | solution.py:58
  41.9 1.4 collective-permute-start.7
  43.8 5.2 %collective-permute-done.6.e1 = f32[4,16,1024]{2,1,0:T(8,128)S(1)} collective-permute-done((f32[4,16,1024]{2,1,0:T(8,128)}, f32[4,16,1024]{2,1,0:T(8,128)S(1)}, u32[]{:S(2)}, u32[]{:S(2)}) %collective-permute-start.6) | collective-permute-done | bytes 262176 | tf_op jit(solution)/shard_map/ppermute | solution.py:58
  49.0 1.1 collective-permute-done.7.e2
  50.1 2.7 %collective-permute-done.8.e3 = f32[4,16,1024]{2,1,0:T(8,128)S(1)} collective-permute-done((f32[4,16,1024]{2,1,0:T(8,128)}, f32[4,16,1024]{2,1,0:T(8,128)S(1)}, u32[]{:S(2)}, u32[]{:S(2)}) %collective-permute-start.8) | collective-permute-done | bytes 262176 | tf_op jit(solution)/shard_map/ppermute | solution.py:58
  53.5 2.3 %shard_map.89 = (f32[64,1024]{1,0:T(8,128)}, f32[64,1024]{1,0:T(8,128)}, f32[64,1024]{1,0:T(8,128)}, f32[64,1024]{1,0:T(8,128)}) custom-call(f32[4,16,1024]{2,1,0:T(8,128)} %get-tuple-element.39.e0, f32[4,16,1024]{2,1,0:T(8,128)} %copy-done.5, f32[4,16,1024]{2,1,0:T(8,128)} %copy-done.9, f32[4,16,1024]{2,1,0:T(8,128)} %copy-done.13), custom_call_target="tpu_custom_call" | custom-call | tf_op jit(solution)/shard_map/pallas_call | solution.py:119
  55.8 2.1 %collective-permute-start.9 = (f32[64,1024]{1,0:T(8,128)}, f32[64,1024]{1,0:T(8,128)S(1)}, u32[]{:S(2)}, u32[]{:S(2)}) collective-permute-start(f32[64,1024]{1,0:T(8,128)} %get-tuple-element.44), channel_id=1, source_target_pairs={{0,24},{1,97},{2,26},{3,99},{4,28},{5,101},{6,30},{7,103},{8,0},{9... | collective-permute-start | bytes 786440 | tf_op jit(solution)/shard_map/ppermute | solution.py:58
  57.9 1.4 collective-permute-start.10
  60.0 4.9 %collective-permute-done.9.i1 = f32[64,1024]{1,0:T(8,128)S(1)} collective-permute-done((f32[64,1024]{1,0:T(8,128)}, f32[64,1024]{1,0:T(8,128)S(1)}, u32[]{:S(2)}, u32[]{:S(2)}) %collective-permute-start.9) | collective-permute-done | bytes 262176 | tf_op jit(solution)/shard_map/ppermute | solution.py:58
  66.0 2.7 %collective-permute-done.11.i3 = f32[64,1024]{1,0:T(8,128)S(1)} collective-permute-done((f32[64,1024]{1,0:T(8,128)}, f32[64,1024]{1,0:T(8,128)S(1)}, u32[]{:S(2)}, u32[]{:S(2)}) %collective-permute-start.11) | collective-permute-done | bytes 262176 | tf_op jit(solution)/shard_map/ppermute | solution.py:58
  69.5 2.2 %shard_map.90.above = f32[256,1024]{1,0:T(8,128)} custom-call(f32[64,1024]{1,0:T(8,128)} %get-tuple-element.43.i0, f32[64,1024]{1,0:T(8,128)} %copy-done.15, f32[64,1024]{1,0:T(8,128)} %copy-done.16, f32[64,1024]{1,0:T(8,128)} %copy-done.18), custom_call_target="tpu_custom_call" | custom-call | tf_op jit(solution)/shard_map/pallas_call | solution.py:119
  71.7 1.9 %fusion = (f32[64,1024]{1,0:T(8,128)}, f32[64,1024]{1,0:T(8,128)}) fusion(f32[256,1024]{1,0:T(8,128)} %shard_map.90.above), kind=kLoop, calls=%fused_computation.4 | loop fusion | bytes 1048576 | tf_op jit(solution)/shard_map/slice | solution.py:397
  73.6 1.3 collective-permute-start.13
  74.9 3.7 %collective-permute-start.12 = (f32[64,1024]{1,0:T(8,128)}, f32[64,1024]{1,0:T(8,128)}, u32[]{:S(2)}, u32[]{:S(2)}) collective-permute-start(f32[64,1024]{1,0:T(8,128)} %get-tuple-element.61), channel_id=1, source_target_pairs={{0,1},{1,2},{2,3},{3,4},{4,5},{5,6},{6,7},{8,9},{9,10},{10,11},{11... | collective-permute-start | bytes 786440 | tf_op jit(solution)/shard_map/ppermute | solution.py:396
  79.5 5.0 %shard_map.91 = (bf16[4,2,2,192,256]{4,3,2,1,0:T(8,128)(2,1)}, bf16[4,2,2,512,256]{4,3,2,1,0:T(8,128)(2,1)}) custom-call(s32[4]{0:T(128)} %stratum.1, f32[16,4,256]{2,1,0:T(4,128)} %select_maximum_fusion.taps), custom_call_target="tpu_custom_call" | custom-call | tf_op jit(solution)/shard_map/pallas_call | solution.py:249
  86.3 18.0 %shard_map.92 = (f32[4,256,1024]{2,1,0:T(8,128)}, f32[64,1024]{1,0:T(8,128)}, f32[64,1024]{1,0:T(8,128)}, f32[64,1024]{1,0:T(8,128)}, f32[64,1024]{1,0:T(8,128)}) custom-call(s32[7]{0:T(128)} %seams.1, f32[4,256,1024]{2,1,0:T(8,128)} %ext.3, f32[4,256,1024]{2,1,0:T(8,128)} %est.1, f32[4,256,1024]{2,1,0:T(8,128)} %mea.1, f32[256,1024]{1,0:T(8,128)} %shard_map.90.above, ...), custom_call_target="tpu_custom_call" | custom-call | tf_op jit(solution)/shard_map/pallas_call | solution.py:358
  104.4 2.0 %collective-permute-start.17 = (f32[64,1024]{1,0:T(8,128)}, f32[64,1024]{1,0:T(8,128)S(1)}, u32[]{:S(2)}, u32[]{:S(2)}) collective-permute-start(f32[64,1024]{1,0:T(8,128)} %get-tuple-element.54), channel_id=1, source_target_pairs={{0,16},{1,65},{2,18},{3,67},{4,20},{5,69},{6,22},{7,71},{8,24},{9,... | collective-permute-start | bytes 786440 | tf_op jit(solution)/shard_map/ppermute | solution.py:58
  106.4 2.0 %collective-permute-start.18 = (f32[64,1024]{1,0:T(8,128)}, f32[64,1024]{1,0:T(8,128)S(1)}, u32[]{:S(2)}, u32[]{:S(2)}) collective-permute-start(f32[64,1024]{1,0:T(8,128)} %get-tuple-element.55), channel_id=1, source_target_pairs={{0,24},{1,97},{2,26},{3,99},{4,28},{5,101},{6,30},{7,103},{8,0},{9... | collective-permute-start | bytes 786440 | tf_op jit(solution)/shard_map/ppermute | solution.py:58
  108.4 6.5 %collective-permute-done.16.r1 = f32[64,1024]{1,0:T(8,128)S(1)} collective-permute-done((f32[64,1024]{1,0:T(8,128)}, f32[64,1024]{1,0:T(8,128)S(1)}, u32[]{:S(2)}, u32[]{:S(2)}) %collective-permute-start.16) | collective-permute-done | bytes 262176 | tf_op jit(solution)/shard_map/ppermute | solution.py:58
  116.6 2.0 %shard_map.93 = (f32[16,1024]{1,0:T(8,128)}, f32[16,1024]{1,0:T(8,128)}, f32[16,1024]{1,0:T(8,128)}, f32[16,1024]{1,0:T(8,128)}) custom-call(f32[64,1024]{1,0:T(8,128)} %get-tuple-element.52.r0, f32[64,1024]{1,0:T(8,128)} %copy-done.6, f32[64,1024]{1,0:T(8,128)} %copy-done.10, f32[64,1024]{1,0:T(8,128)} %copy-done.14), custom_call_target="tpu_custom_call" | custom-call | tf_op jit(solution)/shard_map/pallas_call | solution.py:119
  118.5 2.0 %collective-permute-start.20 = (f32[16,1024]{1,0:T(8,128)}, f32[16,1024]{1,0:T(8,128)S(1)}, u32[]{:S(2)}, u32[]{:S(2)}) collective-permute-start(f32[16,1024]{1,0:T(8,128)} %get-tuple-element.58), channel_id=1, source_target_pairs={{0,64},{1,17},{2,66},{3,19},{4,68},{5,21},{6,70},{7,23},{8,72},{9,... | collective-permute-start | bytes 196616 | tf_op jit(solution)/shard_map/ppermute | solution.py:58
  120.6 1.8 %collective-permute-start.21 = (f32[16,1024]{1,0:T(8,128)}, f32[16,1024]{1,0:T(8,128)S(1)}, u32[]{:S(2)}, u32[]{:S(2)}) collective-permute-start(f32[16,1024]{1,0:T(8,128)} %get-tuple-element.59), channel_id=1, source_target_pairs={{0,96},{1,25},{2,98},{3,27},{4,100},{5,29},{6,102},{7,31},{8,104},... | collective-permute-start | bytes 196616 | tf_op jit(solution)/shard_map/ppermute | solution.py:58
  122.3 2.6 %collective-permute-done.19.r1 = f32[16,1024]{1,0:T(8,128)S(1)} collective-permute-done((f32[16,1024]{1,0:T(8,128)}, f32[16,1024]{1,0:T(8,128)S(1)}, u32[]{:S(2)}, u32[]{:S(2)}) %collective-permute-start.19) | collective-permute-done | bytes 65568 | tf_op jit(solution)/shard_map/ppermute | solution.py:58
  126.4 1.6 %shard_map.94.i0 = f32[16,1024]{1,0:T(8,128)} custom-call(f32[16,1024]{1,0:T(8,128)} %get-tuple-element.56.r0, f32[16,1024]{1,0:T(8,128)} %copy-done.21, f32[16,1024]{1,0:T(8,128)} %copy-done.22, f32[16,1024]{1,0:T(8,128)} %copy-done.23), custom_call_target="tpu_custom_call" | custom-call | tf_op jit(solution)/shard_map/pallas_call | solution.py:119
  128.0 2.7 %collective-permute-start.24 = (f32[16,1024]{1,0:T(8,128)}, f32[16,1024]{1,0:T(8,128)S(1)}, u32[]{:S(2)}, u32[]{:S(2)}) collective-permute-start(f32[16,1024]{1,0:T(8,128)} %shard_map.94.i0), channel_id=1, source_target_pairs={{0,96},{1,25},{2,98},{3,27},{4,100},{5,29},{6,102},{7,31},{8,104},... | collective-permute-start | bytes 196616 | tf_op jit(solution)/shard_map/ppermute | solution.py:58
  131.5 2.0 %collective-permute-done.24.i3 = f32[16,1024]{1,0:T(8,128)S(1)} collective-permute-done((f32[16,1024]{1,0:T(8,128)}, f32[16,1024]{1,0:T(8,128)S(1)}, u32[]{:S(2)}, u32[]{:S(2)}) %collective-permute-start.24) | collective-permute-done | bytes 65568 | tf_op jit(solution)/shard_map/ppermute | solution.py:58
  133.5 3.2 %collective-permute-done.23.i2 = f32[16,1024]{1,0:T(8,128)S(1)} collective-permute-done((f32[16,1024]{1,0:T(8,128)}, f32[16,1024]{1,0:T(8,128)S(1)}, u32[]{:S(2)}, u32[]{:S(2)}) %collective-permute-start.23) | collective-permute-done | bytes 65568 | tf_op jit(solution)/shard_map/ppermute | solution.py:58
  137.9 1.7 %shard_map.95.i0 = f32[64,1024]{1,0:T(8,128)} custom-call(f32[16,1024]{1,0:T(8,128)} %shard_map.94.i0, f32[16,1024]{1,0:T(8,128)} %copy-done.26, f32[16,1024]{1,0:T(8,128)} %copy-done.25, f32[16,1024]{1,0:T(8,128)} %copy-done.24), custom_call_target="tpu_custom_call" | custom-call | tf_op jit(solution)/shard_map/pallas_call | solution.py:119
  139.6 2.6 %collective-permute-start.27 = (f32[64,1024]{1,0:T(8,128)}, f32[64,1024]{1,0:T(8,128)S(1)}, u32[]{:S(2)}, u32[]{:S(2)}) collective-permute-start(f32[64,1024]{1,0:T(8,128)} %shard_map.95.i0), channel_id=1, source_target_pairs={{0,24},{1,97},{2,26},{3,99},{4,28},{5,101},{6,30},{7,103},{8,0},{9... | collective-permute-start | bytes 786440 | tf_op jit(solution)/shard_map/ppermute | solution.py:58
  143.1 6.2 %collective-permute-done.27.i3 = f32[64,1024]{1,0:T(8,128)S(1)} collective-permute-done((f32[64,1024]{1,0:T(8,128)}, f32[64,1024]{1,0:T(8,128)S(1)}, u32[]{:S(2)}, u32[]{:S(2)}) %collective-permute-start.27) | collective-permute-done | bytes 262176 | tf_op jit(solution)/shard_map/ppermute | solution.py:58
  149.3 1.1 collective-permute-done.26.i2
  150.4 2.6 %collective-permute-done.25.i1 = f32[64,1024]{1,0:T(8,128)S(1)} collective-permute-done((f32[64,1024]{1,0:T(8,128)}, f32[64,1024]{1,0:T(8,128)S(1)}, u32[]{:S(2)}, u32[]{:S(2)}) %collective-permute-start.25) | collective-permute-done | bytes 262176 | tf_op jit(solution)/shard_map/ppermute | solution.py:58
  153.8 2.2 %shard_map.96 = f32[256,1024]{1,0:T(8,128)} custom-call(f32[64,1024]{1,0:T(8,128)} %shard_map.95.i0, f32[64,1024]{1,0:T(8,128)} %copy-done.20, f32[64,1024]{1,0:T(8,128)} %copy-done.19, f32[64,1024]{1,0:T(8,128)} %copy-done.17), custom_call_target="tpu_custom_call" | custom-call | tf_op jit(solution)/shard_map/pallas_call | solution.py:119
  (81 shorter events, 14.9 us)
Async XLA Ops:
  6.4 72.2 %copy-start.28 = (f32[16,65]{1,0:T(8,128)S(1)}, f32[16,65]{1,0:T(8,128)}, u32[]{:S(2)}) copy-start(f32[16,65]{1,0:T(8,128)} %param.10) | copy-start | bytes 12484
  6.5 72.3 %copy-start.27 = (f32[16,65]{1,0:T(8,128)S(1)}, f32[16,65]{1,0:T(8,128)}, u32[]{:S(2)}) copy-start(f32[16,65]{1,0:T(8,128)} %param.11) | copy-start | bytes 12484
  6.5 78.1 %collective-permute-start.14 = (f32[4,96,1024]{2,1,0:T(8,128)}, f32[4,96,1024]{2,1,0:T(8,128)S(1)}, u32[]{:S(2)}, u32[]{:S(2)}) collective-permute-start(f32[4,96,1024]{2,1,0:T(8,128)} %get-tuple-element.47), channel_id=1, source_target_pairs={{0,1},{1,2},{2,3},{3,4},{4,5},{5,6},{6,7},{8,9},{9,10},{10,11},{11... | collective-permute-start | bytes 4718600 | tf_op jit(solution)/shard_map/ppermute | solution.py:392
  7.9 76.7 %collective-permute-start.15 = (f32[4,96,1024]{2,1,0:T(8,128)}, f32[4,96,1024]{2,1,0:T(8,128)S(1)}, u32[]{:S(2)}, u32[]{:S(2)}) collective-permute-start(f32[4,96,1024]{2,1,0:T(8,128)} %get-tuple-element.48), channel_id=1, source_target_pairs={{1,0},{2,1},{3,2},{4,3},{5,4},{6,5},{7,6},{9,8},{10,9},{11,10},{12... | collective-permute-start | bytes 4718600 | tf_op jit(solution)/shard_map/ppermute | solution.py:393
  9.2 8.2 %collective-permute-start = (f32[64,1024]{1,0:T(8,128)}, f32[64,1024]{1,0:T(8,128)S(1)}, u32[]{:S(2)}, u32[]{:S(2)}) collective-permute-start(f32[64,1024]{1,0:T(8,128)} %get-tuple-element.32), channel_id=1, source_target_pairs={{0,8},{1,33},{2,10},{3,35},{4,12},{5,37},{6,14},{7,39},{8,16},{9,4... | collective-permute-start | bytes 786440 | tf_op jit(solution)/shard_map/ppermute | solution.py:58
  11.3 10.3 %collective-permute-start.1 = (f32[64,1024]{1,0:T(8,128)}, f32[64,1024]{1,0:T(8,128)S(1)}, u32[]{:S(2)}, u32[]{:S(2)}) collective-permute-start(f32[64,1024]{1,0:T(8,128)} %get-tuple-element.33), channel_id=1, source_target_pairs={{0,16},{1,65},{2,18},{3,67},{4,20},{5,69},{6,22},{7,71},{8,24},{9,... | collective-permute-start | bytes 786440 | tf_op jit(solution)/shard_map/ppermute | solution.py:58
  14.2 7.4 %collective-permute-start.2 = (f32[64,1024]{1,0:T(8,128)}, f32[64,1024]{1,0:T(8,128)S(1)}, u32[]{:S(2)}, u32[]{:S(2)}) collective-permute-start(f32[64,1024]{1,0:T(8,128)} %get-tuple-element.34), channel_id=1, source_target_pairs={{0,24},{1,97},{2,26},{3,99},{4,28},{5,101},{6,30},{7,103},{8,0},{9... | collective-permute-start | bytes 786440 | tf_op jit(solution)/shard_map/ppermute | solution.py:58
  17.3 4.3 %copy-start.3 = (f32[64,1024]{1,0:T(8,128)}, f32[64,1024]{1,0:T(8,128)S(1)}, u32[]{:S(2)}) copy-start(f32[64,1024]{1,0:T(8,128)S(1)} %collective-permute-done.r1) | copy-start | bytes 786436
  21.6 0.8 copy-start.11
  24.7 7.8 %collective-permute-start.3 = (f32[4,16,1024]{2,1,0:T(8,128)}, f32[4,16,1024]{2,1,0:T(8,128)S(1)}, u32[]{:S(2)}, u32[]{:S(2)}) collective-permute-start(f32[4,16,1024]{2,1,0:T(8,128)} %get-tuple-element.36), channel_id=1, source_target_pairs={{0,32},{1,9},{2,34},{3,11},{4,36},{5,13},{6,38},{7,15},{8,40},{9,1... | collective-permute-start | bytes 786440 | tf_op jit(solution)/shard_map/ppermute | solution.py:58
  26.2 10.1 %collective-permute-start.4 = (f32[4,16,1024]{2,1,0:T(8,128)}, f32[4,16,1024]{2,1,0:T(8,128)S(1)}, u32[]{:S(2)}, u32[]{:S(2)}) collective-permute-start(f32[4,16,1024]{2,1,0:T(8,128)} %get-tuple-element.37), channel_id=1, source_target_pairs={{0,64},{1,17},{2,66},{3,19},{4,68},{5,21},{6,70},{7,23},{8,72},{9,... | collective-permute-start | bytes 786440 | tf_op jit(solution)/shard_map/ppermute | solution.py:58
  28.9 7.4 %collective-permute-start.5 = (f32[4,16,1024]{2,1,0:T(8,128)}, f32[4,16,1024]{2,1,0:T(8,128)S(1)}, u32[]{:S(2)}, u32[]{:S(2)}) collective-permute-start(f32[4,16,1024]{2,1,0:T(8,128)} %get-tuple-element.38), channel_id=1, source_target_pairs={{0,96},{1,25},{2,98},{3,27},{4,100},{5,29},{6,102},{7,31},{8,104},... | collective-permute-start | bytes 786440 | tf_op jit(solution)/shard_map/ppermute | solution.py:58
  32.5 3.8 %copy-start.4 = (f32[4,16,1024]{2,1,0:T(8,128)}, f32[4,16,1024]{2,1,0:T(8,128)S(1)}, u32[]{:S(2)}) copy-start(f32[4,16,1024]{2,1,0:T(8,128)S(1)} %collective-permute-done.3.c1) | copy-start | bytes 786436
  36.3 0.8 copy-start.12
  39.5 9.5 %collective-permute-start.6 = (f32[4,16,1024]{2,1,0:T(8,128)}, f32[4,16,1024]{2,1,0:T(8,128)S(1)}, u32[]{:S(2)}, u32[]{:S(2)}) collective-permute-start(f32[4,16,1024]{2,1,0:T(8,128)} %get-tuple-element.40), channel_id=1, source_target_pairs={{0,96},{1,25},{2,98},{3,27},{4,100},{5,29},{6,102},{7,31},{8,104},... | collective-permute-start | bytes 786440 | tf_op jit(solution)/shard_map/ppermute | solution.py:58
  41.9 8.2 %collective-permute-start.7 = (f32[4,16,1024]{2,1,0:T(8,128)}, f32[4,16,1024]{2,1,0:T(8,128)S(1)}, u32[]{:S(2)}, u32[]{:S(2)}) collective-permute-start(f32[4,16,1024]{2,1,0:T(8,128)} %get-tuple-element.41), channel_id=1, source_target_pairs={{0,64},{1,17},{2,66},{3,19},{4,68},{5,21},{6,70},{7,23},{8,72},{9,... | collective-permute-start | bytes 786440 | tf_op jit(solution)/shard_map/ppermute | solution.py:58
  43.4 9.5 %collective-permute-start.8 = (f32[4,16,1024]{2,1,0:T(8,128)}, f32[4,16,1024]{2,1,0:T(8,128)S(1)}, u32[]{:S(2)}, u32[]{:S(2)}) collective-permute-start(f32[4,16,1024]{2,1,0:T(8,128)} %get-tuple-element.42), channel_id=1, source_target_pairs={{0,32},{1,9},{2,34},{3,11},{4,36},{5,13},{6,38},{7,15},{8,40},{9,1... | collective-permute-start | bytes 786440 | tf_op jit(solution)/shard_map/ppermute | solution.py:58
  49.0 3.9 %copy-start.5 = (f32[4,16,1024]{2,1,0:T(8,128)}, f32[4,16,1024]{2,1,0:T(8,128)S(1)}, u32[]{:S(2)}) copy-start(f32[4,16,1024]{2,1,0:T(8,128)S(1)} %collective-permute-done.6.e1) | copy-start | bytes 786436
  50.1 2.7 %copy-start.9 = (f32[4,16,1024]{2,1,0:T(8,128)}, f32[4,16,1024]{2,1,0:T(8,128)S(1)}, u32[]{:S(2)}) copy-start(f32[4,16,1024]{2,1,0:T(8,128)S(1)} %collective-permute-done.7.e2) | copy-start | bytes 786436
  55.8 9.1 %collective-permute-start.9 = (f32[64,1024]{1,0:T(8,128)}, f32[64,1024]{1,0:T(8,128)S(1)}, u32[]{:S(2)}, u32[]{:S(2)}) collective-permute-start(f32[64,1024]{1,0:T(8,128)} %get-tuple-element.44), channel_id=1, source_target_pairs={{0,24},{1,97},{2,26},{3,99},{4,28},{5,101},{6,30},{7,103},{8,0},{9... | collective-permute-start | bytes 786440 | tf_op jit(solution)/shard_map/ppermute | solution.py:58
  57.9 8.2 %collective-permute-start.10 = (f32[64,1024]{1,0:T(8,128)}, f32[64,1024]{1,0:T(8,128)S(1)}, u32[]{:S(2)}, u32[]{:S(2)}) collective-permute-start(f32[64,1024]{1,0:T(8,128)} %get-tuple-element.45), channel_id=1, source_target_pairs={{0,16},{1,65},{2,18},{3,67},{4,20},{5,69},{6,22},{7,71},{8,24},{9,... | collective-permute-start | bytes 786440 | tf_op jit(solution)/shard_map/ppermute | solution.py:58
  59.3 9.5 %collective-permute-start.11 = (f32[64,1024]{1,0:T(8,128)}, f32[64,1024]{1,0:T(8,128)S(1)}, u32[]{:S(2)}, u32[]{:S(2)}) collective-permute-start(f32[64,1024]{1,0:T(8,128)} %get-tuple-element.46), channel_id=1, source_target_pairs={{0,8},{1,33},{2,10},{3,35},{4,12},{5,37},{6,14},{7,39},{8,16},{9,4... | collective-permute-start | bytes 786440 | tf_op jit(solution)/shard_map/ppermute | solution.py:58
  64.9 3.9 %copy-start.15 = (f32[64,1024]{1,0:T(8,128)}, f32[64,1024]{1,0:T(8,128)S(1)}, u32[]{:S(2)}) copy-start(f32[64,1024]{1,0:T(8,128)S(1)} %collective-permute-done.9.i1) | copy-start | bytes 786436
  66.0 2.7 %copy-start.16 = (f32[64,1024]{1,0:T(8,128)}, f32[64,1024]{1,0:T(8,128)S(1)}, u32[]{:S(2)}) copy-start(f32[64,1024]{1,0:T(8,128)S(1)} %collective-permute-done.10.i2) | copy-start | bytes 786436
  73.6 10.9 %collective-permute-start.13 = (f32[64,1024]{1,0:T(8,128)}, f32[64,1024]{1,0:T(8,128)S(1)}, u32[]{:S(2)}, u32[]{:S(2)}) collective-permute-start(f32[64,1024]{1,0:T(8,128)} %get-tuple-element.60), channel_id=1, source_target_pairs={{1,0},{2,1},{3,2},{4,3},{5,4},{6,5},{7,6},{9,8},{10,9},{11,10},{12... | collective-permute-start | bytes 786440 | tf_op jit(solution)/shard_map/ppermute | solution.py:397
  74.9 9.6 %collective-permute-start.12 = (f32[64,1024]{1,0:T(8,128)}, f32[64,1024]{1,0:T(8,128)}, u32[]{:S(2)}, u32[]{:S(2)}) collective-permute-start(f32[64,1024]{1,0:T(8,128)} %get-tuple-element.61), channel_id=1, source_target_pairs={{0,1},{1,2},{2,3},{3,4},{4,5},{5,6},{6,7},{8,9},{9,10},{10,11},{11... | collective-permute-start | bytes 786440 | tf_op jit(solution)/shard_map/ppermute | solution.py:396
  84.5 0.7 copy-start.2
  84.5 1.3 copy-start
  84.6 1.7 %copy-start.1 = (f32[4,96,1024]{2,1,0:T(8,128)}, f32[4,96,1024]{2,1,0:T(8,128)S(1)}, u32[]{:S(2)}) copy-start(f32[4,96,1024]{2,1,0:T(8,128)S(1)} %collective-permute-done.15.rim_bot) | copy-start | bytes 4718596
  104.3 10.7 %collective-permute-start.16 = (f32[64,1024]{1,0:T(8,128)}, f32[64,1024]{1,0:T(8,128)S(1)}, u32[]{:S(2)}, u32[]{:S(2)}) collective-permute-start(f32[64,1024]{1,0:T(8,128)} %get-tuple-element.53), channel_id=1, source_target_pairs={{0,8},{1,33},{2,10},{3,35},{4,12},{5,37},{6,14},{7,39},{8,16},{9,4... | collective-permute-start | bytes 786440 | tf_op jit(solution)/shard_map/ppermute | solution.py:58
  104.4 10.6 %collective-permute-start.17 = (f32[64,1024]{1,0:T(8,128)}, f32[64,1024]{1,0:T(8,128)S(1)}, u32[]{:S(2)}, u32[]{:S(2)}) collective-permute-start(f32[64,1024]{1,0:T(8,128)} %get-tuple-element.54), channel_id=1, source_target_pairs={{0,16},{1,65},{2,18},{3,67},{4,20},{5,69},{6,22},{7,71},{8,24},{9,... | collective-permute-start | bytes 786440 | tf_op jit(solution)/shard_map/ppermute | solution.py:58
  106.4 9.4 %collective-permute-start.18 = (f32[64,1024]{1,0:T(8,128)}, f32[64,1024]{1,0:T(8,128)S(1)}, u32[]{:S(2)}, u32[]{:S(2)}) collective-permute-start(f32[64,1024]{1,0:T(8,128)} %get-tuple-element.55), channel_id=1, source_target_pairs={{0,24},{1,97},{2,26},{3,99},{4,28},{5,101},{6,30},{7,103},{8,0},{9... | collective-permute-start | bytes 786440 | tf_op jit(solution)/shard_map/ppermute | solution.py:58
  114.9 0.9 copy-start.6
  115.0 0.9 copy-start.10
  118.5 6.4 %collective-permute-start.19 = (f32[16,1024]{1,0:T(8,128)}, f32[16,1024]{1,0:T(8,128)S(1)}, u32[]{:S(2)}, u32[]{:S(2)}) collective-permute-start(f32[16,1024]{1,0:T(8,128)} %get-tuple-element.57), channel_id=1, source_target_pairs={{0,32},{1,9},{2,34},{3,11},{4,36},{5,13},{6,38},{7,15},{8,40},{9,1... | collective-permute-start | bytes 196616 | tf_op jit(solution)/shard_map/ppermute | solution.py:58
  118.5 6.4 %collective-permute-start.20 = (f32[16,1024]{1,0:T(8,128)}, f32[16,1024]{1,0:T(8,128)S(1)}, u32[]{:S(2)}, u32[]{:S(2)}) collective-permute-start(f32[16,1024]{1,0:T(8,128)} %get-tuple-element.58), channel_id=1, source_target_pairs={{0,64},{1,17},{2,66},{3,19},{4,68},{5,21},{6,70},{7,23},{8,72},{9,... | collective-permute-start | bytes 196616 | tf_op jit(solution)/shard_map/ppermute | solution.py:58
  120.6 5.2 %collective-permute-start.21 = (f32[16,1024]{1,0:T(8,128)}, f32[16,1024]{1,0:T(8,128)S(1)}, u32[]{:S(2)}, u32[]{:S(2)}) collective-permute-start(f32[16,1024]{1,0:T(8,128)} %get-tuple-element.59), channel_id=1, source_target_pairs={{0,96},{1,25},{2,98},{3,27},{4,100},{5,29},{6,102},{7,31},{8,104},... | collective-permute-start | bytes 196616 | tf_op jit(solution)/shard_map/ppermute | solution.py:58
  124.9 0.9 copy-start.21
  124.9 0.9 copy-start.22
  128.0 5.5 %collective-permute-start.24 = (f32[16,1024]{1,0:T(8,128)}, f32[16,1024]{1,0:T(8,128)S(1)}, u32[]{:S(2)}, u32[]{:S(2)}) collective-permute-start(f32[16,1024]{1,0:T(8,128)} %shard_map.94.i0), channel_id=1, source_target_pairs={{0,96},{1,25},{2,98},{3,27},{4,100},{5,29},{6,102},{7,31},{8,104},... | collective-permute-start | bytes 196616 | tf_op jit(solution)/shard_map/ppermute | solution.py:58
  130.6 6.0 %collective-permute-start.23 = (f32[16,1024]{1,0:T(8,128)}, f32[16,1024]{1,0:T(8,128)S(1)}, u32[]{:S(2)}, u32[]{:S(2)}) collective-permute-start(f32[16,1024]{1,0:T(8,128)} %shard_map.94.i0), channel_id=1, source_target_pairs={{0,64},{1,17},{2,66},{3,19},{4,68},{5,21},{6,70},{7,23},{8,72},{9,... | collective-permute-start | bytes 196616 | tf_op jit(solution)/shard_map/ppermute | solution.py:58
  131.3 6.0 %collective-permute-start.22 = (f32[16,1024]{1,0:T(8,128)}, f32[16,1024]{1,0:T(8,128)S(1)}, u32[]{:S(2)}, u32[]{:S(2)}) collective-permute-start(f32[16,1024]{1,0:T(8,128)} %shard_map.94.i0), channel_id=1, source_target_pairs={{0,32},{1,9},{2,34},{3,11},{4,36},{5,13},{6,38},{7,15},{8,40},{9,1... | collective-permute-start | bytes 196616 | tf_op jit(solution)/shard_map/ppermute | solution.py:58
  133.5 3.9 %copy-start.24 = (f32[16,1024]{1,0:T(8,128)}, f32[16,1024]{1,0:T(8,128)S(1)}, u32[]{:S(2)}) copy-start(f32[16,1024]{1,0:T(8,128)S(1)} %collective-permute-done.24.i3) | copy-start | bytes 196612
  139.6 9.7 %collective-permute-start.27 = (f32[64,1024]{1,0:T(8,128)}, f32[64,1024]{1,0:T(8,128)S(1)}, u32[]{:S(2)}, u32[]{:S(2)}) collective-permute-start(f32[64,1024]{1,0:T(8,128)} %shard_map.95.i0), channel_id=1, source_target_pairs={{0,24},{1,97},{2,26},{3,99},{4,28},{5,101},{6,30},{7,103},{8,0},{9... | collective-permute-start | bytes 786440 | tf_op jit(solution)/shard_map/ppermute | solution.py:58
  142.3 8.2 %collective-permute-start.26 = (f32[64,1024]{1,0:T(8,128)}, f32[64,1024]{1,0:T(8,128)S(1)}, u32[]{:S(2)}, u32[]{:S(2)}) collective-permute-start(f32[64,1024]{1,0:T(8,128)} %shard_map.95.i0), channel_id=1, source_target_pairs={{0,16},{1,65},{2,18},{3,67},{4,20},{5,69},{6,22},{7,71},{8,24},{9,... | collective-permute-start | bytes 786440 | tf_op jit(solution)/shard_map/ppermute | solution.py:58
  142.5 10.6 %collective-permute-start.25 = (f32[64,1024]{1,0:T(8,128)}, f32[64,1024]{1,0:T(8,128)S(1)}, u32[]{:S(2)}, u32[]{:S(2)}) collective-permute-start(f32[64,1024]{1,0:T(8,128)} %shard_map.95.i0), channel_id=1, source_target_pairs={{0,8},{1,33},{2,10},{3,35},{4,12},{5,37},{6,14},{7,39},{8,16},{9,4... | collective-permute-start | bytes 786440 | tf_op jit(solution)/shard_map/ppermute | solution.py:58
  149.3 3.8 %copy-start.17 = (f32[64,1024]{1,0:T(8,128)}, f32[64,1024]{1,0:T(8,128)S(1)}, u32[]{:S(2)}) copy-start(f32[64,1024]{1,0:T(8,128)S(1)} %collective-permute-done.27.i3) | copy-start | bytes 786436
  150.4 2.6 %copy-start.19 = (f32[64,1024]{1,0:T(8,128)}, f32[64,1024]{1,0:T(8,128)S(1)}, u32[]{:S(2)}) copy-start(f32[64,1024]{1,0:T(8,128)S(1)} %collective-permute-done.26.i2) | copy-start | bytes 786436
  (9 other events, 6.2 us)

commit v2 on v1

v2 whole, which is shorter than its diff:
```python
import jax
import jax.numpy as jnp
from jax import lax
from jax.experimental import pallas as pl
from jax.experimental.pallas import tpu as pltpu
from jax.sharding import PartitionSpec as P

SIDE = 4
HALF = 32
TAPS = 65
BF = jnp.bfloat16
F32 = jnp.float32


def params(mib):
    return pltpu.CompilerParams(vmem_limit_bytes=mib << 20)


def whole():
    return pl.BlockSpec(memory_space=pltpu.VMEM)


def smem():
    return pl.BlockSpec(memory_space=pltpu.SMEM)


def place():
    depth = lax.axis_index("depth")
    tile = lax.axis_index("tile")
    return depth // SIDE, depth % SIDE, tile % 2, tile


PAIRINGS = {
    (0, 0): (("y", 1), ("y", 3), ("x", 1), ("x", 3)),
    (0, 1): (("x", 1), ("x", 3), ("y", 1), ("y", 3)),
    (1, 0): (("y", 3), ("y", 1), ("x", 3), ("x", 1)),
    (1, 1): (("x", 3), ("x", 1), ("y", 3), ("y", 1)),
}


def pairs(piece, number, tiles):
    result = []
    for x in range(SIDE):
        for y in range(SIDE):
            for tile in range(tiles):
                axis, flip = PAIRINGS[(tile % 2, piece)][number]
                tx, ty = (x, y ^ flip) if axis == "y" else (x ^ flip, y)
                result.append(((x * SIDE + y) * tiles + tile, (tx * SIDE + ty) * tiles + tile))
    return result


def swap(value, piece, number):
    return lax.ppermute(value, ("depth", "tile"), pairs(piece, number, lax.axis_size("tile")))


def side(piece):
    x, y, core, _ = place()
    bits = []
    for c in range(2):
        axis, flip = PAIRINGS[(c, piece)][0]
        value = y if axis == "y" else x
        bits.append((value + 1) // 2 % 2 if flip == 1 else value // 2)
    return jnp.where(core == 0, bits[0], bits[1])


def split(value):
    high = value.astype(BF)
    return high, (value - high.astype(F32)).astype(BF)


def rows_at(index, size):
    return pl.ds(pl.multiple_of(index * size, size), size)


def sums_kernel(ext, out, buf, sems):
    block = out.shape[0] // sems.shape[0]
    copies = []
    for i in range(sems.shape[0]):
        rows = pl.ds(i * block, block)
        copies.append(pltpu.make_async_copy(ext.at[:, rows], buf.at[:, rows], sems.at[i]))
        copies[-1].start()
    for i, copy in enumerate(copies):
        copy.wait()
        rows = pl.ds(i * block, block)
        total = buf[0, rows]
        for plane in range(1, buf.shape[0]):
            total = total + buf[plane, rows]
        out[rows] = total


def sums(extinction):
    planes, rows, cols = extinction.shape
    return pl.pallas_call(
        sums_kernel,
        in_specs=[pl.BlockSpec(memory_space=pl.ANY)],
        out_specs=whole(),
        out_shape=jax.ShapeDtypeStruct((rows, cols), F32),
        scratch_shapes=[pltpu.VMEM((planes, rows, cols), F32), pltpu.SemaphoreType.DMA((8,))],
        compiler_params=params(60),
    )(extinction)


def rims_kernel(ext_top, ext_bot, est_top, est_bot, mea_top, mea_bot, up, down, acc_top, acc_bot):
    rim = 2 * HALF
    for ext, est, mea, out, acc in (
        (ext_top, est_top, mea_top, up, acc_top),
        (ext_bot, est_bot, mea_bot, down, acc_bot),
    ):

        @pl.when(pl.program_id(0) == 0)
        def _():
            acc[...] = jnp.zeros_like(acc)

        out[0, :rim] = jnp.exp(-acc[...]) * est[0]
        out[0, rim:] = mea[0]
        acc[...] += ext[0]


def rims(extinction, estimate, measured):
    planes, rows, cols = extinction.shape
    rim = 2 * HALF
    far = rows // rim - 1
    top = pl.BlockSpec((1, rim, cols), lambda p: (p, 0, 0))
    bot = pl.BlockSpec((1, rim, cols), lambda p: (p, far, 0))
    out = pl.BlockSpec((1, rim + HALF, cols), lambda p: (p, 0, 0))
    return pl.pallas_call(
        rims_kernel,
        grid=(planes,),
        in_specs=[
            top, bot, top, bot,
            pl.BlockSpec((1, HALF, cols), lambda p: (p, 0, 0)),
            pl.BlockSpec((1, HALF, cols), lambda p: (p, rows // HALF - 1, 0)),
        ],
        out_specs=[out, out],
        out_shape=[jax.ShapeDtypeStruct((planes, rim + HALF, cols), F32)] * 2,
        scratch_shapes=[pltpu.VMEM((rim, cols), F32)] * 2,
        compiler_params=params(60),
        cost_estimate=pl.CostEstimate(flops=1 << 20, bytes_accessed=8 << 20, transcendentals=1 << 19),
    )(extinction, extinction, estimate, estimate, measured, measured)


def scan_kernel(parts, out):
    running = jnp.zeros(parts.shape[1:], F32)
    for slab in range(parts.shape[0]):
        value = parts[slab]
        out[slab] = running
        running = running + value


def above_of(total, meanwhile):
    rows, cols = total.shape
    slabs = lax.axis_size("depth")
    parts = total.reshape(slabs, rows // slabs, cols)
    parts = lax.all_to_all(parts, "depth", 0, 0, tiled=True)
    prefixes = pl.pallas_call(
        scan_kernel,
        in_specs=[whole()],
        out_specs=whole(),
        out_shape=jax.ShapeDtypeStruct(parts.shape, F32),
        compiler_params=params(16),
    )(parts)
    prefixes, meanwhile = lax.optimization_barrier((prefixes, meanwhile))
    return lax.all_to_all(prefixes, "depth", 0, 0, tiled=True).reshape(rows, cols), meanwhile


def highest(parts):
    joined = []
    held = [jnp.maximum(keep, swap(give, piece, 0)) for piece, (keep, give) in enumerate(parts)]
    for number in range(1, 4):
        held = [jnp.maximum(value, swap(value, piece, number)) for piece, value in enumerate(held)]
    for piece, mine in enumerate(held):
        other = swap(mine, piece, 0)
        first = side(piece) == 0
        joined += [jnp.where(first, mine, other), jnp.where(first, other, mine)]
    return jnp.concatenate(joined)


def bands_kernel(stratum, taps, v_ref, l_ref):
    def toeplitz(row, count, shift):
        line = taps[0, row : row + 1]
        line = line / jnp.sum(line, axis=1, keepdims=True)
        wide = jnp.broadcast_to(line, (count, line.shape[1]))
        return pltpu.roll(wide, shift, 1, stride=1, stride_axis=0)

    for way in range(2):
        band = toeplitz(way, v_ref.shape[3], 0)
        v_ref[0, way, 0], v_ref[0, way, 1] = split(band)
        ring = toeplitz(3 - way, 256, 256 - HALF)
        k = lax.broadcasted_iota(jnp.int32, ring.shape, 0)
        n = lax.broadcasted_iota(jnp.int32, ring.shape, 1)
        zero = jnp.zeros_like(ring)
        main = jnp.where(jnp.abs(n - k) <= HALF, ring, zero)
        left = jnp.where(k - n > HALF, ring, zero)[128:]
        right = jnp.where(n - k > HALF, ring, zero)[:128]
        for at, part in ((0, left), (128, main), (384, right)):
            high, low = split(part)
            l_ref[0, way, 0, at : at + part.shape[0]] = high
            l_ref[0, way, 1, at : at + part.shape[0]] = low


def bands(psf_rows, psf_cols, stratum):
    planes = stratum.shape[0]
    taps = jnp.stack([psf_rows, psf_rows[:, ::-1], psf_cols, psf_cols[:, ::-1]], axis=1)
    taps = jnp.pad(taps, ((0, 0), (0, 0), (0, 256 - TAPS)))
    return pl.pallas_call(
        bands_kernel,
        grid_spec=pltpu.PrefetchScalarGridSpec(
            num_scalar_prefetch=1,
            grid=(planes,),
            in_specs=[pl.BlockSpec((1, 4, 256), lambda p, s: (s[p], 0, 0))],
            out_specs=[
                pl.BlockSpec((1, 2, 2, 192, 256), lambda p, s: (p, 0, 0, 0, 0)),
                pl.BlockSpec((1, 2, 2, 512, 256), lambda p, s: (p, 0, 0, 0, 0)),
            ],
        ),
        out_shape=[
            jax.ShapeDtypeStruct((planes, 2, 2, 192, 256), BF),
            jax.ShapeDtypeStruct((planes, 2, 2, 512, 256), BF),
        ],
        compiler_params=params(60),
        cost_estimate=pl.CostEstimate(flops=1 << 22, bytes_accessed=6 << 20, transcendentals=0),
    )(stratum, taps)


def dot(a, b):
    return jnp.dot(a, b, preferred_element_type=F32)


def dot3(a_high, a_low, b_high, b_low):
    return dot(a_high, b_high) + (dot(a_high, b_low) + dot(a_low, b_high))


def step_kernel(
    seams, ext, est, mea, above, above_top, above_bot, rim_top, rim_bot, v_ref, l_ref,
    upd, o0, o1, o2, o3, optical, top, wh, wl, mh, ml, qh, ql, nh, nl,
):
    plane = pl.program_id(0)
    _, _, _, tile = place()
    rows, cols = optical.shape
    rim = 2 * HALF
    ends = lax.axis_size("tile") - 1
    join_top = jnp.where(tile > 0, seams[jnp.maximum(tile - 1, 0)], 0) == 1
    join_bot = jnp.where(tile < ends, seams[jnp.minimum(tile, ends - 1)], 0) == 1

    @pl.when(plane == 0)
    def _():
        optical[...] = above[...]
        for ref in (mh, ml, nh, nl):
            edge = jnp.zeros((ref.shape[0], 128), BF)
            ref[:, :128] = edge
            ref[:, ref.shape[1] - 128 :] = edge

    for joined, far, packed, at in (
        (join_top, above_top, rim_top, 0),
        (join_bot, above_bot, rim_bot, rows + rim),
    ):
        value = jnp.where(joined, jnp.exp(-far[...]) * packed[0, :rim], 0.0)
        wh[at : at + rim], wl[at : at + rim] = split(value)
    for r in range(0, rows, 64):
        depth = optical[r : r + 64]
        value = jnp.exp(-depth) * est[0, r : r + 64]
        wh[rim + r : rim + r + 64], wl[rim + r : rim + r + 64] = split(value)
        optical[r : r + 64] = depth + ext[0, r : r + 64]

    def vertical(way, sh, sl, dh, dl):
        total = dh.shape[0]
        for at in range(0, total, 192):
            m = min(192, total - at)
            depth = min(256, m + rim)
            th, tl = v_ref[0, way, 0, :m, :depth], v_ref[0, way, 1, :m, :depth]
            for c in range(0, cols, 256):
                result = dot3(th, tl, sh[at : at + depth, c : c + 256], sl[at : at + depth, c : c + 256])
                dh[at : at + m, 128 + c : 384 + c], dl[at : at + m, 128 + c : 384 + c] = split(result)

    vertical(0, wh, wl, mh, ml)
    lh, ll = l_ref.at[0, 0, 0], l_ref.at[0, 0, 1]
    for c in range(0, cols, 256):
        for a, b in ((0, 160), (160, 320)):
            blurred = dot3(mh[a:b, c : c + 512], ml[a:b, c : c + 512], lh[...], ll[...])
            s = slice(c, c + 256)
            if a == 0:
                halo = jnp.where(join_top, rim_top[0, rim:, s] / blurred[:HALF], 0.0)
                inner = mea[0, : b - HALF, s] / blurred[HALF:]
                qh[:HALF, s], ql[:HALF, s] = split(halo)
                qh[HALF:b, s], ql[HALF:b, s] = split(inner)
            else:
                halo = jnp.where(join_bot, rim_bot[0, rim:, s] / blurred[b - a - HALF :], 0.0)
                inner = mea[0, a - HALF :, s] / blurred[: b - a - HALF]
                qh[b - HALF :, s], ql[b - HALF :, s] = split(halo)
                qh[a : b - HALF, s], ql[a : b - HALF, s] = split(inner)

    vertical(1, qh, ql, nh, nl)
    lh, ll = l_ref.at[0, 1, 0], l_ref.at[0, 1, 1]
    for c in range(0, cols, 256):
        s = slice(c, c + 256)
        for a in range(0, rows, 128):
            t = slice(a, a + 128)
            spread = dot3(nh[t, c : c + 512], nl[t, c : c + 512], lh[...], ll[...])
            result = est[0, t, s] * spread
            upd[0, t, s] = result
            top[t, s] = jnp.maximum(jnp.where(plane == 0, result, top[t, s]), result)

    @pl.when(plane == pl.num_programs(0) - 1)
    def _():
        quarter = rows // 4
        for piece, (keep, give) in enumerate(((o0, o1), (o2, o3))):
            kept = side(piece)
            keep[...] = top[rows_at(2 * piece + kept, quarter)]
            give[...] = top[rows_at(2 * piece + 1 - kept, quarter)]


def step(seams, ext, est, mea, above, above_top, above_bot, rim_top, rim_bot, v, l):
    planes, rows, cols = ext.shape
    rim, quarter = 2 * HALF, rows // 4
    stack = pl.BlockSpec((1, rows, cols), lambda p: (p, 0, 0))
    pack = pl.BlockSpec((1, rim + HALF, cols), lambda p: (p, 0, 0))
    part = pl.BlockSpec((quarter, cols), lambda p: (0, 0))
    return pl.pallas_call(
        step_kernel,
        grid=(planes,),
        in_specs=[
            smem(), stack, stack, stack, whole(), whole(), whole(), pack, pack,
            pl.BlockSpec((1,) + v.shape[1:], lambda p: (p, 0, 0, 0, 0)),
            pl.BlockSpec((1,) + l.shape[1:], lambda p: (p, 0, 0, 0, 0)),
        ],
        out_specs=[stack] + [part] * 4,
        out_shape=[jax.ShapeDtypeStruct((planes, rows, cols), F32)]
        + [jax.ShapeDtypeStruct((quarter, cols), F32)] * 4,
        scratch_shapes=[
            pltpu.VMEM((rows, cols), F32),
            pltpu.VMEM((rows, cols), F32),
            pltpu.VMEM((rows + 2 * rim, cols), BF),
            pltpu.VMEM((rows + 2 * rim, cols), BF),
            pltpu.VMEM((rows + rim, cols + 256), BF),
            pltpu.VMEM((rows + rim, cols + 256), BF),
            pltpu.VMEM((rows + rim, cols), BF),
            pltpu.VMEM((rows + rim, cols), BF),
            pltpu.VMEM((rows, cols + 256), BF),
            pltpu.VMEM((rows, cols + 256), BF),
        ],
        compiler_params=params(44),
        cost_estimate=pl.CostEstimate(flops=12 << 30, bytes_accessed=24 << 20, transcendentals=1 << 20),
    )(seams, ext, est, mea, above, above_top, above_bot, rim_top, rim_bot, v, l)


def on_device(measured, estimate, extinction, psf_rows, psf_cols, stratum, seam_flags):
    rows = measured.shape[1]
    rim = 2 * HALF
    tiles = lax.axis_size("tile")
    onward = [(i, i + 1) for i in range(tiles - 1)]
    backward = [(i + 1, i) for i in range(tiles - 1)]
    above, (v, l) = above_of(sums(extinction), bands(psf_rows, psf_cols, stratum))
    up, down = rims(extinction, estimate, measured)
    rim_top = lax.ppermute(down, "tile", onward)
    rim_bot = lax.ppermute(up, "tile", backward)
    above_top = lax.ppermute(above[rows - rim :], "tile", onward)
    above_bot = lax.ppermute(above[:rim], "tile", backward)
    updated, keep_a, give_a, keep_b, give_b = step(
        seam_flags, extinction, estimate, measured, above, above_top, above_bot, rim_top, rim_bot, v, l
    )
    return updated, highest([(keep_a, give_a), (keep_b, give_b)])


def solution(mesh):
    return jax.shard_map(
        on_device,
        mesh=mesh,
        in_specs=(
            P("depth", "tile", None),
            P("depth", "tile", None),
            P("depth", "tile", None),
            P(),
            P(),
            P("depth"),
            P(),
        ),
        out_specs=(P("depth", "tile", None), P("tile", None)),
        check_vma=False,
    )
```

time: 158 us -> 122 us (0.77)
  the two profiles are of different devices: /device:TPU:0 before, /device:TPU:98 now
where the time goes in v2:
time: 122 us; the launch traced here: 121 us
  starting transfers between devices  40.2 us (33%)
  Pallas kernels  29.4 us (24%)
  waiting for transfers between devices  26.3 us (22%)
  blocking collectives  22.3 us (18%)
  other arithmetic  2.11 us (2%)
    ppermute x10, waiting for transfers between devices, swap(): lax.ppermute(value, ('depth', 'tile'), pairs(piece, number, lax.axis_size...  22.4 us
    all_to_all x1, blocking collectives, above_of(): lax.all_to_all(prefixes, 'depth', 0, 0, tiled=True).reshape(rows, cols)  22.3 us
    ppermute x10, starting transfers between devices, swap(): lax.ppermute(value, ('depth', 'tile'), pairs(piece, number, lax.axis_size...  21.4 us
    pallas_call x1, Pallas kernels, step(): pl.pallas_call(step_kernel, grid=(planes,), in_specs=[smem(), stack, stac...  16.4 us
    all_to_all x1, starting transfers between devices, above_of(): parts = lax.all_to_all(parts, 'depth', 0, 0, tiled=True)  7.49 us
    pallas_call x1, Pallas kernels, bands(): pl.pallas_call(bands_kernel, grid_spec=pltpu.PrefetchScalarGridSpec(num_s...  5.08 us
    pallas_call x1, Pallas kernels, rims(): pl.pallas_call(rims_kernel, grid=(planes,), in_specs=[top, bot, top, bot,...  4.64 us
    ppermute x1, starting transfers between devices, on_device(): rim_bot = lax.ppermute(up, 'tile', backward)  3.64 us
  transfers between devices with their start and end apart: 15, of which 10 were waited for; matrix products, arithmetic and copies ran while one was open for 1% of the time, Pallas kernels for 8%

profile of v2, /device:TPU:98, one launch (start us, length us, event | category | flops | bytes accessed | tf_op | source)
XLA Modules:
  0.0 121.4 jit_solution(16566370770439622792)
XLA Ops:
  0.6 3.2 %shard_map.86 = f32[256,1024]{1,0:T(8,128)} custom-call(f32[4,256,1024]{2,1,0:T(8,128)} %ext.3), custom_call_target="tpu_custom_call" | custom-call | tf_op jit(solution)/shard_map/pallas_call | solution.py:93
  3.9 7.5 %all-to-all-start = ((f32[16,16,1024]{2,1,0:T(8,128)}), f32[16,16,1024]{2,1,0:T(8,128)S(1)}, u32[]{:S(2)}, u32[]{:S(2)}) async-start(f32[16,16,1024]{2,1,0:T(8,128)} %bitcast.9), calls=%async_computation | async-start | bytes 2097152 | tf_op jit(solution)/shard_map/all_to_all | solution.py:154
  11.3 0.0 copy-start.2
  11.3 0.0 copy-start.3
  11.4 4.6 %shard_map.89 = (f32[4,96,1024]{2,1,0:T(8,128)}, f32[4,96,1024]{2,1,0:T(8,128)}) custom-call(f32[4,256,1024]{2,1,0:T(8,128)} %ext.3, f32[4,256,1024]{2,1,0:T(8,128)} %ext.3, f32[4,256,1024]{2,1,0:T(8,128)} %est.1, f32[4,256,1024]{2,1,0:T(8,128)} %est.1, f32[4,256,1024]{2,1,0:T(8,128)} %mea.1, f32[4,256,1024]{2,1,0:T(8,128)} %mea.1), custom_call_target="tpu_custom_call" | custom-call | flops 1048576 | bytes 8388608 | tf_op jit(solution)/shard_map/pallas_call | solution.py:126
  16.0 0.0 copy-start.1
  16.0 2.0 %collective-permute-start.2 = (f32[4,96,1024]{2,1,0:T(8,128)}, f32[4,96,1024]{2,1,0:T(8,128)S(1)}, u32[]{:S(2)}, u32[]{:S(2)}) collective-permute-start(f32[4,96,1024]{2,1,0:T(8,128)} %get-tuple-element.17), channel_id=1, source_target_pairs={{0,1},{1,2},{2,3},{3,4},{4,5},{5,6},{6,7},{8,9},{9,10},{10,11},{11... | collective-permute-start | bytes 4718600 | tf_op jit(solution)/shard_map/ppermute | solution.py:354
  18.1 3.6 %collective-permute-start.3 = (f32[4,96,1024]{2,1,0:T(8,128)}, f32[4,96,1024]{2,1,0:T(8,128)}, u32[]{:S(2)}, u32[]{:S(2)}) collective-permute-start(f32[4,96,1024]{2,1,0:T(8,128)} %get-tuple-element.18), channel_id=1, source_target_pairs={{1,0},{2,1},{3,2},{4,3},{5,4},{6,5},{7,6},{9,8},{10,9},{11,10},{12... | collective-permute-start | bytes 4718600 | tf_op jit(solution)/shard_map/ppermute | solution.py:355
  21.7 0.0 copy-done.2
  21.7 0.1 rev.7
  21.8 0.0 copy-done.3
  21.8 0.1 rev.6
  21.9 0.7 select_maximum_fusion.taps
  22.5 5.1 %shard_map.88 = (bf16[4,2,2,192,256]{4,3,2,1,0:T(8,128)(2,1)}, bf16[4,2,2,512,256]{4,3,2,1,0:T(8,128)(2,1)}) custom-call(s32[4]{0:T(128)} %stratum.1, f32[16,4,256]{2,1,0:T(4,128)} %select_maximum_fusion.taps), custom_call_target="tpu_custom_call" | custom-call | flops 4194304 | bytes 6291456 | tf_op jit(solution)/shard_map/pallas_call | solution.py:205
  27.6 0.0 all-to-all-done.parts
  27.6 0.0 copy-start
  27.6 0.1 shard_map.87
  27.7 22.3 %all_to_all.10 = f32[16,16,1024]{2,1,0:T(8,128)S(1)} all-to-all(f32[16,16,1024]{2,1,0:T(8,128)S(1)} %shard_map.87), channel_id=1, replica_groups=mesh['depth'=16,'tile'=8] {'depth'}, dimensions={0} | all-to-all | bytes 2097152 | tf_op jit(solution)/shard_map/all_to_all | solution.py:163
  50.0 1.9 %collective-permute-start = (f32[64,1024]{1,0:T(8,128)S(1)}, f32[64,1024]{1,0:T(8,128)S(1)}, u32[]{:S(2)}, u32[]{:S(2)}) collective-permute-start(f32[64,1024]{1,0:T(8,128)S(1)} %bitcast.11), channel_id=1, source_target_pairs={{0,1},{1,2},{2,3},{3,4},{4,5},{5,6},{6,7},{8,9},{9,10},{10,11},{11... | collective-permute-start | bytes 786440 | tf_op jit(solution)/shard_map/ppermute | solution.py:356
  52.0 3.6 %collective-permute-start.1 = (f32[64,1024]{1,0:T(8,128)S(1)}, f32[64,1024]{1,0:T(8,128)S(1)}, u32[]{:S(2)}, u32[]{:S(2)}) collective-permute-start(f32[64,1024]{1,0:T(8,128)S(1)} %bitcast.10), channel_id=1, source_target_pairs={{1,0},{2,1},{3,2},{4,3},{5,4},{6,5},{7,6},{9,8},{10,9},{11,10},{12... | collective-permute-start | bytes 786440 | tf_op jit(solution)/shard_map/ppermute | solution.py:357
  55.6 0.0 collective-permute-done.2.rim_top
  55.6 0.0 collective-permute-done.3.rim_bot
  55.6 2.1 %collective-permute-done.above_top = f32[64,1024]{1,0:T(8,128)S(1)} collective-permute-done((f32[64,1024]{1,0:T(8,128)S(1)}, f32[64,1024]{1,0:T(8,128)S(1)}, u32[]{:S(2)}, u32[]{:S(2)}) %collective-permute-start) | collective-permute-done | bytes 262176 | tf_op jit(solution)/shard_map/ppermute | solution.py:356
  57.7 1.8 %collective-permute-done.1.above_bot = f32[64,1024]{1,0:T(8,128)S(1)} collective-permute-done((f32[64,1024]{1,0:T(8,128)S(1)}, f32[64,1024]{1,0:T(8,128)S(1)}, u32[]{:S(2)}, u32[]{:S(2)}) %collective-permute-start.1) | collective-permute-done | bytes 262176 | tf_op jit(solution)/shard_map/ppermute | solution.py:357
  59.5 0.0 copy-done.1
  59.5 0.0 copy-done
  59.5 16.4 %shard_map.90 = (f32[4,256,1024]{2,1,0:T(8,128)}, f32[64,1024]{1,0:T(8,128)S(1)}, f32[64,1024]{1,0:T(8,128)S(1)}, f32[64,1024]{1,0:T(8,128)S(1)}, f32[64,1024]{1,0:T(8,128)S(1)}) custom-call(s32[7]{0:T(128)S(1)} %copy-done.1, f32[4,256,1024]{2,1,0:T(8,128)} %ext.3, f32[4,256,1024]{2,1,0:T(8,128)} %est.1, f32[4,256,1024]{2,1,0:T(8,128)} %mea.1, ...), custom_call_target="tpu_custom_call" | custom-call | flops 12884901888 | bytes 25165824 | tf_op jit(solution)/shard_map/pallas_call | solution.py:318
  75.9 1.9 %collective-permute-start.9 = (f32[64,1024]{1,0:T(8,128)S(1)}, f32[64,1024]{1,0:T(8,128)S(1)}, u32[]{:S(2)}, u32[]{:S(2)}) collective-permute-start(f32[64,1024]{1,0:T(8,128)S(1)} %get-tuple-element.25), channel_id=1, source_target_pairs={{0,32},{1,97},{2,34},{3,99},{4,36},{5,101},{6,38},{7,103},{8,40},{... | collective-permute-start | bytes 786440 | tf_op jit(solution)/shard_map/ppermute | solution.py:53
  77.8 0.4 collective-permute-start.4
  78.2 5.0 %collective-permute-done.9 = f32[64,1024]{1,0:T(8,128)S(1)} collective-permute-done((f32[64,1024]{1,0:T(8,128)S(1)}, f32[64,1024]{1,0:T(8,128)S(1)}, u32[]{:S(2)}, u32[]{:S(2)}) %collective-permute-start.9) | collective-permute-done | bytes 262176 | tf_op jit(solution)/shard_map/ppermute | solution.py:53
  83.2 1.6 %collective-permute-start.10 = (f32[64,1024]{1,0:T(8,128)S(1)}, f32[64,1024]{1,0:T(8,128)S(1)}, u32[]{:S(2)}, u32[]{:S(2)}) collective-permute-start(f32[64,1024]{1,0:T(8,128)S(1)} %max.28), channel_id=1, source_target_pairs={{0,96},{1,33},{2,98},{3,35},{4,100},{5,37},{6,102},{7,39},{8,104},... | collective-permute-start | bytes 786440 | tf_op jit(solution)/shard_map/ppermute | solution.py:53
  84.8 0.6 collective-permute-done.4
  85.5 1.2 collective-permute-start.5
  86.6 3.1 %collective-permute-done.10 = f32[64,1024]{1,0:T(8,128)S(1)} collective-permute-done((f32[64,1024]{1,0:T(8,128)S(1)}, f32[64,1024]{1,0:T(8,128)S(1)}, u32[]{:S(2)}, u32[]{:S(2)}) %collective-permute-start.10) | collective-permute-done | bytes 262176 | tf_op jit(solution)/shard_map/ppermute | solution.py:53
  89.7 0.8 collective-permute-start.11
  90.6 4.1 %collective-permute-done.5 = f32[64,1024]{1,0:T(8,128)S(1)} collective-permute-done((f32[64,1024]{1,0:T(8,128)S(1)}, f32[64,1024]{1,0:T(8,128)S(1)}, u32[]{:S(2)}, u32[]{:S(2)}) %collective-permute-start.5) | collective-permute-done | bytes 262176 | tf_op jit(solution)/shard_map/ppermute | solution.py:53
  94.8 1.7 %collective-permute-start.6 = (f32[64,1024]{1,0:T(8,128)S(1)}, f32[64,1024]{1,0:T(8,128)S(1)}, u32[]{:S(2)}, u32[]{:S(2)}) collective-permute-start(f32[64,1024]{1,0:T(8,128)S(1)} %max.25), channel_id=1, source_target_pairs={{0,32},{1,97},{2,34},{3,99},{4,36},{5,101},{6,38},{7,103},{8,40},{... | collective-permute-start | bytes 786440 | tf_op jit(solution)/shard_map/ppermute | solution.py:53
  96.4 0.0 collective-permute-done.11
  96.5 4.2 %collective-permute-start.12 = (f32[64,1024]{1,0:T(8,128)S(1)}, f32[64,1024]{1,0:T(8,128)S(1)}, u32[]{:S(2)}, u32[]{:S(2)}) collective-permute-start(f32[64,1024]{1,0:T(8,128)S(1)} %max.30), channel_id=1, source_target_pairs={{0,24},{1,9},{2,26},{3,11},{4,28},{5,13},{6,30},{7,15},{8,16},{9,1... | collective-permute-start | bytes 786440 | tf_op jit(solution)/shard_map/ppermute | solution.py:53
  100.7 1.8 %collective-permute-done.6 = f32[64,1024]{1,0:T(8,128)S(1)} collective-permute-done((f32[64,1024]{1,0:T(8,128)S(1)}, f32[64,1024]{1,0:T(8,128)S(1)}, u32[]{:S(2)}, u32[]{:S(2)}) %collective-permute-start.6) | collective-permute-done | bytes 262176 | tf_op jit(solution)/shard_map/ppermute | solution.py:53
  102.5 1.2 collective-permute-start.7
  103.7 1.6 %collective-permute-done.12 = f32[64,1024]{1,0:T(8,128)S(1)} collective-permute-done((f32[64,1024]{1,0:T(8,128)S(1)}, f32[64,1024]{1,0:T(8,128)S(1)}, u32[]{:S(2)}, u32[]{:S(2)}) %collective-permute-start.12) | collective-permute-done | bytes 262176 | tf_op jit(solution)/shard_map/ppermute | solution.py:53
  105.4 8.4 %collective-permute-start.13 = (f32[64,1024]{1,0:T(8,128)S(1)}, f32[64,1024]{1,0:T(8,128)S(1)}, u32[]{:S(2)}, u32[]{:S(2)}) collective-permute-start(f32[64,1024]{1,0:T(8,128)S(1)} %max.31), channel_id=1, source_target_pairs={{0,32},{1,97},{2,34},{3,99},{4,36},{5,101},{6,38},{7,103},{8,40},{... | collective-permute-start | bytes 786440 | tf_op jit(solution)/shard_map/ppermute | solution.py:53
  113.7 0.0 collective-permute-done.7
  113.8 0.1 collective-permute-start.8
  114.0 4.1 %collective-permute-done.13 = f32[64,1024]{1,0:T(8,128)S(1)} collective-permute-done((f32[64,1024]{1,0:T(8,128)S(1)}, f32[64,1024]{1,0:T(8,128)S(1)}, u32[]{:S(2)}, u32[]{:S(2)}) %collective-permute-start.13) | collective-permute-done | bytes 262176 | tf_op jit(solution)/shard_map/ppermute | solution.py:53
  118.1 2.1 %collective-permute-done.8 = f32[64,1024]{1,0:T(8,128)S(1)} collective-permute-done((f32[64,1024]{1,0:T(8,128)S(1)}, f32[64,1024]{1,0:T(8,128)S(1)}, u32[]{:S(2)}, u32[]{:S(2)}) %collective-permute-start.8) | collective-permute-done | bytes 262176 | tf_op jit(solution)/shard_map/ppermute | solution.py:53
  120.3 1.1 pad_maximum_fusion
  (11 shorter events, 0.4 us)
Async XLA Ops:
  3.9 23.8 %all-to-all-start = ((f32[16,16,1024]{2,1,0:T(8,128)}), f32[16,16,1024]{2,1,0:T(8,128)S(1)}, u32[]{:S(2)}, u32[]{:S(2)}) async-start(f32[16,16,1024]{2,1,0:T(8,128)} %bitcast.9), calls=%async_computation | async-start | bytes 2097152 | tf_op jit(solution)/shard_map/all_to_all | solution.py:154
  11.3 10.4 %copy-start.2 = (f32[16,65]{1,0:T(8,128)S(1)}, f32[16,65]{1,0:T(8,128)}, u32[]{:S(2)}) copy-start(f32[16,65]{1,0:T(8,128)} %param.11) | copy-start | bytes 12484
  11.3 10.4 %copy-start.3 = (f32[16,65]{1,0:T(8,128)S(1)}, f32[16,65]{1,0:T(8,128)}, u32[]{:S(2)}) copy-start(f32[16,65]{1,0:T(8,128)} %param.10) | copy-start | bytes 12484
  16.0 43.5 %copy-start.1 = (s32[7]{0:T(128)S(1)}, s32[7]{0:T(128)}, u32[]{:S(2)}) copy-start(s32[7]{0:T(128)} %seams.1) | copy-start | bytes 88
  16.0 39.6 %collective-permute-start.2 = (f32[4,96,1024]{2,1,0:T(8,128)}, f32[4,96,1024]{2,1,0:T(8,128)S(1)}, u32[]{:S(2)}, u32[]{:S(2)}) collective-permute-start(f32[4,96,1024]{2,1,0:T(8,128)} %get-tuple-element.17), channel_id=1, source_target_pairs={{0,1},{1,2},{2,3},{3,4},{4,5},{5,6},{6,7},{8,9},{9,10},{10,11},{11... | collective-permute-start | bytes 4718600 | tf_op jit(solution)/shard_map/ppermute | solution.py:354
  18.1 37.6 %collective-permute-start.3 = (f32[4,96,1024]{2,1,0:T(8,128)}, f32[4,96,1024]{2,1,0:T(8,128)}, u32[]{:S(2)}, u32[]{:S(2)}) collective-permute-start(f32[4,96,1024]{2,1,0:T(8,128)} %get-tuple-element.18), channel_id=1, source_target_pairs={{1,0},{2,1},{3,2},{4,3},{5,4},{6,5},{7,6},{9,8},{10,9},{11,10},{12... | collective-permute-start | bytes 4718600 | tf_op jit(solution)/shard_map/ppermute | solution.py:355
  27.6 31.9 %copy-start = (bf16[4,2,2,192,256]{4,3,2,1,0:T(8,128)(2,1)S(1)}, bf16[4,2,2,192,256]{4,3,2,1,0:T(8,128)(2,1)}, u32[]{:S(2)}) copy-start(bf16[4,2,2,192,256]{4,3,2,1,0:T(8,128)(2,1)} %get-tuple-element.19.v_ref) | copy-start | bytes 4718596
  50.0 7.7 %collective-permute-start = (f32[64,1024]{1,0:T(8,128)S(1)}, f32[64,1024]{1,0:T(8,128)S(1)}, u32[]{:S(2)}, u32[]{:S(2)}) collective-permute-start(f32[64,1024]{1,0:T(8,128)S(1)} %bitcast.11), channel_id=1, source_target_pairs={{0,1},{1,2},{2,3},{3,4},{4,5},{5,6},{6,7},{8,9},{9,10},{10,11},{11... | collective-permute-start | bytes 786440 | tf_op jit(solution)/shard_map/ppermute | solution.py:356
  52.0 7.5 %collective-permute-start.1 = (f32[64,1024]{1,0:T(8,128)S(1)}, f32[64,1024]{1,0:T(8,128)S(1)}, u32[]{:S(2)}, u32[]{:S(2)}) collective-permute-start(f32[64,1024]{1,0:T(8,128)S(1)} %bitcast.10), channel_id=1, source_target_pairs={{1,0},{2,1},{3,2},{4,3},{5,4},{6,5},{7,6},{9,8},{10,9},{11,10},{12... | collective-permute-start | bytes 786440 | tf_op jit(solution)/shard_map/ppermute | solution.py:357
  75.9 7.3 %collective-permute-start.9 = (f32[64,1024]{1,0:T(8,128)S(1)}, f32[64,1024]{1,0:T(8,128)S(1)}, u32[]{:S(2)}, u32[]{:S(2)}) collective-permute-start(f32[64,1024]{1,0:T(8,128)S(1)} %get-tuple-element.25), channel_id=1, source_target_pairs={{0,32},{1,97},{2,34},{3,99},{4,36},{5,101},{6,38},{7,103},{8,40},{... | collective-permute-start | bytes 786440 | tf_op jit(solution)/shard_map/ppermute | solution.py:53
  77.8 7.6 %collective-permute-start.4 = (f32[64,1024]{1,0:T(8,128)S(1)}, f32[64,1024]{1,0:T(8,128)S(1)}, u32[]{:S(2)}, u32[]{:S(2)}) collective-permute-start(f32[64,1024]{1,0:T(8,128)S(1)} %get-tuple-element.23), channel_id=1, source_target_pairs={{0,8},{1,25},{2,10},{3,27},{4,12},{5,29},{6,14},{7,31},{8,0},{9,17... | collective-permute-start | bytes 786440 | tf_op jit(solution)/shard_map/ppermute | solution.py:53
  83.2 6.5 %collective-permute-start.10 = (f32[64,1024]{1,0:T(8,128)S(1)}, f32[64,1024]{1,0:T(8,128)S(1)}, u32[]{:S(2)}, u32[]{:S(2)}) collective-permute-start(f32[64,1024]{1,0:T(8,128)S(1)} %max.28), channel_id=1, source_target_pairs={{0,96},{1,33},{2,98},{3,35},{4,100},{5,37},{6,102},{7,39},{8,104},... | collective-permute-start | bytes 786440 | tf_op jit(solution)/shard_map/ppermute | solution.py:53
  85.5 9.2 %collective-permute-start.5 = (f32[64,1024]{1,0:T(8,128)S(1)}, f32[64,1024]{1,0:T(8,128)S(1)}, u32[]{:S(2)}, u32[]{:S(2)}) collective-permute-start(f32[64,1024]{1,0:T(8,128)S(1)} %max.24), channel_id=1, source_target_pairs={{0,24},{1,9},{2,26},{3,11},{4,28},{5,13},{6,30},{7,15},{8,16},{9,1... | collective-permute-start | bytes 786440 | tf_op jit(solution)/shard_map/ppermute | solution.py:53
  89.7 6.7 %collective-permute-start.11 = (f32[64,1024]{1,0:T(8,128)S(1)}, f32[64,1024]{1,0:T(8,128)S(1)}, u32[]{:S(2)}, u32[]{:S(2)}) collective-permute-start(f32[64,1024]{1,0:T(8,128)S(1)} %max.29), channel_id=1, source_target_pairs={{0,8},{1,25},{2,10},{3,27},{4,12},{5,29},{6,14},{7,31},{8,0},{9,17... | collective-permute-start | bytes 786440 | tf_op jit(solution)/shard_map/ppermute | solution.py:53
  94.8 7.7 %collective-permute-start.6 = (f32[64,1024]{1,0:T(8,128)S(1)}, f32[64,1024]{1,0:T(8,128)S(1)}, u32[]{:S(2)}, u32[]{:S(2)}) collective-permute-start(f32[64,1024]{1,0:T(8,128)S(1)} %max.25), channel_id=1, source_target_pairs={{0,32},{1,97},{2,34},{3,99},{4,36},{5,101},{6,38},{7,103},{8,40},{... | collective-permute-start | bytes 786440 | tf_op jit(solution)/shard_map/ppermute | solution.py:53
  96.5 8.8 %collective-permute-start.12 = (f32[64,1024]{1,0:T(8,128)S(1)}, f32[64,1024]{1,0:T(8,128)S(1)}, u32[]{:S(2)}, u32[]{:S(2)}) collective-permute-start(f32[64,1024]{1,0:T(8,128)S(1)} %max.30), channel_id=1, source_target_pairs={{0,24},{1,9},{2,26},{3,11},{4,28},{5,13},{6,30},{7,15},{8,16},{9,1... | collective-permute-start | bytes 786440 | tf_op jit(solution)/shard_map/ppermute | solution.py:53
  102.5 11.2 %collective-permute-start.7 = (f32[64,1024]{1,0:T(8,128)S(1)}, f32[64,1024]{1,0:T(8,128)S(1)}, u32[]{:S(2)}, u32[]{:S(2)}) collective-permute-start(f32[64,1024]{1,0:T(8,128)S(1)} %max.26), channel_id=1, source_target_pairs={{0,96},{1,33},{2,98},{3,35},{4,100},{5,37},{6,102},{7,39},{8,104},... | collective-permute-start | bytes 786440 | tf_op jit(solution)/shard_map/ppermute | solution.py:53
  105.4 12.7 %collective-permute-start.13 = (f32[64,1024]{1,0:T(8,128)S(1)}, f32[64,1024]{1,0:T(8,128)S(1)}, u32[]{:S(2)}, u32[]{:S(2)}) collective-permute-start(f32[64,1024]{1,0:T(8,128)S(1)} %max.31), channel_id=1, source_target_pairs={{0,32},{1,97},{2,34},{3,99},{4,36},{5,101},{6,38},{7,103},{8,40},{... | collective-permute-start | bytes 786440 | tf_op jit(solution)/shard_map/ppermute | solution.py:53
  113.8 6.5 %collective-permute-start.8 = (f32[64,1024]{1,0:T(8,128)S(1)}, f32[64,1024]{1,0:T(8,128)S(1)}, u32[]{:S(2)}, u32[]{:S(2)}) collective-permute-start(f32[64,1024]{1,0:T(8,128)S(1)} %max.27), channel_id=1, source_target_pairs={{0,8},{1,25},{2,10},{3,27},{4,12},{5,29},{6,14},{7,31},{8,0},{9,17... | collective-permute-start | bytes 786440 | tf_op jit(solution)/shard_map/ppermute | solution.py:53

commit v3 on v2

--- a/solution.py
+++ b/solution.py
@@ -24,18 +24,10 @@
     return pl.BlockSpec(memory_space=pltpu.SMEM)
 
 
-def place():
-    depth = lax.axis_index("depth")
-    tile = lax.axis_index("tile")
-    return depth // SIDE, depth % SIDE, tile % 2, tile
-
-
-PAIRINGS = {
-    (0, 0): (("y", 1), ("y", 3), ("x", 1), ("x", 3)),
-    (0, 1): (("x", 1), ("x", 3), ("y", 1), ("y", 3)),
-    (1, 0): (("y", 3), ("y", 1), ("x", 3), ("x", 1)),
-    (1, 1): (("x", 3), ("x", 1), ("y", 3), ("y", 1)),
-}
+PAIRINGS = (
+    (("y", 1), ("y", 3), ("x", 1), ("x", 3)),
+    (("x", 1), ("x", 3), ("y", 1), ("y", 3)),
+)
 
 
 def pairs(piece, number, tiles):
@@ -43,7 +35,7 @@
     for x in range(SIDE):
         for y in range(SIDE):
             for tile in range(tiles):
-                axis, flip = PAIRINGS[(tile % 2, piece)][number]
+                axis, flip = PAIRINGS[piece][number]
                 tx, ty = (x, y ^ flip) if axis == "y" else (x ^ flip, y)
                 result.append(((x * SIDE + y) * tiles + tile, (tx * SIDE + ty) * tiles + tile))
     return result
@@ -54,13 +46,10 @@
 
 
 def side(piece):
-    x, y, core, _ = place()
-    bits = []
-    for c in range(2):
-        axis, flip = PAIRINGS[(c, piece)][0]
-        value = y if axis == "y" else x
-        bits.append((value + 1) // 2 % 2 if flip == 1 else value // 2)
-    return jnp.where(core == 0, bits[0], bits[1])
+    depth = lax.axis_index("depth")
+    axis, _ = PAIRINGS[piece][0]
+    value = depth % SIDE if axis == "y" else depth // SIDE
+    return (value + 1) // 2 % 2
 
 
 def split(value):
@@ -100,43 +89,44 @@
     )(extinction)
 
 
-def rims_kernel(ext_top, ext_bot, est_top, est_bot, mea_top, mea_bot, up, down, acc_top, acc_bot):
+def rims_kernel(ext, est, mea, up, down, ext_buf, est_buf, mea_buf, sems):
     rim = 2 * HALF
-    for ext, est, mea, out, acc in (
-        (ext_top, est_top, mea_top, up, acc_top),
-        (ext_bot, est_bot, mea_bot, down, acc_bot),
-    ):
-
-        @pl.when(pl.program_id(0) == 0)
-        def _():
-            acc[...] = jnp.zeros_like(acc)
-
-        out[0, :rim] = jnp.exp(-acc[...]) * est[0]
-        out[0, rim:] = mea[0]
-        acc[...] += ext[0]
+    planes, rows, _ = ext.shape
+    ends = ((0, 0, up), (rows - rim, rows - HALF, down))
+    copies = []
+    for i, (wide, narrow, _) in enumerate(ends):
+        for j, (source, buf, at, size) in enumerate(
+            ((ext, ext_buf, wide, rim), (est, est_buf, wide, rim), (mea, mea_buf, narrow, HALF))
+        ):
+            copies.append(pltpu.make_async_copy(source.at[:, pl.ds(at, size)], buf.at[i], sems.at[3 * i + j]))
+            copies[-1].start()
+    for i, (_, _, out) in enumerate(ends):
+        for copy in copies[3 * i : 3 * i + 3]:
+            copy.wait()
+        depth = jnp.zeros(ext_buf.shape[2:], F32)
+        for plane in range(planes):
+            out[plane, :rim] = jnp.exp(-depth) * est_buf[i, plane]
+            out[plane, rim:] = mea_buf[i, plane]
+            depth = depth + ext_buf[i, plane]
 
 
 def rims(extinction, estimate, measured):
     planes, rows, cols = extinction.shape
     rim = 2 * HALF
-    far = rows // rim - 1
-    top = pl.BlockSpec((1, rim, cols), lambda p: (p, 0, 0))
-    bot = pl.BlockSpec((1, rim, cols), lambda p: (p, far, 0))
-    out = pl.BlockSpec((1, rim + HALF, cols), lambda p: (p, 0, 0))
     return pl.pallas_call(
         rims_kernel,
-        grid=(planes,),
-        in_specs=[
-            top, bot, top, bot,
-            pl.BlockSpec((1, HALF, cols), lambda p: (p, 0, 0)),
-            pl.BlockSpec((1, HALF, cols), lambda p: (p, rows // HALF - 1, 0)),
+        in_specs=[pl.BlockSpec(memory_space=pl.ANY)] * 3,
+        out_specs=[whole()] * 2,
+        out_shape=[jax.ShapeDtypeStruct((planes, rim + HALF, cols), F32)] * 2,
+        scratch_shapes=[
+            pltpu.VMEM((2, planes, rim, cols), F32),
+            pltpu.VMEM((2, planes, rim, cols), F32),
+            pltpu.VMEM((2, planes, HALF, cols), F32),
+            pltpu.SemaphoreType.DMA((6,)),
         ],
-        out_specs=[out, out],
-        out_shape=[jax.ShapeDtypeStruct((planes, rim + HALF, cols), F32)] * 2,
-        scratch_shapes=[pltpu.VMEM((rim, cols), F32)] * 2,
         compiler_params=params(60),
         cost_estimate=pl.CostEstimate(flops=1 << 20, bytes_accessed=8 << 20, transcendentals=1 << 19),
-    )(extinction, extinction, estimate, estimate, measured, measured)
+    )(extinction, estimate, measured)
 
 
 def scan_kernel(parts, out):
@@ -192,10 +182,12 @@
         main = jnp.where(jnp.abs(n - k) <= HALF, ring, zero)
         left = jnp.where(k - n > HALF, ring, zero)[128:]
         right = jnp.where(n - k > HALF, ring, zero)[:128]
-        for at, part in ((0, left), (128, main), (384, right)):
-            high, low = split(part)
-            l_ref[0, way, 0, at : at + part.shape[0]] = high
-            l_ref[0, way, 1, at : at + part.shape[0]] = low
+        l_ref[0, way, :256], l_ref[0, way, 256:512] = split(main)
+        high, low = split(left + right)
+        pair = jnp.concatenate([high[:HALF], high[128 - HALF :]], axis=0)
+        l_ref[0, way, 512 : 512 + 2 * HALF] = pair
+        l_ref[0, way, 512 + 2 * HALF : 640] = pair
+        l_ref[0, way, 640:] = low
 
 
 def bands(psf_rows, psf_cols, stratum):
@@ -210,12 +202,12 @@
             in_specs=[pl.BlockSpec((1, 4, 256), lambda p, s: (s[p], 0, 0))],
             out_specs=[
                 pl.BlockSpec((1, 2, 2, 192, 256), lambda p, s: (p, 0, 0, 0, 0)),
-                pl.BlockSpec((1, 2, 2, 512, 256), lambda p, s: (p, 0, 0, 0, 0)),
+                pl.BlockSpec((1, 2, 768, 256), lambda p, s: (p, 0, 0, 0)),
             ],
         ),
         out_shape=[
             jax.ShapeDtypeStruct((planes, 2, 2, 192, 256), BF),
-            jax.ShapeDtypeStruct((planes, 2, 2, 512, 256), BF),
+            jax.ShapeDtypeStruct((planes, 2, 768, 256), BF),
         ],
         compiler_params=params(60),
         cost_estimate=pl.CostEstimate(flops=1 << 22, bytes_accessed=6 << 20, transcendentals=0),
@@ -226,16 +218,35 @@
     return jnp.dot(a, b, preferred_element_type=F32)
 
 
-def dot3(a_high, a_low, b_high, b_low):
-    return dot(a_high, b_high) + (dot(a_high, b_low) + dot(a_low, b_high))
+def corners(high, low, out):
+    for c in range(0, out.shape[1], 256):
+        left, right = slice(c, c + 128), slice(c + 384, c + 512)
+        for r in range(0, out.shape[0], 64):
+            t = slice(r, r + 64)
+            lane = lax.broadcasted_iota(jnp.int32, (64, 128), 1)
+            near = lane < 64
+            h = jnp.where(near, high[t, right].astype(F32), high[t, left].astype(F32))
+            w = jnp.where(near, low[t, right].astype(F32), low[t, left].astype(F32))
+            between = (lane >= HALF) & (lane < 128 - HALF)
+            out[t, c : c + 128] = jnp.where(between, pltpu.roll(w, 64, 1), h).astype(BF)
+            out[t, c + 128 : c + 256] = h.astype(BF)
+
+
+def lateral(high, low, corner, rows, c, band):
+    s = slice(c + 128, c + 384)
+    source = jnp.concatenate(
+        [high[rows, s], high[rows, s], low[rows, s], corner[rows, c : c + 256]], axis=1
+    )
+    weights = jnp.concatenate([band[:512], band[:256], band[512:]], axis=0)
+    return dot(source, weights)
 
 
 def step_kernel(
     seams, ext, est, mea, above, above_top, above_bot, rim_top, rim_bot, v_ref, l_ref,
-    upd, o0, o1, o2, o3, optical, top, wh, wl, mh, ml, qh, ql, nh, nl,
+    upd, o0, o1, o2, o3, optical, top, wh, wl, mh, ml, qh, ql, nh, nl, corner,
 ):
     plane = pl.program_id(0)
-    _, _, _, tile = place()
+    tile = lax.axis_index("tile")
     rows, cols = optical.shape
     rim = 2 * HALF
     ends = lax.axis_size("tile") - 1
@@ -269,36 +280,30 @@
             depth = min(256, m + rim)
             th, tl = v_ref[0, way, 0, :m, :depth], v_ref[0, way, 1, :m, :depth]
             for c in range(0, cols, 256):
-                result = dot3(th, tl, sh[at : at + depth, c : c + 256], sl[at : at + depth, c : c + 256])
+                both = dot(jnp.concatenate([th, tl], axis=0), sh[at : at + depth, c : c + 256])
+                result = both[:m] + (both[m:] + dot(th, sl[at : at + depth, c : c + 256]))
                 dh[at : at + m, 128 + c : 384 + c], dl[at : at + m, 128 + c : 384 + c] = split(result)
 
     vertical(0, wh, wl, mh, ml)
-    lh, ll = l_ref.at[0, 0, 0], l_ref.at[0, 0, 1]
-    for c in range(0, cols, 256):
-        for a, b in ((0, 160), (160, 320)):
-            blurred = dot3(mh[a:b, c : c + 512], ml[a:b, c : c + 512], lh[...], ll[...])
-            s = slice(c, c + 256)
-            if a == 0:
-                halo = jnp.where(join_top, rim_top[0, rim:, s] / blurred[:HALF], 0.0)
-                inner = mea[0, : b - HALF, s] / blurred[HALF:]
-                qh[:HALF, s], ql[:HALF, s] = split(halo)
-                qh[HALF:b, s], ql[HALF:b, s] = split(inner)
-            else:
-                halo = jnp.where(join_bot, rim_bot[0, rim:, s] / blurred[b - a - HALF :], 0.0)
-                inner = mea[0, a - HALF :, s] / blurred[: b - a - HALF]
-                qh[b - HALF :, s], ql[b - HALF :, s] = split(halo)
-                qh[a : b - HALF, s], ql[a : b - HALF, s] = split(inner)
-
-    vertical(1, qh, ql, nh, nl)
-    lh, ll = l_ref.at[0, 1, 0], l_ref.at[0, 1, 1]
+    corners(mh, ml, corner)
     for c in range(0, cols, 256):
         s = slice(c, c + 256)
-        for a in range(0, rows, 128):
-            t = slice(a, a + 128)
-            spread = dot3(nh[t, c : c + 512], nl[t, c : c + 512], lh[...], ll[...])
-            result = est[0, t, s] * spread
-            upd[0, t, s] = result
-            top[t, s] = jnp.maximum(jnp.where(plane == 0, result, top[t, s]), result)
+        blurred = lateral(mh, ml, corner, slice(0, rows + rim), c, l_ref.at[0, 0])
+        q0 = jnp.where(join_top, rim_top[0, rim:, s] / blurred[:HALF], 0.0)
+        q1 = mea[0, :, s] / blurred[HALF : HALF + rows]
+        q2 = jnp.where(join_bot, rim_bot[0, rim:, s] / blurred[HALF + rows :], 0.0)
+        qh[:HALF, s], ql[:HALF, s] = split(q0)
+        qh[HALF : HALF + rows, s], ql[HALF : HALF + rows, s] = split(q1)
+        qh[HALF + rows :, s], ql[HALF + rows :, s] = split(q2)
+
+    vertical(1, qh, ql, nh, nl)
+    ours = corner.at[pl.ds(0, rows)]
+    corners(nh, nl, ours)
+    for c in range(0, cols, 256):
+        s = slice(c, c + 256)
+        result = est[0, :, s] * lateral(nh, nl, ours, slice(0, rows), c, l_ref.at[0, 1])
+        upd[0, :, s] = result
+        top[:, s] = jnp.maximum(jnp.where(plane == 0, result, top[:, s]), result)
 
     @pl.when(plane == pl.num_programs(0) - 1)
     def _():
@@ -321,7 +326,7 @@
         in_specs=[
             smem(), stack, stack, stack, whole(), whole(), whole(), pack, pack,
             pl.BlockSpec((1,) + v.shape[1:], lambda p: (p, 0, 0, 0, 0)),
-            pl.BlockSpec((1,) + l.shape[1:], lambda p: (p, 0, 0, 0, 0)),
+            pl.BlockSpec((1,) + l.shape[1:], lambda p: (p, 0, 0, 0)),
         ],
         out_specs=[stack] + [part] * 4,
         out_shape=[jax.ShapeDtypeStruct((planes, rows, cols), F32)]
@@ -337,6 +342,7 @@
             pltpu.VMEM((rows + rim, cols), BF),
             pltpu.VMEM((rows, cols + 256), BF),
             pltpu.VMEM((rows, cols + 256), BF),
+            pltpu.VMEM((rows + rim, cols), BF),
         ],
         compiler_params=params(44),
         cost_estimate=pl.CostEstimate(flops=12 << 30, bytes_accessed=24 << 20, transcendentals=1 << 20),

time: 122 us -> 120 us (0.984)
  the two profiles are of different devices: /device:TPU:98 before, /device:TPU:32 now
where the time goes in v3:
time: 120 us; the launch traced here: 119 us
  waiting for transfers between devices  42.2 us (35%)
  Pallas kernels  26.6 us (22%)
  starting transfers between devices  24.6 us (20%)
  blocking collectives  22.5 us (19%)
  other arithmetic  2.11 us (2%)
    ppermute x10, waiting for transfers between devices, swap(): lax.ppermute(value, ('depth', 'tile'), pairs(piece, number, lax.axis_size...  36.2 us
    all_to_all x1, blocking collectives, above_of(): lax.all_to_all(prefixes, 'depth', 0, 0, tiled=True).reshape(rows, cols)  22.5 us
    pallas_call x1, Pallas kernels, step(): pl.pallas_call(step_kernel, grid=(planes,), in_specs=[smem(), stack, stac...  14.2 us
    all_to_all x1, starting transfers between devices, above_of(): parts = lax.all_to_all(parts, 'depth', 0, 0, tiled=True)  7.05 us
    ppermute x10, starting transfers between devices, swap(): lax.ppermute(value, ('depth', 'tile'), pairs(piece, number, lax.axis_size...  6.43 us
    pallas_call x1, Pallas kernels, bands(): pl.pallas_call(bands_kernel, grid_spec=pltpu.PrefetchScalarGridSpec(num_s...  4.8 us
    pallas_call x1, Pallas kernels, rims(): pl.pallas_call(rims_kernel, in_specs=[pl.BlockSpec(memory_space=pl.ANY)]...  4.23 us
    ppermute x1, starting transfers between devices, on_device(): rim_bot = lax.ppermute(up, 'tile', backward)  3.64 us
  transfers between devices with their start and end apart: 15, of which 12 were waited for; matrix products, arithmetic and copies ran while one was open for 1% of the time, Pallas kernels for 8%

profile of v3, /device:TPU:32, one launch (start us, length us, event | category | flops | bytes accessed | tf_op | source)
XLA Modules:
  0.0 119.1 jit_solution(4045729970178576400)
XLA Ops:
  0.6 3.2 %shard_map.86 = f32[256,1024]{1,0:T(8,128)} custom-call(f32[4,256,1024]{2,1,0:T(8,128)} %ext.5), custom_call_target="tpu_custom_call" | custom-call | tf_op jit(solution)/shard_map/pallas_call | solution.py:82
  3.9 7.0 %all-to-all-start = ((f32[16,16,1024]{2,1,0:T(8,128)}), f32[16,16,1024]{2,1,0:T(8,128)S(1)}, u32[]{:S(2)}, u32[]{:S(2)}) async-start(f32[16,16,1024]{2,1,0:T(8,128)} %bitcast.9), calls=%async_computation | async-start | bytes 2097152 | tf_op jit(solution)/shard_map/all_to_all | solution.py:144
  10.9 0.0 copy-start.2
  10.9 0.0 copy-start.3
  10.9 4.2 %shard_map.89 = (f32[4,96,1024]{2,1,0:T(8,128)}, f32[4,96,1024]{2,1,0:T(8,128)}) custom-call(f32[4,256,1024]{2,1,0:T(8,128)} %ext.5, f32[4,256,1024]{2,1,0:T(8,128)} %est.3, f32[4,256,1024]{2,1,0:T(8,128)} %mea.3), custom_call_target="tpu_custom_call" | custom-call | flops 1048576 | bytes 8388608 | tf_op jit(solution)/shard_map/pallas_call | solution.py:116
  15.2 0.0 copy-start.1
  15.2 1.9 %collective-permute-start.2 = (f32[4,96,1024]{2,1,0:T(8,128)}, f32[4,96,1024]{2,1,0:T(8,128)S(1)}, u32[]{:S(2)}, u32[]{:S(2)}) collective-permute-start(f32[4,96,1024]{2,1,0:T(8,128)} %get-tuple-element.17), channel_id=1, source_target_pairs={{0,1},{1,2},{2,3},{3,4},{4,5},{5,6},{6,7},{8,9},{9,10},{10,11},{11... | collective-permute-start | bytes 4718600 | tf_op jit(solution)/shard_map/ppermute | solution.py:360
  17.1 3.6 %collective-permute-start.3 = (f32[4,96,1024]{2,1,0:T(8,128)}, f32[4,96,1024]{2,1,0:T(8,128)}, u32[]{:S(2)}, u32[]{:S(2)}) collective-permute-start(f32[4,96,1024]{2,1,0:T(8,128)} %get-tuple-element.18), channel_id=1, source_target_pairs={{1,0},{2,1},{3,2},{4,3},{5,4},{6,5},{7,6},{9,8},{10,9},{11,10},{12... | collective-permute-start | bytes 4718600 | tf_op jit(solution)/shard_map/ppermute | solution.py:361
  20.8 0.0 copy-done.2
  20.8 0.1 rev.7
  20.8 0.0 copy-done.3
  20.8 0.1 rev.6
  20.9 0.7 select_maximum_fusion.taps
  21.6 4.8 %shard_map.88 = (bf16[4,2,2,192,256]{4,3,2,1,0:T(8,128)(2,1)}, bf16[4,2,768,256]{3,2,1,0:T(8,128)(2,1)}) custom-call(s32[4]{0:T(128)} %stratum.1, f32[16,4,256]{2,1,0:T(4,128)} %select_maximum_fusion.taps), custom_call_target="tpu_custom_call" | custom-call | flops 4194304 | bytes 6291456 | tf_op jit(solution)/shard_map/pallas_call | solution.py:197
  26.4 2.2 %all-to-all-done.parts = f32[16,16,1024]{2,1,0:T(8,128)S(1)} async-done(((f32[16,16,1024]{2,1,0:T(8,128)}), f32[16,16,1024]{2,1,0:T(8,128)S(1)}, u32[]{:S(2)}, u32[]{:S(2)}) %all-to-all-start) | async-done | bytes 1048608 | tf_op jit(solution)/shard_map/all_to_all | solution.py:144
  28.6 0.0 copy-start
  28.6 0.1 shard_map.87
  28.7 22.5 %all_to_all.10 = f32[16,16,1024]{2,1,0:T(8,128)S(1)} all-to-all(f32[16,16,1024]{2,1,0:T(8,128)S(1)} %shard_map.87), channel_id=1, replica_groups=mesh['depth'=16,'tile'=8] {'depth'}, dimensions={0} | all-to-all | bytes 2097152 | tf_op jit(solution)/shard_map/all_to_all | solution.py:153
  51.3 1.9 %collective-permute-start = (f32[64,1024]{1,0:T(8,128)S(1)}, f32[64,1024]{1,0:T(8,128)S(1)}, u32[]{:S(2)}, u32[]{:S(2)}) collective-permute-start(f32[64,1024]{1,0:T(8,128)S(1)} %bitcast.11), channel_id=1, source_target_pairs={{0,1},{1,2},{2,3},{3,4},{4,5},{5,6},{6,7},{8,9},{9,10},{10,11},{11... | collective-permute-start | bytes 786440 | tf_op jit(solution)/shard_map/ppermute | solution.py:362
  53.2 3.6 %collective-permute-start.1 = (f32[64,1024]{1,0:T(8,128)S(1)}, f32[64,1024]{1,0:T(8,128)S(1)}, u32[]{:S(2)}, u32[]{:S(2)}) collective-permute-start(f32[64,1024]{1,0:T(8,128)S(1)} %bitcast.10), channel_id=1, source_target_pairs={{1,0},{2,1},{3,2},{4,3},{5,4},{6,5},{7,6},{9,8},{10,9},{11,10},{12... | collective-permute-start | bytes 786440 | tf_op jit(solution)/shard_map/ppermute | solution.py:363
  56.8 0.0 collective-permute-done.2.rim_top
  56.8 0.0 collective-permute-done.3.rim_bot
  56.9 2.1 %collective-permute-done.above_top = f32[64,1024]{1,0:T(8,128)S(1)} collective-permute-done((f32[64,1024]{1,0:T(8,128)S(1)}, f32[64,1024]{1,0:T(8,128)S(1)}, u32[]{:S(2)}, u32[]{:S(2)}) %collective-permute-start) | collective-permute-done | bytes 262176 | tf_op jit(solution)/shard_map/ppermute | solution.py:362
  58.9 1.8 %collective-permute-done.1.above_bot = f32[64,1024]{1,0:T(8,128)S(1)} collective-permute-done((f32[64,1024]{1,0:T(8,128)S(1)}, f32[64,1024]{1,0:T(8,128)S(1)}, u32[]{:S(2)}, u32[]{:S(2)}) %collective-permute-start.1) | collective-permute-done | bytes 262176 | tf_op jit(solution)/shard_map/ppermute | solution.py:363
  60.7 0.0 copy-done.1
  60.7 0.0 copy-done
  60.7 14.2 %shard_map.90 = (f32[4,256,1024]{2,1,0:T(8,128)}, f32[64,1024]{1,0:T(8,128)S(1)}, f32[64,1024]{1,0:T(8,128)S(1)}, f32[64,1024]{1,0:T(8,128)S(1)}, f32[64,1024]{1,0:T(8,128)S(1)}) custom-call(s32[7]{0:T(128)S(1)} %copy-done.1, f32[4,256,1024]{2,1,0:T(8,128)} %ext.5, f32[4,256,1024]{2,1,0:T(8,128)} %est.3, f32[4,256,1024]{2,1,0:T(8,128)} %mea.3, ...), custom_call_target="tpu_custom_call" | custom-call | flops 12884901888 | bytes 25165824 | tf_op jit(solution)/shard_map/pallas_call | solution.py:323
  74.9 0.0 collective-permute-start.9
  74.9 0.6 collective-permute-start.4
  75.5 8.0 %collective-permute-done.9 = f32[64,1024]{1,0:T(8,128)S(1)} collective-permute-done((f32[64,1024]{1,0:T(8,128)S(1)}, f32[64,1024]{1,0:T(8,128)S(1)}, u32[]{:S(2)}, u32[]{:S(2)}) %collective-permute-start.9) | collective-permute-done | bytes 262176 | tf_op jit(solution)/shard_map/ppermute | solution.py:45
  83.5 0.8 collective-permute-start.10
  84.3 0.0 collective-permute-done.4
  84.3 0.8 collective-permute-start.5
  85.2 8.3 %collective-permute-done.10 = f32[64,1024]{1,0:T(8,128)S(1)} collective-permute-done((f32[64,1024]{1,0:T(8,128)S(1)}, f32[64,1024]{1,0:T(8,128)S(1)}, u32[]{:S(2)}, u32[]{:S(2)}) %collective-permute-start.10) | collective-permute-done | bytes 262176 | tf_op jit(solution)/shard_map/ppermute | solution.py:45
  93.5 0.6 collective-permute-start.11
  94.2 0.5 collective-permute-done.5
  94.7 1.0 collective-permute-start.6
  95.6 5.8 %collective-permute-done.11 = f32[64,1024]{1,0:T(8,128)S(1)} collective-permute-done((f32[64,1024]{1,0:T(8,128)S(1)}, f32[64,1024]{1,0:T(8,128)S(1)}, u32[]{:S(2)}, u32[]{:S(2)}) %collective-permute-start.11) | collective-permute-done | bytes 262176 | tf_op jit(solution)/shard_map/ppermute | solution.py:45
  101.5 1.0 collective-permute-start.12
  102.5 0.4 collective-permute-done.6
  102.9 1.4 %collective-permute-start.7 = (f32[64,1024]{1,0:T(8,128)S(1)}, f32[64,1024]{1,0:T(8,128)S(1)}, u32[]{:S(2)}, u32[]{:S(2)}) collective-permute-start(f32[64,1024]{1,0:T(8,128)S(1)} %max.26), channel_id=1, source_target_pairs={{0,96},{1,97},{2,98},{3,99},{4,100},{5,101},{6,102},{7,103},{8,104... | collective-permute-start | bytes 786440 | tf_op jit(solution)/shard_map/ppermute | solution.py:45
  104.3 5.4 %collective-permute-done.12 = f32[64,1024]{1,0:T(8,128)S(1)} collective-permute-done((f32[64,1024]{1,0:T(8,128)S(1)}, f32[64,1024]{1,0:T(8,128)S(1)}, u32[]{:S(2)}, u32[]{:S(2)}) %collective-permute-start.12) | collective-permute-done | bytes 262176 | tf_op jit(solution)/shard_map/ppermute | solution.py:45
  109.8 0.2 collective-permute-start.13
  110.0 1.5 %collective-permute-done.7 = f32[64,1024]{1,0:T(8,128)S(1)} collective-permute-done((f32[64,1024]{1,0:T(8,128)S(1)}, f32[64,1024]{1,0:T(8,128)S(1)}, u32[]{:S(2)}, u32[]{:S(2)}) %collective-permute-start.7) | collective-permute-done | bytes 262176 | tf_op jit(solution)/shard_map/ppermute | solution.py:45
  111.5 0.1 collective-permute-start.8
  111.7 4.5 %collective-permute-done.13 = f32[64,1024]{1,0:T(8,128)S(1)} collective-permute-done((f32[64,1024]{1,0:T(8,128)S(1)}, f32[64,1024]{1,0:T(8,128)S(1)}, u32[]{:S(2)}, u32[]{:S(2)}) %collective-permute-start.13) | collective-permute-done | bytes 262176 | tf_op jit(solution)/shard_map/ppermute | solution.py:45
  116.3 1.7 %collective-permute-done.8 = f32[64,1024]{1,0:T(8,128)S(1)} collective-permute-done((f32[64,1024]{1,0:T(8,128)S(1)}, f32[64,1024]{1,0:T(8,128)S(1)}, u32[]{:S(2)}, u32[]{:S(2)}) %collective-permute-start.8) | collective-permute-done | bytes 262176 | tf_op jit(solution)/shard_map/ppermute | solution.py:45
  118.0 1.1 pad_maximum_fusion
  (11 shorter events, 0.4 us)
Async XLA Ops:
  3.9 24.8 %all-to-all-start = ((f32[16,16,1024]{2,1,0:T(8,128)}), f32[16,16,1024]{2,1,0:T(8,128)S(1)}, u32[]{:S(2)}, u32[]{:S(2)}) async-start(f32[16,16,1024]{2,1,0:T(8,128)} %bitcast.9), calls=%async_computation | async-start | bytes 2097152 | tf_op jit(solution)/shard_map/all_to_all | solution.py:144
  10.9 9.9 %copy-start.2 = (f32[16,65]{1,0:T(8,128)S(1)}, f32[16,65]{1,0:T(8,128)}, u32[]{:S(2)}) copy-start(f32[16,65]{1,0:T(8,128)} %param.11) | copy-start | bytes 12484
  10.9 9.9 %copy-start.3 = (f32[16,65]{1,0:T(8,128)S(1)}, f32[16,65]{1,0:T(8,128)}, u32[]{:S(2)}) copy-start(f32[16,65]{1,0:T(8,128)} %param.10) | copy-start | bytes 12484
  15.2 45.5 %copy-start.1 = (s32[7]{0:T(128)S(1)}, s32[7]{0:T(128)}, u32[]{:S(2)}) copy-start(s32[7]{0:T(128)} %seams.1) | copy-start | bytes 88
  15.2 41.7 %collective-permute-start.2 = (f32[4,96,1024]{2,1,0:T(8,128)}, f32[4,96,1024]{2,1,0:T(8,128)S(1)}, u32[]{:S(2)}, u32[]{:S(2)}) collective-permute-start(f32[4,96,1024]{2,1,0:T(8,128)} %get-tuple-element.17), channel_id=1, source_target_pairs={{0,1},{1,2},{2,3},{3,4},{4,5},{5,6},{6,7},{8,9},{9,10},{10,11},{11... | collective-permute-start | bytes 4718600 | tf_op jit(solution)/shard_map/ppermute | solution.py:360
  17.1 39.7 %collective-permute-start.3 = (f32[4,96,1024]{2,1,0:T(8,128)}, f32[4,96,1024]{2,1,0:T(8,128)}, u32[]{:S(2)}, u32[]{:S(2)}) collective-permute-start(f32[4,96,1024]{2,1,0:T(8,128)} %get-tuple-element.18), channel_id=1, source_target_pairs={{1,0},{2,1},{3,2},{4,3},{5,4},{6,5},{7,6},{9,8},{10,9},{11,10},{12... | collective-permute-start | bytes 4718600 | tf_op jit(solution)/shard_map/ppermute | solution.py:361
  28.6 32.1 %copy-start = (bf16[4,2,2,192,256]{4,3,2,1,0:T(8,128)(2,1)S(1)}, bf16[4,2,2,192,256]{4,3,2,1,0:T(8,128)(2,1)}, u32[]{:S(2)}) copy-start(bf16[4,2,2,192,256]{4,3,2,1,0:T(8,128)(2,1)} %get-tuple-element.19.v_ref) | copy-start | bytes 4718596
  51.3 7.7 %collective-permute-start = (f32[64,1024]{1,0:T(8,128)S(1)}, f32[64,1024]{1,0:T(8,128)S(1)}, u32[]{:S(2)}, u32[]{:S(2)}) collective-permute-start(f32[64,1024]{1,0:T(8,128)S(1)} %bitcast.11), channel_id=1, source_target_pairs={{0,1},{1,2},{2,3},{3,4},{4,5},{5,6},{6,7},{8,9},{9,10},{10,11},{11... | collective-permute-start | bytes 786440 | tf_op jit(solution)/shard_map/ppermute | solution.py:362
  53.2 7.5 %collective-permute-start.1 = (f32[64,1024]{1,0:T(8,128)S(1)}, f32[64,1024]{1,0:T(8,128)S(1)}, u32[]{:S(2)}, u32[]{:S(2)}) collective-permute-start(f32[64,1024]{1,0:T(8,128)S(1)} %bitcast.10), channel_id=1, source_target_pairs={{1,0},{2,1},{3,2},{4,3},{5,4},{6,5},{7,6},{9,8},{10,9},{11,10},{12... | collective-permute-start | bytes 786440 | tf_op jit(solution)/shard_map/ppermute | solution.py:363
  74.9 8.6 %collective-permute-start.9 = (f32[64,1024]{1,0:T(8,128)S(1)}, f32[64,1024]{1,0:T(8,128)S(1)}, u32[]{:S(2)}, u32[]{:S(2)}) collective-permute-start(f32[64,1024]{1,0:T(8,128)S(1)} %get-tuple-element.25), channel_id=1, source_target_pairs={{0,32},{1,33},{2,34},{3,35},{4,36},{5,37},{6,38},{7,39},{8,40},{9,... | collective-permute-start | bytes 786440 | tf_op jit(solution)/shard_map/ppermute | solution.py:45
  74.9 9.4 %collective-permute-start.4 = (f32[64,1024]{1,0:T(8,128)S(1)}, f32[64,1024]{1,0:T(8,128)S(1)}, u32[]{:S(2)}, u32[]{:S(2)}) collective-permute-start(f32[64,1024]{1,0:T(8,128)S(1)} %get-tuple-element.23), channel_id=1, source_target_pairs={{0,8},{1,9},{2,10},{3,11},{4,12},{5,13},{6,14},{7,15},{8,0},{9,1},... | collective-permute-start | bytes 786440 | tf_op jit(solution)/shard_map/ppermute | solution.py:45
  83.5 9.9 %collective-permute-start.10 = (f32[64,1024]{1,0:T(8,128)S(1)}, f32[64,1024]{1,0:T(8,128)S(1)}, u32[]{:S(2)}, u32[]{:S(2)}) collective-permute-start(f32[64,1024]{1,0:T(8,128)S(1)} %max.28), channel_id=1, source_target_pairs={{0,96},{1,97},{2,98},{3,99},{4,100},{5,101},{6,102},{7,103},{8,104... | collective-permute-start | bytes 786440 | tf_op jit(solution)/shard_map/ppermute | solution.py:45
  84.3 10.3 %collective-permute-start.5 = (f32[64,1024]{1,0:T(8,128)S(1)}, f32[64,1024]{1,0:T(8,128)S(1)}, u32[]{:S(2)}, u32[]{:S(2)}) collective-permute-start(f32[64,1024]{1,0:T(8,128)S(1)} %max.24), channel_id=1, source_target_pairs={{0,24},{1,25},{2,26},{3,27},{4,28},{5,29},{6,30},{7,31},{8,16},{9,... | collective-permute-start | bytes 786440 | tf_op jit(solution)/shard_map/ppermute | solution.py:45
  93.5 7.9 %collective-permute-start.11 = (f32[64,1024]{1,0:T(8,128)S(1)}, f32[64,1024]{1,0:T(8,128)S(1)}, u32[]{:S(2)}, u32[]{:S(2)}) collective-permute-start(f32[64,1024]{1,0:T(8,128)S(1)} %max.29), channel_id=1, source_target_pairs={{0,8},{1,9},{2,10},{3,11},{4,12},{5,13},{6,14},{7,15},{8,0},{9,1},... | collective-permute-start | bytes 786440 | tf_op jit(solution)/shard_map/ppermute | solution.py:45
  94.7 8.2 %collective-permute-start.6 = (f32[64,1024]{1,0:T(8,128)S(1)}, f32[64,1024]{1,0:T(8,128)S(1)}, u32[]{:S(2)}, u32[]{:S(2)}) collective-permute-start(f32[64,1024]{1,0:T(8,128)S(1)} %max.25), channel_id=1, source_target_pairs={{0,32},{1,33},{2,34},{3,35},{4,36},{5,37},{6,38},{7,39},{8,40},{9,... | collective-permute-start | bytes 786440 | tf_op jit(solution)/shard_map/ppermute | solution.py:45
  101.5 8.2 %collective-permute-start.12 = (f32[64,1024]{1,0:T(8,128)S(1)}, f32[64,1024]{1,0:T(8,128)S(1)}, u32[]{:S(2)}, u32[]{:S(2)}) collective-permute-start(f32[64,1024]{1,0:T(8,128)S(1)} %max.30), channel_id=1, source_target_pairs={{0,24},{1,25},{2,26},{3,27},{4,28},{5,29},{6,30},{7,31},{8,16},{9,... | collective-permute-start | bytes 786440 | tf_op jit(solution)/shard_map/ppermute | solution.py:45
  102.9 8.6 %collective-permute-start.7 = (f32[64,1024]{1,0:T(8,128)S(1)}, f32[64,1024]{1,0:T(8,128)S(1)}, u32[]{:S(2)}, u32[]{:S(2)}) collective-permute-start(f32[64,1024]{1,0:T(8,128)S(1)} %max.26), channel_id=1, source_target_pairs={{0,96},{1,97},{2,98},{3,99},{4,100},{5,101},{6,102},{7,103},{8,104... | collective-permute-start | bytes 786440 | tf_op jit(solution)/shard_map/ppermute | solution.py:45
  109.8 6.5 %collective-permute-start.13 = (f32[64,1024]{1,0:T(8,128)S(1)}, f32[64,1024]{1,0:T(8,128)S(1)}, u32[]{:S(2)}, u32[]{:S(2)}) collective-permute-start(f32[64,1024]{1,0:T(8,128)S(1)} %max.31), channel_id=1, source_target_pairs={{0,32},{1,33},{2,34},{3,35},{4,36},{5,37},{6,38},{7,39},{8,40},{9,... | collective-permute-start | bytes 786440 | tf_op jit(solution)/shard_map/ppermute | solution.py:45
  111.5 6.5 %collective-permute-start.8 = (f32[64,1024]{1,0:T(8,128)S(1)}, f32[64,1024]{1,0:T(8,128)S(1)}, u32[]{:S(2)}, u32[]{:S(2)}) collective-permute-start(f32[64,1024]{1,0:T(8,128)S(1)} %max.27), channel_id=1, source_target_pairs={{0,8},{1,9},{2,10},{3,11},{4,12},{5,13},{6,14},{7,15},{8,0},{9,1},... | collective-permute-start | bytes 786440 | tf_op jit(solution)/shard_map/ppermute | solution.py:45

commit v4 on v3

--- a/solution.py
+++ b/solution.py
@@ -89,10 +89,15 @@
     )(extinction)
 
 
-def rims_kernel(ext, est, mea, up, down, ext_buf, est_buf, mea_buf, sems):
+def rims_kernel(ext, est, mea, beside, across, ext_buf, est_buf, mea_buf, sems):
     rim = 2 * HALF
     planes, rows, _ = ext.shape
-    ends = ((0, 0, up), (rows - rim, rows - HALF, down))
+    core = lax.axis_index("tile") % 2
+    ends = []
+    for at_far, out in ((core == 0, beside), (core == 1, across)):
+        wide = pl.multiple_of(jnp.where(at_far, rows - rim, 0), HALF)
+        narrow = pl.multiple_of(jnp.where(at_far, rows - HALF, 0), HALF)
+        ends.append((wide, narrow, out))
     copies = []
     for i, (wide, narrow, _) in enumerate(ends):
         for j, (source, buf, at, size) in enumerate(
@@ -242,7 +247,7 @@
 
 
 def step_kernel(
-    seams, ext, est, mea, above, above_top, above_bot, rim_top, rim_bot, v_ref, l_ref,
+    seams, ext, est, mea, above, above_across, above_beside, rim_across, rim_beside, v_ref, l_ref,
     upd, o0, o1, o2, o3, optical, top, wh, wl, mh, ml, qh, ql, nh, nl, corner,
 ):
     plane = pl.program_id(0)
@@ -261,11 +266,18 @@
             ref[:, :128] = edge
             ref[:, ref.shape[1] - 128 :] = edge
 
-    for joined, far, packed, at in (
-        (join_top, above_top, rim_top, 0),
-        (join_bot, above_bot, rim_bot, rows + rim),
-    ):
-        value = jnp.where(joined, jnp.exp(-far[...]) * packed[0, :rim], 0.0)
+    core = tile % 2
+
+    def top_of(across, beside):
+        return jnp.where(core == 0, across, beside)
+
+    def bot_of(across, beside):
+        return jnp.where(core == 0, beside, across)
+
+    for joined, pick, at in ((join_top, top_of, 0), (join_bot, bot_of, rows + rim)):
+        far = pick(above_across[...], above_beside[...])
+        packed = pick(rim_across[0, :rim], rim_beside[0, :rim])
+        value = jnp.where(joined, jnp.exp(-far) * packed, 0.0)
         wh[at : at + rim], wl[at : at + rim] = split(value)
     for r in range(0, rows, 64):
         depth = optical[r : r + 64]
@@ -289,9 +301,11 @@
     for c in range(0, cols, 256):
         s = slice(c, c + 256)
         blurred = lateral(mh, ml, corner, slice(0, rows + rim), c, l_ref.at[0, 0])
-        q0 = jnp.where(join_top, rim_top[0, rim:, s] / blurred[:HALF], 0.0)
+        q0 = top_of(rim_across[0, rim:, s], rim_beside[0, rim:, s]) / blurred[:HALF]
+        q0 = jnp.where(join_top, q0, 0.0)
         q1 = mea[0, :, s] / blurred[HALF : HALF + rows]
-        q2 = jnp.where(join_bot, rim_bot[0, rim:, s] / blurred[HALF + rows :], 0.0)
+        q2 = bot_of(rim_across[0, rim:, s], rim_beside[0, rim:, s]) / blurred[HALF + rows :]
+        q2 = jnp.where(join_bot, q2, 0.0)
         qh[:HALF, s], ql[:HALF, s] = split(q0)
         qh[HALF : HALF + rows, s], ql[HALF : HALF + rows, s] = split(q1)
         qh[HALF + rows :, s], ql[HALF + rows :, s] = split(q2)
@@ -314,7 +328,7 @@
             give[...] = top[rows_at(2 * piece + 1 - kept, quarter)]
 
 
-def step(seams, ext, est, mea, above, above_top, above_bot, rim_top, rim_bot, v, l):
+def step(seams, ext, est, mea, above, above_across, above_beside, rim_across, rim_beside, v, l):
     planes, rows, cols = ext.shape
     rim, quarter = 2 * HALF, rows // 4
     stack = pl.BlockSpec((1, rows, cols), lambda p: (p, 0, 0))
@@ -344,25 +358,30 @@
             pltpu.VMEM((rows, cols + 256), BF),
             pltpu.VMEM((rows + rim, cols), BF),
         ],
-        compiler_params=params(44),
+        compiler_params=params(48),
         cost_estimate=pl.CostEstimate(flops=12 << 30, bytes_accessed=24 << 20, transcendentals=1 << 20),
-    )(seams, ext, est, mea, above, above_top, above_bot, rim_top, rim_bot, v, l)
+    )(seams, ext, est, mea, above, above_across, above_beside, rim_across, rim_beside, v, l)
 
 
 def on_device(measured, estimate, extinction, psf_rows, psf_cols, stratum, seam_flags):
     rows = measured.shape[1]
     rim = 2 * HALF
     tiles = lax.axis_size("tile")
-    onward = [(i, i + 1) for i in range(tiles - 1)]
-    backward = [(i + 1, i) for i in range(tiles - 1)]
+    beside = [(i, i ^ 1) for i in range(tiles)]
+    across = [p for i in range(1, tiles - 1, 2) for p in ((i, i + 1), (i + 1, i))]
+    first_core = lax.axis_index("tile") % 2 == 0
     above, (v, l) = above_of(sums(extinction), bands(psf_rows, psf_cols, stratum))
-    up, down = rims(extinction, estimate, measured)
-    rim_top = lax.ppermute(down, "tile", onward)
-    rim_bot = lax.ppermute(up, "tile", backward)
-    above_top = lax.ppermute(above[rows - rim :], "tile", onward)
-    above_bot = lax.ppermute(above[:rim], "tile", backward)
+    send_beside, send_across = rims(extinction, estimate, measured)
+    rim_across = lax.ppermute(send_across, "tile", across)
+    rim_beside = lax.ppermute(send_beside, "tile", beside)
+
+    def rim_of(at_far):
+        return lax.dynamic_slice_in_dim(above, jnp.where(at_far, rows - rim, 0), rim)
+
+    above_across = lax.ppermute(rim_of(~first_core), "tile", across)
+    above_beside = lax.ppermute(rim_of(first_core), "tile", beside)
     updated, keep_a, give_a, keep_b, give_b = step(
-        seam_flags, extinction, estimate, measured, above, above_top, above_bot, rim_top, rim_bot, v, l
+        seam_flags, extinction, estimate, measured, above, above_across, above_beside, rim_across, rim_beside, v, l
     )
     return updated, highest([(keep_a, give_a), (keep_b, give_b)])
 

time: 120 us -> 116 us (0.967)
  the two profiles are of different devices: /device:TPU:32 before, /device:TPU:0 now
where the time goes in v4:
time: 116 us
  waiting for transfers between devices  57.1 us (49%)
  Pallas kernels  28.1 us (24%)
  starting transfers between devices  27.3 us (24%)
  other arithmetic  2.1 us (2%)
    ppermute x10, waiting for transfers between devices, swap(): lax.ppermute(value, ('depth', 'tile'), pairs(piece, number, lax.axis_size...  34.5 us
    all_to_all x1, waiting for transfers between devices, above_of(): lax.all_to_all(prefixes, 'depth', 0, 0, tiled=True).reshape(rows, cols)  17.7 us
    pallas_call x1, Pallas kernels, step(): pl.pallas_call(step_kernel, grid=(planes,), in_specs=[smem(), stack, stac...  14.8 us
    ppermute x10, starting transfers between devices, swap(): lax.ppermute(value, ('depth', 'tile'), pairs(piece, number, lax.axis_size...  8.51 us
    all_to_all x1, starting transfers between devices, above_of(): parts = lax.all_to_all(parts, 'depth', 0, 0, tiled=True)  7.13 us
    pallas_call x1, Pallas kernels, bands(): pl.pallas_call(bands_kernel, grid_spec=pltpu.PrefetchScalarGridSpec(num_s...  4.83 us
    pallas_call x1, Pallas kernels, rims(): pl.pallas_call(rims_kernel, in_specs=[pl.BlockSpec(memory_space=pl.ANY)]...  4.23 us
    all_to_all x1, waiting for transfers between devices, above_of(): parts = lax.all_to_all(parts, 'depth', 0, 0, tiled=True)  3.73 us
  transfers between devices with their start and end apart: 16, of which 11 were waited for; matrix products, arithmetic and copies ran while one was open for 1% of the time, Pallas kernels for 9%

profile of v4, /device:TPU:0, one launch (start us, length us, event | category | flops | bytes accessed | tf_op | source)
XLA Modules:
  0.0 115.7 jit_solution(14581958427634937383)
XLA Ops:
  0.6 3.2 %shard_map.86 = f32[256,1024]{1,0:T(8,128)} custom-call(f32[4,256,1024]{2,1,0:T(8,128)} %ext.5), custom_call_target="tpu_custom_call" | custom-call | tf_op jit(solution)/shard_map/pallas_call | solution.py:82
  3.9 7.1 %all-to-all-start = ((f32[16,16,1024]{2,1,0:T(8,128)}), f32[16,16,1024]{2,1,0:T(8,128)S(1)}, u32[]{:S(2)}, u32[]{:S(2)}) async-start(f32[16,16,1024]{2,1,0:T(8,128)} %bitcast.8), calls=%async_computation | async-start | bytes 2097152 | tf_op jit(solution)/shard_map/all_to_all | solution.py:149
  11.0 0.0 copy-start.1
  11.0 0.0 copy-start.2
  11.0 4.2 %shard_map.89 = (f32[4,96,1024]{2,1,0:T(8,128)}, f32[4,96,1024]{2,1,0:T(8,128)}) custom-call(f32[4,256,1024]{2,1,0:T(8,128)} %ext.5, f32[4,256,1024]{2,1,0:T(8,128)} %est.3, f32[4,256,1024]{2,1,0:T(8,128)} %mea.3), custom_call_target="tpu_custom_call" | custom-call | flops 1048576 | bytes 8388608 | tf_op jit(solution)/shard_map/pallas_call | solution.py:121
  15.2 0.0 copy-start
  15.3 0.8 collective-permute-start.2
  16.0 3.3 %collective-permute-start.3 = (f32[4,96,1024]{2,1,0:T(8,128)}, f32[4,96,1024]{2,1,0:T(8,128)}, u32[]{:S(2)}, u32[]{:S(2)}) collective-permute-start(f32[4,96,1024]{2,1,0:T(8,128)} %get-tuple-element.18), channel_id=1, source_target_pairs={{0,1},{1,0},{2,3},{3,2},{4,5},{5,4},{6,7},{7,6},{8,9},{9,8},{10,11... | collective-permute-start | bytes 4718600 | tf_op jit(solution)/shard_map/ppermute | solution.py:376
  19.3 0.0 copy-done.1
  19.3 0.1 rev.7
  19.4 0.0 copy-done.2
  19.4 0.1 rev.6
  19.4 0.7 select_maximum_fusion.taps
  20.1 4.8 %shard_map.88 = (bf16[4,2,2,192,256]{4,3,2,1,0:T(8,128)(2,1)}, bf16[4,2,768,256]{3,2,1,0:T(8,128)(2,1)}) custom-call(s32[4]{0:T(128)} %stratum.1, f32[16,4,256]{2,1,0:T(4,128)} %select_maximum_fusion.taps), custom_call_target="tpu_custom_call" | custom-call | flops 4194304 | bytes 6291456 | tf_op jit(solution)/shard_map/pallas_call | solution.py:202
  25.0 3.7 %all-to-all-done.parts = f32[16,16,1024]{2,1,0:T(8,128)S(1)} async-done(((f32[16,16,1024]{2,1,0:T(8,128)}), f32[16,16,1024]{2,1,0:T(8,128)S(1)}, u32[]{:S(2)}, u32[]{:S(2)}) %all-to-all-start) | async-done | bytes 1048608 | tf_op jit(solution)/shard_map/all_to_all | solution.py:149
  28.7 1.0 shard_map.87
  29.7 3.7 %all-to-all-start.1 = ((f32[16,16,1024]{2,1,0:T(8,128)}), f32[16,16,1024]{2,1,0:T(8,128)S(1)}, u32[]{:S(2)}, u32[]{:S(2)}) async-start(f32[16,16,1024]{2,1,0:T(8,128)} %shard_map.87), calls=%async_computation.1 | async-start | bytes 2097152 | tf_op jit(solution)/shard_map/all_to_all | solution.py:158
  33.4 17.7 %all-to-all-done.1 = f32[16,16,1024]{2,1,0:T(8,128)S(1)} async-done(((f32[16,16,1024]{2,1,0:T(8,128)}), f32[16,16,1024]{2,1,0:T(8,128)S(1)}, u32[]{:S(2)}, u32[]{:S(2)}) %all-to-all-start.1) | async-done | bytes 1048608 | tf_op jit(solution)/shard_map/all_to_all | solution.py:158
  51.2 0.7 collective-permute-start
  51.9 3.3 %collective-permute-start.1 = (f32[64,1024]{1,0:T(8,128)S(1)}, f32[64,1024]{1,0:T(8,128)S(1)}, u32[]{:S(2)}, u32[]{:S(2)}) collective-permute-start(f32[64,1024]{1,0:T(8,128)S(1)} %get-tuple-element.26), channel_id=1, source_target_pairs={{0,1},{1,0},{2,3},{3,2},{4,5},{5,4},{6,7},{7,6},{8,9},{9,8},{10,11... | collective-permute-start | bytes 786440 | tf_op jit(solution)/shard_map/ppermute | solution.py:382
  55.2 0.0 collective-permute-done.2.rim_across
  55.2 0.0 collective-permute-done.3.rim_beside
  55.2 0.0 collective-permute-done.above_across
  55.2 1.1 collective-permute-done.1.above_beside
  56.4 0.0 copy-done
  56.4 14.8 %shard_map.90 = (f32[4,256,1024]{2,1,0:T(8,128)}, f32[64,1024]{1,0:T(8,128)S(1)}, f32[64,1024]{1,0:T(8,128)S(1)}, f32[64,1024]{1,0:T(8,128)S(1)}, f32[64,1024]{1,0:T(8,128)S(1)}) custom-call(s32[7]{0:T(128)S(1)} %copy-done, f32[4,256,1024]{2,1,0:T(8,128)} %ext.5, f32[4,256,1024]{2,1,0:T(8,128)} %est.3, f32[4,256,1024]{2,1,0:T(8,128)} %mea.3, ...), custom_call_target="tpu_custom_call" | custom-call | flops 12884901888 | bytes 25165824 | tf_op jit(solution)/shard_map/pallas_call | solution.py:337
  71.2 0.0 collective-permute-start.9
  71.2 0.6 collective-permute-start.4
  71.9 6.6 %collective-permute-done.9 = f32[64,1024]{1,0:T(8,128)S(1)} collective-permute-done((f32[64,1024]{1,0:T(8,128)S(1)}, f32[64,1024]{1,0:T(8,128)S(1)}, u32[]{:S(2)}, u32[]{:S(2)}) %collective-permute-start.9) | collective-permute-done | bytes 262176 | tf_op jit(solution)/shard_map/ppermute | solution.py:45
  78.5 0.7 collective-permute-start.10
  79.2 0.0 collective-permute-done.4
  79.3 0.6 collective-permute-start.5
  79.9 8.4 %collective-permute-done.10 = f32[64,1024]{1,0:T(8,128)S(1)} collective-permute-done((f32[64,1024]{1,0:T(8,128)S(1)}, f32[64,1024]{1,0:T(8,128)S(1)}, u32[]{:S(2)}, u32[]{:S(2)}) %collective-permute-start.10) | collective-permute-done | bytes 262176 | tf_op jit(solution)/shard_map/ppermute | solution.py:45
  88.3 0.7 collective-permute-start.11
  88.9 0.4 collective-permute-done.5
  89.4 1.3 %collective-permute-start.6 = (f32[64,1024]{1,0:T(8,128)S(1)}, f32[64,1024]{1,0:T(8,128)S(1)}, u32[]{:S(2)}, u32[]{:S(2)}) collective-permute-start(f32[64,1024]{1,0:T(8,128)S(1)} %max.25), channel_id=1, source_target_pairs={{0,32},{1,33},{2,34},{3,35},{4,36},{5,37},{6,38},{7,39},{8,40},{9,... | collective-permute-start | bytes 786440 | tf_op jit(solution)/shard_map/ppermute | solution.py:45
  90.7 6.8 %collective-permute-done.11 = f32[64,1024]{1,0:T(8,128)S(1)} collective-permute-done((f32[64,1024]{1,0:T(8,128)S(1)}, f32[64,1024]{1,0:T(8,128)S(1)}, u32[]{:S(2)}, u32[]{:S(2)}) %collective-permute-start.11) | collective-permute-done | bytes 262176 | tf_op jit(solution)/shard_map/ppermute | solution.py:45
  97.5 0.2 collective-permute-start.12
  97.7 0.2 collective-permute-done.6
  97.9 2.7 %collective-permute-start.7 = (f32[64,1024]{1,0:T(8,128)S(1)}, f32[64,1024]{1,0:T(8,128)S(1)}, u32[]{:S(2)}, u32[]{:S(2)}) collective-permute-start(f32[64,1024]{1,0:T(8,128)S(1)} %max.26), channel_id=1, source_target_pairs={{0,96},{1,97},{2,98},{3,99},{4,100},{5,101},{6,102},{7,103},{8,104... | collective-permute-start | bytes 786440 | tf_op jit(solution)/shard_map/ppermute | solution.py:45
  100.6 6.3 %collective-permute-done.12 = f32[64,1024]{1,0:T(8,128)S(1)} collective-permute-done((f32[64,1024]{1,0:T(8,128)S(1)}, f32[64,1024]{1,0:T(8,128)S(1)}, u32[]{:S(2)}, u32[]{:S(2)}) %collective-permute-start.12) | collective-permute-done | bytes 262176 | tf_op jit(solution)/shard_map/ppermute | solution.py:45
  107.0 0.1 collective-permute-start.13
  107.1 0.0 collective-permute-done.7
  107.1 1.6 %collective-permute-start.8 = (f32[64,1024]{1,0:T(8,128)S(1)}, f32[64,1024]{1,0:T(8,128)S(1)}, u32[]{:S(2)}, u32[]{:S(2)}) collective-permute-start(f32[64,1024]{1,0:T(8,128)S(1)} %max.27), channel_id=1, source_target_pairs={{0,8},{1,9},{2,10},{3,11},{4,12},{5,13},{6,14},{7,15},{8,0},{9,1},... | collective-permute-start | bytes 786440 | tf_op jit(solution)/shard_map/ppermute | solution.py:45
  108.7 5.7 %collective-permute-done.13 = f32[64,1024]{1,0:T(8,128)S(1)} collective-permute-done((f32[64,1024]{1,0:T(8,128)S(1)}, f32[64,1024]{1,0:T(8,128)S(1)}, u32[]{:S(2)}, u32[]{:S(2)}) %collective-permute-start.13) | collective-permute-done | bytes 262176 | tf_op jit(solution)/shard_map/ppermute | solution.py:45
  114.4 0.1 collective-permute-done.8
  114.6 1.1 pad_maximum_fusion
  (11 shorter events, 0.4 us)
Async XLA Ops:
  3.9 24.8 %all-to-all-start = ((f32[16,16,1024]{2,1,0:T(8,128)}), f32[16,16,1024]{2,1,0:T(8,128)S(1)}, u32[]{:S(2)}, u32[]{:S(2)}) async-start(f32[16,16,1024]{2,1,0:T(8,128)} %bitcast.8), calls=%async_computation | async-start | bytes 2097152 | tf_op jit(solution)/shard_map/all_to_all | solution.py:149
  11.0 8.3 %copy-start.1 = (f32[16,65]{1,0:T(8,128)S(1)}, f32[16,65]{1,0:T(8,128)}, u32[]{:S(2)}) copy-start(f32[16,65]{1,0:T(8,128)} %param.11) | copy-start | bytes 12484
  11.0 8.4 %copy-start.2 = (f32[16,65]{1,0:T(8,128)S(1)}, f32[16,65]{1,0:T(8,128)}, u32[]{:S(2)}) copy-start(f32[16,65]{1,0:T(8,128)} %param.10) | copy-start | bytes 12484
  15.2 41.1 %copy-start = (s32[7]{0:T(128)S(1)}, s32[7]{0:T(128)}, u32[]{:S(2)}) copy-start(s32[7]{0:T(128)} %seams.1) | copy-start | bytes 88
  15.3 40.0 %collective-permute-start.2 = (f32[4,96,1024]{2,1,0:T(8,128)}, f32[4,96,1024]{2,1,0:T(8,128)S(1)}, u32[]{:S(2)}, u32[]{:S(2)}) collective-permute-start(f32[4,96,1024]{2,1,0:T(8,128)} %get-tuple-element.17), channel_id=1, source_target_pairs={{1,2},{2,1},{3,4},{4,3},{5,6},{6,5},{9,10},{10,9},{11,12},{12,11},... | collective-permute-start | bytes 4718600 | tf_op jit(solution)/shard_map/ppermute | solution.py:375
  16.0 39.2 %collective-permute-start.3 = (f32[4,96,1024]{2,1,0:T(8,128)}, f32[4,96,1024]{2,1,0:T(8,128)}, u32[]{:S(2)}, u32[]{:S(2)}) collective-permute-start(f32[4,96,1024]{2,1,0:T(8,128)} %get-tuple-element.18), channel_id=1, source_target_pairs={{0,1},{1,0},{2,3},{3,2},{4,5},{5,4},{6,7},{7,6},{8,9},{9,8},{10,11... | collective-permute-start | bytes 4718600 | tf_op jit(solution)/shard_map/ppermute | solution.py:376
  29.7 21.4 %all-to-all-start.1 = ((f32[16,16,1024]{2,1,0:T(8,128)}), f32[16,16,1024]{2,1,0:T(8,128)S(1)}, u32[]{:S(2)}, u32[]{:S(2)}) async-start(f32[16,16,1024]{2,1,0:T(8,128)} %shard_map.87), calls=%async_computation.1 | async-start | bytes 2097152 | tf_op jit(solution)/shard_map/all_to_all | solution.py:158
  51.2 4.0 %collective-permute-start = (f32[64,1024]{1,0:T(8,128)S(1)}, f32[64,1024]{1,0:T(8,128)S(1)}, u32[]{:S(2)}, u32[]{:S(2)}) collective-permute-start(f32[64,1024]{1,0:T(8,128)S(1)} %get-tuple-element.27), channel_id=1, source_target_pairs={{1,2},{2,1},{3,4},{4,3},{5,6},{6,5},{9,10},{10,9},{11,12},{12,11},... | collective-permute-start | bytes 786440 | tf_op jit(solution)/shard_map/ppermute | solution.py:381
  51.9 4.5 %collective-permute-start.1 = (f32[64,1024]{1,0:T(8,128)S(1)}, f32[64,1024]{1,0:T(8,128)S(1)}, u32[]{:S(2)}, u32[]{:S(2)}) collective-permute-start(f32[64,1024]{1,0:T(8,128)S(1)} %get-tuple-element.26), channel_id=1, source_target_pairs={{0,1},{1,0},{2,3},{3,2},{4,5},{5,4},{6,7},{7,6},{8,9},{9,8},{10,11... | collective-permute-start | bytes 786440 | tf_op jit(solution)/shard_map/ppermute | solution.py:382
  71.2 7.3 %collective-permute-start.9 = (f32[64,1024]{1,0:T(8,128)S(1)}, f32[64,1024]{1,0:T(8,128)S(1)}, u32[]{:S(2)}, u32[]{:S(2)}) collective-permute-start(f32[64,1024]{1,0:T(8,128)S(1)} %get-tuple-element.25), channel_id=1, source_target_pairs={{0,32},{1,33},{2,34},{3,35},{4,36},{5,37},{6,38},{7,39},{8,40},{9,... | collective-permute-start | bytes 786440 | tf_op jit(solution)/shard_map/ppermute | solution.py:45
  71.2 8.0 %collective-permute-start.4 = (f32[64,1024]{1,0:T(8,128)S(1)}, f32[64,1024]{1,0:T(8,128)S(1)}, u32[]{:S(2)}, u32[]{:S(2)}) collective-permute-start(f32[64,1024]{1,0:T(8,128)S(1)} %get-tuple-element.23), channel_id=1, source_target_pairs={{0,8},{1,9},{2,10},{3,11},{4,12},{5,13},{6,14},{7,15},{8,0},{9,1},... | collective-permute-start | bytes 786440 | tf_op jit(solution)/shard_map/ppermute | solution.py:45
  78.5 9.7 %collective-permute-start.10 = (f32[64,1024]{1,0:T(8,128)S(1)}, f32[64,1024]{1,0:T(8,128)S(1)}, u32[]{:S(2)}, u32[]{:S(2)}) collective-permute-start(f32[64,1024]{1,0:T(8,128)S(1)} %max.28), channel_id=1, source_target_pairs={{0,96},{1,97},{2,98},{3,99},{4,100},{5,101},{6,102},{7,103},{8,104... | collective-permute-start | bytes 786440 | tf_op jit(solution)/shard_map/ppermute | solution.py:45
  79.3 10.1 %collective-permute-start.5 = (f32[64,1024]{1,0:T(8,128)S(1)}, f32[64,1024]{1,0:T(8,128)S(1)}, u32[]{:S(2)}, u32[]{:S(2)}) collective-permute-start(f32[64,1024]{1,0:T(8,128)S(1)} %max.24), channel_id=1, source_target_pairs={{0,24},{1,25},{2,26},{3,27},{4,28},{5,29},{6,30},{7,31},{8,16},{9,... | collective-permute-start | bytes 786440 | tf_op jit(solution)/shard_map/ppermute | solution.py:45
  88.3 9.1 %collective-permute-start.11 = (f32[64,1024]{1,0:T(8,128)S(1)}, f32[64,1024]{1,0:T(8,128)S(1)}, u32[]{:S(2)}, u32[]{:S(2)}) collective-permute-start(f32[64,1024]{1,0:T(8,128)S(1)} %max.29), channel_id=1, source_target_pairs={{0,8},{1,9},{2,10},{3,11},{4,12},{5,13},{6,14},{7,15},{8,0},{9,1},... | collective-permute-start | bytes 786440 | tf_op jit(solution)/shard_map/ppermute | solution.py:45
  89.4 8.5 %collective-permute-start.6 = (f32[64,1024]{1,0:T(8,128)S(1)}, f32[64,1024]{1,0:T(8,128)S(1)}, u32[]{:S(2)}, u32[]{:S(2)}) collective-permute-start(f32[64,1024]{1,0:T(8,128)S(1)} %max.25), channel_id=1, source_target_pairs={{0,32},{1,33},{2,34},{3,35},{4,36},{5,37},{6,38},{7,39},{8,40},{9,... | collective-permute-start | bytes 786440 | tf_op jit(solution)/shard_map/ppermute | solution.py:45
  97.5 9.5 %collective-permute-start.12 = (f32[64,1024]{1,0:T(8,128)S(1)}, f32[64,1024]{1,0:T(8,128)S(1)}, u32[]{:S(2)}, u32[]{:S(2)}) collective-permute-start(f32[64,1024]{1,0:T(8,128)S(1)} %max.30), channel_id=1, source_target_pairs={{0,24},{1,25},{2,26},{3,27},{4,28},{5,29},{6,30},{7,31},{8,16},{9,... | collective-permute-start | bytes 786440 | tf_op jit(solution)/shard_map/ppermute | solution.py:45
  97.9 9.2 %collective-permute-start.7 = (f32[64,1024]{1,0:T(8,128)S(1)}, f32[64,1024]{1,0:T(8,128)S(1)}, u32[]{:S(2)}, u32[]{:S(2)}) collective-permute-start(f32[64,1024]{1,0:T(8,128)S(1)} %max.26), channel_id=1, source_target_pairs={{0,96},{1,97},{2,98},{3,99},{4,100},{5,101},{6,102},{7,103},{8,104... | collective-permute-start | bytes 786440 | tf_op jit(solution)/shard_map/ppermute | solution.py:45
  107.0 7.4 %collective-permute-start.13 = (f32[64,1024]{1,0:T(8,128)S(1)}, f32[64,1024]{1,0:T(8,128)S(1)}, u32[]{:S(2)}, u32[]{:S(2)}) collective-permute-start(f32[64,1024]{1,0:T(8,128)S(1)} %max.31), channel_id=1, source_target_pairs={{0,32},{1,33},{2,34},{3,35},{4,36},{5,37},{6,38},{7,39},{8,40},{9,... | collective-permute-start | bytes 786440 | tf_op jit(solution)/shard_map/ppermute | solution.py:45
  107.1 7.4 %collective-permute-start.8 = (f32[64,1024]{1,0:T(8,128)S(1)}, f32[64,1024]{1,0:T(8,128)S(1)}, u32[]{:S(2)}, u32[]{:S(2)}) collective-permute-start(f32[64,1024]{1,0:T(8,128)S(1)} %max.27), channel_id=1, source_target_pairs={{0,8},{1,9},{2,10},{3,11},{4,12},{5,13},{6,14},{7,15},{8,0},{9,1},... | collective-permute-start | bytes 786440 | tf_op jit(solution)/shard_map/ppermute | solution.py:45

commit v5 on v4

--- a/solution.py
+++ b/solution.py
@@ -142,11 +142,13 @@
         running = running + value
 
 
-def above_of(total, meanwhile):
+def above_of(total, meanwhile, args):
     rows, cols = total.shape
     slabs = lax.axis_size("depth")
     parts = total.reshape(slabs, rows // slabs, cols)
     parts = lax.all_to_all(parts, "depth", 0, 0, tiled=True)
+    parts, args = lax.optimization_barrier((parts, args))
+    made = meanwhile(*args)
     prefixes = pl.pallas_call(
         scan_kernel,
         in_specs=[whole()],
@@ -154,8 +156,8 @@
         out_shape=jax.ShapeDtypeStruct(parts.shape, F32),
         compiler_params=params(16),
     )(parts)
-    prefixes, meanwhile = lax.optimization_barrier((prefixes, meanwhile))
-    return lax.all_to_all(prefixes, "depth", 0, 0, tiled=True).reshape(rows, cols), meanwhile
+    above = lax.all_to_all(prefixes, "depth", 0, 0, tiled=True).reshape(rows, cols)
+    return lax.optimization_barrier((above, made))
 
 
 def highest(parts):
@@ -370,7 +372,7 @@
     beside = [(i, i ^ 1) for i in range(tiles)]
     across = [p for i in range(1, tiles - 1, 2) for p in ((i, i + 1), (i + 1, i))]
     first_core = lax.axis_index("tile") % 2 == 0
-    above, (v, l) = above_of(sums(extinction), bands(psf_rows, psf_cols, stratum))
+    above, (v, l) = above_of(sums(extinction), bands, (psf_rows, psf_cols, stratum))
     send_beside, send_across = rims(extinction, estimate, measured)
     rim_across = lax.ppermute(send_across, "tile", across)
     rim_beside = lax.ppermute(send_beside, "tile", beside)

time: 116 us -> 114 us (0.983)
  waiting for transfers between devices: 57.1 us -> 55.3 us
    all_to_all x1, waiting for transfers between devices: 17.7 us -> 9.55 us  [above_of(): lax.all_to_all(prefixes, 'depth', 0, 0, tiled=True).reshape(rows, cols)]
    all_to_all x1, waiting for transfers between devices: 3.73 us -> 9.27 us  [above_of(): parts = lax.all_to_all(parts, 'depth', 0, 0, tiled=True)]
where the time goes in v5:
time: 114 us
  waiting for transfers between devices  55.3 us (49%)
  Pallas kernels  28.1 us (25%)
  starting transfers between devices  27 us (24%)
  other arithmetic  2.1 us (2%)
    ppermute x10, waiting for transfers between devices, swap(): lax.ppermute(value, ('depth', 'tile'), pairs(piece, number, lax.axis_size...  35.3 us
    pallas_call x1, Pallas kernels, step(): pl.pallas_call(step_kernel, grid=(planes,), in_specs=[smem(), stack, stac...  14.8 us
    all_to_all x1, waiting for transfers between devices, above_of(): lax.all_to_all(prefixes, 'depth', 0, 0, tiled=True).reshape(rows, cols)  9.55 us
    all_to_all x1, waiting for transfers between devices, above_of(): parts = lax.all_to_all(parts, 'depth', 0, 0, tiled=True)  9.27 us
    ppermute x10, starting transfers between devices, swap(): lax.ppermute(value, ('depth', 'tile'), pairs(piece, number, lax.axis_size...  8.04 us
    all_to_all x1, starting transfers between devices, above_of(): parts = lax.all_to_all(parts, 'depth', 0, 0, tiled=True)  7.13 us
    pallas_call x1, Pallas kernels, bands(): pl.pallas_call(bands_kernel, grid_spec=pltpu.PrefetchScalarGridSpec(num_s...  4.82 us
    pallas_call x1, Pallas kernels, rims(): pl.pallas_call(rims_kernel, in_specs=[pl.BlockSpec(memory_space=pl.ANY)]...  4.23 us
  transfers between devices with their start and end apart: 16, of which 11 were waited for; matrix products, arithmetic and copies ran while one was open for 1% of the time, Pallas kernels for 9%

profile of v5, /device:TPU:0, one launch (start us, length us, event | category | flops | bytes accessed | tf_op | source)
XLA Modules:
  0.0 113.5 jit_solution(15773409897235895780)
XLA Ops:
  0.6 3.2 %shard_map.86 = f32[256,1024]{1,0:T(8,128)} custom-call(f32[4,256,1024]{2,1,0:T(8,128)} %ext.5), custom_call_target="tpu_custom_call" | custom-call | tf_op jit(solution)/shard_map/pallas_call | solution.py:82
  3.9 7.1 %all-to-all-start = ((f32[16,16,1024]{2,1,0:T(8,128)}), f32[16,16,1024]{2,1,0:T(8,128)S(1)}, u32[]{:S(2)}, u32[]{:S(2)}) async-start(f32[16,16,1024]{2,1,0:T(8,128)} %bitcast.8), calls=%async_computation | async-start | bytes 2097152 | tf_op jit(solution)/shard_map/all_to_all | solution.py:149
  11.0 4.2 %shard_map.89 = (f32[4,96,1024]{2,1,0:T(8,128)}, f32[4,96,1024]{2,1,0:T(8,128)}) custom-call(f32[4,256,1024]{2,1,0:T(8,128)} %ext.5, f32[4,256,1024]{2,1,0:T(8,128)} %est.3, f32[4,256,1024]{2,1,0:T(8,128)} %mea.3), custom_call_target="tpu_custom_call" | custom-call | flops 1048576 | bytes 8388608 | tf_op jit(solution)/shard_map/pallas_call | solution.py:121
  15.2 0.0 copy-start.1
  15.2 0.0 copy-start.2
  15.2 0.0 copy-start
  15.3 0.9 collective-permute-start.2
  16.2 3.3 %collective-permute-start.3 = (f32[4,96,1024]{2,1,0:T(8,128)}, f32[4,96,1024]{2,1,0:T(8,128)}, u32[]{:S(2)}, u32[]{:S(2)}) collective-permute-start(f32[4,96,1024]{2,1,0:T(8,128)} %get-tuple-element.26), channel_id=1, source_target_pairs={{0,1},{1,0},{2,3},{3,2},{4,5},{5,4},{6,7},{7,6},{8,9},{9,8},{10,11... | collective-permute-start | bytes 4718600 | tf_op jit(solution)/shard_map/ppermute | solution.py:378
  19.4 9.3 %all-to-all-done.parts = f32[16,16,1024]{2,1,0:T(8,128)S(1)} async-done(((f32[16,16,1024]{2,1,0:T(8,128)}), f32[16,16,1024]{2,1,0:T(8,128)S(1)}, u32[]{:S(2)}, u32[]{:S(2)}) %all-to-all-start) | async-done | bytes 1048608 | tf_op jit(solution)/shard_map/all_to_all | solution.py:149
  28.7 1.0 shard_map.87
  29.7 3.7 %all-to-all-start.1 = ((f32[16,16,1024]{2,1,0:T(8,128)}), f32[16,16,1024]{2,1,0:T(8,128)S(1)}, u32[]{:S(2)}, u32[]{:S(2)}) async-start(f32[16,16,1024]{2,1,0:T(8,128)} %shard_map.87), calls=%async_computation.1 | async-start | bytes 2097152 | tf_op jit(solution)/shard_map/all_to_all | solution.py:159
  33.4 0.0 copy-done.1
  33.4 0.1 rev.7
  33.5 0.0 copy-done.2
  33.5 0.1 rev.6
  33.6 0.7 select_maximum_fusion.taps
  34.3 4.8 %shard_map.88 = (bf16[4,2,2,192,256]{4,3,2,1,0:T(8,128)(2,1)}, bf16[4,2,768,256]{3,2,1,0:T(8,128)(2,1)}) custom-call(s32[4]{0:T(128)} %stratum, f32[16,4,256]{2,1,0:T(4,128)} %select_maximum_fusion.taps), custom_call_target="tpu_custom_call" | custom-call | flops 4194304 | bytes 6291456 | tf_op jit(solution)/shard_map/pallas_call | solution.py:204
  39.1 9.5 %all-to-all-done.1 = f32[16,16,1024]{2,1,0:T(8,128)S(1)} async-done(((f32[16,16,1024]{2,1,0:T(8,128)}), f32[16,16,1024]{2,1,0:T(8,128)S(1)}, u32[]{:S(2)}, u32[]{:S(2)}) %all-to-all-start.1) | async-done | bytes 1048608 | tf_op jit(solution)/shard_map/all_to_all | solution.py:159
  48.7 0.7 collective-permute-start
  49.3 3.3 %collective-permute-start.1 = (f32[64,1024]{1,0:T(8,128)S(1)}, f32[64,1024]{1,0:T(8,128)S(1)}, u32[]{:S(2)}, u32[]{:S(2)}) collective-permute-start(f32[64,1024]{1,0:T(8,128)S(1)} %get-tuple-element.34), channel_id=1, source_target_pairs={{0,1},{1,0},{2,3},{3,2},{4,5},{5,4},{6,7},{7,6},{8,9},{9,8},{10,11... | collective-permute-start | bytes 786440 | tf_op jit(solution)/shard_map/ppermute | solution.py:384
  52.7 0.0 collective-permute-done.2.rim_across
  52.7 0.0 collective-permute-done.3.rim_beside
  52.7 0.0 collective-permute-done.above_across
  52.7 1.1 %collective-permute-done.1.above_beside = f32[64,1024]{1,0:T(8,128)S(1)} collective-permute-done((f32[64,1024]{1,0:T(8,128)S(1)}, f32[64,1024]{1,0:T(8,128)S(1)}, u32[]{:S(2)}, u32[]{:S(2)}) %collective-permute-start.1) | collective-permute-done | bytes 262176 | tf_op jit(solution)/shard_map/ppermute | solution.py:384
  53.9 0.0 copy-done
  53.9 14.8 %shard_map.90 = (f32[4,256,1024]{2,1,0:T(8,128)}, f32[64,1024]{1,0:T(8,128)S(1)}, f32[64,1024]{1,0:T(8,128)S(1)}, f32[64,1024]{1,0:T(8,128)S(1)}, f32[64,1024]{1,0:T(8,128)S(1)}) custom-call(s32[7]{0:T(128)S(1)} %copy-done, f32[4,256,1024]{2,1,0:T(8,128)} %ext.5, f32[4,256,1024]{2,1,0:T(8,128)} %est.3, f32[4,256,1024]{2,1,0:T(8,128)} %mea.3, ...), custom_call_target="tpu_custom_call" | custom-call | flops 12884901888 | bytes 25165824 | tf_op jit(solution)/shard_map/pallas_call | solution.py:339
  68.7 0.0 collective-permute-start.9
  68.7 0.6 collective-permute-start.4
  69.3 6.6 %collective-permute-done.9 = f32[64,1024]{1,0:T(8,128)S(1)} collective-permute-done((f32[64,1024]{1,0:T(8,128)S(1)}, f32[64,1024]{1,0:T(8,128)S(1)}, u32[]{:S(2)}, u32[]{:S(2)}) %collective-permute-start.9) | collective-permute-done | bytes 262176 | tf_op jit(solution)/shard_map/ppermute | solution.py:45
  76.0 1.3 %collective-permute-start.10 = (f32[64,1024]{1,0:T(8,128)S(1)}, f32[64,1024]{1,0:T(8,128)S(1)}, u32[]{:S(2)}, u32[]{:S(2)}) collective-permute-start(f32[64,1024]{1,0:T(8,128)S(1)} %max.28), channel_id=1, source_target_pairs={{0,96},{1,97},{2,98},{3,99},{4,100},{5,101},{6,102},{7,103},{8,104... | collective-permute-start | bytes 786440 | tf_op jit(solution)/shard_map/ppermute | solution.py:45
  77.3 0.0 collective-permute-done.4
  77.4 0.7 collective-permute-start.5
  78.0 7.7 %collective-permute-done.10 = f32[64,1024]{1,0:T(8,128)S(1)} collective-permute-done((f32[64,1024]{1,0:T(8,128)S(1)}, f32[64,1024]{1,0:T(8,128)S(1)}, u32[]{:S(2)}, u32[]{:S(2)}) %collective-permute-start.10) | collective-permute-done | bytes 262176 | tf_op jit(solution)/shard_map/ppermute | solution.py:45
  85.8 0.6 collective-permute-start.11
  86.4 1.0 collective-permute-done.5
  87.5 0.7 collective-permute-start.6
  88.2 6.7 %collective-permute-done.11 = f32[64,1024]{1,0:T(8,128)S(1)} collective-permute-done((f32[64,1024]{1,0:T(8,128)S(1)}, f32[64,1024]{1,0:T(8,128)S(1)}, u32[]{:S(2)}, u32[]{:S(2)}) %collective-permute-start.11) | collective-permute-done | bytes 262176 | tf_op jit(solution)/shard_map/ppermute | solution.py:45
  94.9 1.1 collective-permute-start.12
  96.0 0.0 collective-permute-done.6
  96.1 2.0 %collective-permute-start.7 = (f32[64,1024]{1,0:T(8,128)S(1)}, f32[64,1024]{1,0:T(8,128)S(1)}, u32[]{:S(2)}, u32[]{:S(2)}) collective-permute-start(f32[64,1024]{1,0:T(8,128)S(1)} %max.26), channel_id=1, source_target_pairs={{0,96},{1,97},{2,98},{3,99},{4,100},{5,101},{6,102},{7,103},{8,104... | collective-permute-start | bytes 786440 | tf_op jit(solution)/shard_map/ppermute | solution.py:45
  98.1 6.3 %collective-permute-done.12 = f32[64,1024]{1,0:T(8,128)S(1)} collective-permute-done((f32[64,1024]{1,0:T(8,128)S(1)}, f32[64,1024]{1,0:T(8,128)S(1)}, u32[]{:S(2)}, u32[]{:S(2)}) %collective-permute-start.12) | collective-permute-done | bytes 262176 | tf_op jit(solution)/shard_map/ppermute | solution.py:45
  104.5 0.1 collective-permute-start.13
  104.5 0.7 collective-permute-done.7
  105.3 0.9 collective-permute-start.8
  106.2 5.7 %collective-permute-done.13 = f32[64,1024]{1,0:T(8,128)S(1)} collective-permute-done((f32[64,1024]{1,0:T(8,128)S(1)}, f32[64,1024]{1,0:T(8,128)S(1)}, u32[]{:S(2)}, u32[]{:S(2)}) %collective-permute-start.13) | collective-permute-done | bytes 262176 | tf_op jit(solution)/shard_map/ppermute | solution.py:45
  111.9 0.5 collective-permute-done.8
  112.5 1.1 pad_maximum_fusion
  (11 shorter events, 0.4 us)
Async XLA Ops:
  3.9 24.8 %all-to-all-start = ((f32[16,16,1024]{2,1,0:T(8,128)}), f32[16,16,1024]{2,1,0:T(8,128)S(1)}, u32[]{:S(2)}, u32[]{:S(2)}) async-start(f32[16,16,1024]{2,1,0:T(8,128)} %bitcast.8), calls=%async_computation | async-start | bytes 2097152 | tf_op jit(solution)/shard_map/all_to_all | solution.py:149
  15.2 18.2 %copy-start.1 = (f32[16,65]{1,0:T(8,128)S(1)}, f32[16,65]{1,0:T(8,128)}, u32[]{:S(2)}) copy-start(f32[16,65]{1,0:T(8,128)} %param.11) | copy-start | bytes 12484
  15.2 18.3 %copy-start.2 = (f32[16,65]{1,0:T(8,128)S(1)}, f32[16,65]{1,0:T(8,128)}, u32[]{:S(2)}) copy-start(f32[16,65]{1,0:T(8,128)} %param.10) | copy-start | bytes 12484
  15.2 38.6 %copy-start = (s32[7]{0:T(128)S(1)}, s32[7]{0:T(128)}, u32[]{:S(2)}) copy-start(s32[7]{0:T(128)} %seams.1) | copy-start | bytes 88
  15.3 37.4 %collective-permute-start.2 = (f32[4,96,1024]{2,1,0:T(8,128)}, f32[4,96,1024]{2,1,0:T(8,128)S(1)}, u32[]{:S(2)}, u32[]{:S(2)}) collective-permute-start(f32[4,96,1024]{2,1,0:T(8,128)} %get-tuple-element.25), channel_id=1, source_target_pairs={{1,2},{2,1},{3,4},{4,3},{5,6},{6,5},{9,10},{10,9},{11,12},{12,11},... | collective-permute-start | bytes 4718600 | tf_op jit(solution)/shard_map/ppermute | solution.py:377
  16.2 36.5 %collective-permute-start.3 = (f32[4,96,1024]{2,1,0:T(8,128)}, f32[4,96,1024]{2,1,0:T(8,128)}, u32[]{:S(2)}, u32[]{:S(2)}) collective-permute-start(f32[4,96,1024]{2,1,0:T(8,128)} %get-tuple-element.26), channel_id=1, source_target_pairs={{0,1},{1,0},{2,3},{3,2},{4,5},{5,4},{6,7},{7,6},{8,9},{9,8},{10,11... | collective-permute-start | bytes 4718600 | tf_op jit(solution)/shard_map/ppermute | solution.py:378
  29.7 18.9 %all-to-all-start.1 = ((f32[16,16,1024]{2,1,0:T(8,128)}), f32[16,16,1024]{2,1,0:T(8,128)S(1)}, u32[]{:S(2)}, u32[]{:S(2)}) async-start(f32[16,16,1024]{2,1,0:T(8,128)} %shard_map.87), calls=%async_computation.1 | async-start | bytes 2097152 | tf_op jit(solution)/shard_map/all_to_all | solution.py:159
  48.7 4.0 %collective-permute-start = (f32[64,1024]{1,0:T(8,128)S(1)}, f32[64,1024]{1,0:T(8,128)S(1)}, u32[]{:S(2)}, u32[]{:S(2)}) collective-permute-start(f32[64,1024]{1,0:T(8,128)S(1)} %get-tuple-element.35), channel_id=1, source_target_pairs={{1,2},{2,1},{3,4},{4,3},{5,6},{6,5},{9,10},{10,9},{11,12},{12,11},... | collective-permute-start | bytes 786440 | tf_op jit(solution)/shard_map/ppermute | solution.py:383
  49.3 4.5 %collective-permute-start.1 = (f32[64,1024]{1,0:T(8,128)S(1)}, f32[64,1024]{1,0:T(8,128)S(1)}, u32[]{:S(2)}, u32[]{:S(2)}) collective-permute-start(f32[64,1024]{1,0:T(8,128)S(1)} %get-tuple-element.34), channel_id=1, source_target_pairs={{0,1},{1,0},{2,3},{3,2},{4,5},{5,4},{6,7},{7,6},{8,9},{9,8},{10,11... | collective-permute-start | bytes 786440 | tf_op jit(solution)/shard_map/ppermute | solution.py:384
  68.7 7.3 %collective-permute-start.9 = (f32[64,1024]{1,0:T(8,128)S(1)}, f32[64,1024]{1,0:T(8,128)S(1)}, u32[]{:S(2)}, u32[]{:S(2)}) collective-permute-start(f32[64,1024]{1,0:T(8,128)S(1)} %get-tuple-element.33), channel_id=1, source_target_pairs={{0,32},{1,33},{2,34},{3,35},{4,36},{5,37},{6,38},{7,39},{8,40},{9,... | collective-permute-start | bytes 786440 | tf_op jit(solution)/shard_map/ppermute | solution.py:45
  68.7 8.6 %collective-permute-start.4 = (f32[64,1024]{1,0:T(8,128)S(1)}, f32[64,1024]{1,0:T(8,128)S(1)}, u32[]{:S(2)}, u32[]{:S(2)}) collective-permute-start(f32[64,1024]{1,0:T(8,128)S(1)} %get-tuple-element.31), channel_id=1, source_target_pairs={{0,8},{1,9},{2,10},{3,11},{4,12},{5,13},{6,14},{7,15},{8,0},{9,1},... | collective-permute-start | bytes 786440 | tf_op jit(solution)/shard_map/ppermute | solution.py:45
  76.0 9.8 %collective-permute-start.10 = (f32[64,1024]{1,0:T(8,128)S(1)}, f32[64,1024]{1,0:T(8,128)S(1)}, u32[]{:S(2)}, u32[]{:S(2)}) collective-permute-start(f32[64,1024]{1,0:T(8,128)S(1)} %max.28), channel_id=1, source_target_pairs={{0,96},{1,97},{2,98},{3,99},{4,100},{5,101},{6,102},{7,103},{8,104... | collective-permute-start | bytes 786440 | tf_op jit(solution)/shard_map/ppermute | solution.py:45
  77.4 10.1 %collective-permute-start.5 = (f32[64,1024]{1,0:T(8,128)S(1)}, f32[64,1024]{1,0:T(8,128)S(1)}, u32[]{:S(2)}, u32[]{:S(2)}) collective-permute-start(f32[64,1024]{1,0:T(8,128)S(1)} %max.24), channel_id=1, source_target_pairs={{0,24},{1,25},{2,26},{3,27},{4,28},{5,29},{6,30},{7,31},{8,16},{9,... | collective-permute-start | bytes 786440 | tf_op jit(solution)/shard_map/ppermute | solution.py:45
  85.8 9.1 %collective-permute-start.11 = (f32[64,1024]{1,0:T(8,128)S(1)}, f32[64,1024]{1,0:T(8,128)S(1)}, u32[]{:S(2)}, u32[]{:S(2)}) collective-permute-start(f32[64,1024]{1,0:T(8,128)S(1)} %max.29), channel_id=1, source_target_pairs={{0,8},{1,9},{2,10},{3,11},{4,12},{5,13},{6,14},{7,15},{8,0},{9,1},... | collective-permute-start | bytes 786440 | tf_op jit(solution)/shard_map/ppermute | solution.py:45
  87.5 8.6 %collective-permute-start.6 = (f32[64,1024]{1,0:T(8,128)S(1)}, f32[64,1024]{1,0:T(8,128)S(1)}, u32[]{:S(2)}, u32[]{:S(2)}) collective-permute-start(f32[64,1024]{1,0:T(8,128)S(1)} %max.25), channel_id=1, source_target_pairs={{0,32},{1,33},{2,34},{3,35},{4,36},{5,37},{6,38},{7,39},{8,40},{9,... | collective-permute-start | bytes 786440 | tf_op jit(solution)/shard_map/ppermute | solution.py:45
  94.9 9.5 %collective-permute-start.12 = (f32[64,1024]{1,0:T(8,128)S(1)}, f32[64,1024]{1,0:T(8,128)S(1)}, u32[]{:S(2)}, u32[]{:S(2)}) collective-permute-start(f32[64,1024]{1,0:T(8,128)S(1)} %max.30), channel_id=1, source_target_pairs={{0,24},{1,25},{2,26},{3,27},{4,28},{5,29},{6,30},{7,31},{8,16},{9,... | collective-permute-start | bytes 786440 | tf_op jit(solution)/shard_map/ppermute | solution.py:45
  96.1 9.2 %collective-permute-start.7 = (f32[64,1024]{1,0:T(8,128)S(1)}, f32[64,1024]{1,0:T(8,128)S(1)}, u32[]{:S(2)}, u32[]{:S(2)}) collective-permute-start(f32[64,1024]{1,0:T(8,128)S(1)} %max.26), channel_id=1, source_target_pairs={{0,96},{1,97},{2,98},{3,99},{4,100},{5,101},{6,102},{7,103},{8,104... | collective-permute-start | bytes 786440 | tf_op jit(solution)/shard_map/ppermute | solution.py:45
  104.5 7.4 %collective-permute-start.13 = (f32[64,1024]{1,0:T(8,128)S(1)}, f32[64,1024]{1,0:T(8,128)S(1)}, u32[]{:S(2)}, u32[]{:S(2)}) collective-permute-start(f32[64,1024]{1,0:T(8,128)S(1)} %max.31), channel_id=1, source_target_pairs={{0,32},{1,33},{2,34},{3,35},{4,36},{5,37},{6,38},{7,39},{8,40},{9,... | collective-permute-start | bytes 786440 | tf_op jit(solution)/shard_map/ppermute | solution.py:45
  105.3 7.1 %collective-permute-start.8 = (f32[64,1024]{1,0:T(8,128)S(1)}, f32[64,1024]{1,0:T(8,128)S(1)}, u32[]{:S(2)}, u32[]{:S(2)}) collective-permute-start(f32[64,1024]{1,0:T(8,128)S(1)} %max.27), channel_id=1, source_target_pairs={{0,8},{1,9},{2,10},{3,11},{4,12},{5,13},{6,14},{7,15},{8,0},{9,1},... | collective-permute-start | bytes 786440 | tf_op jit(solution)/shard_map/ppermute | solution.py:45

commit v6 on v5

--- a/solution.py
+++ b/solution.py
@@ -24,32 +24,28 @@
     return pl.BlockSpec(memory_space=pltpu.SMEM)
 
 
-PAIRINGS = (
-    (("y", 1), ("y", 3), ("x", 1), ("x", 3)),
-    (("x", 1), ("x", 3), ("y", 1), ("y", 3)),
-)
-
-
-def pairs(piece, number, tiles):
+def first_place():
+    depth = lax.axis_index("depth")
+    return jnp.where(lax.axis_index("tile") % 2 == 0, depth % SIDE, depth // SIDE)
+
+
+def shifts(stage, k, tiles):
     result = []
     for x in range(SIDE):
         for y in range(SIDE):
             for tile in range(tiles):
-                axis, flip = PAIRINGS[piece][number]
-                tx, ty = (x, y ^ flip) if axis == "y" else (x ^ flip, y)
+                along_y = (tile % 2 == 0) == (stage == 0)
+                tx, ty = (x, (y + k) % SIDE) if along_y else ((x + k) % SIDE, y)
                 result.append(((x * SIDE + y) * tiles + tile, (tx * SIDE + ty) * tiles + tile))
     return result
 
 
-def swap(value, piece, number):
-    return lax.ppermute(value, ("depth", "tile"), pairs(piece, number, lax.axis_size("tile")))
-
-
-def side(piece):
-    depth = lax.axis_index("depth")
-    axis, _ = PAIRINGS[piece][0]
-    value = depth % SIDE if axis == "y" else depth // SIDE
-    return (value + 1) // 2 % 2
+def around(stage, parts):
+    tiles = lax.axis_size("tile")
+    got = [parts[0]] + [None] * (SIDE - 1)
+    for k in (2, 1, 3):
+        got[k] = lax.ppermute(parts[k], ("depth", "tile"), shifts(stage, k, tiles))
+    return got
 
 
 def split(value):
@@ -160,16 +156,21 @@
     return lax.optimization_barrier((above, made))
 
 
+def top_of_four(parts):
+    return jnp.maximum(jnp.maximum(parts[0], parts[1]), jnp.maximum(parts[2], parts[3]))
+
+
 def highest(parts):
-    joined = []
-    held = [jnp.maximum(keep, swap(give, piece, 0)) for piece, (keep, give) in enumerate(parts)]
-    for number in range(1, 4):
-        held = [jnp.maximum(value, swap(value, piece, number)) for piece, value in enumerate(held)]
-    for piece, mine in enumerate(held):
-        other = swap(mine, piece, 0)
-        first = side(piece) == 0
-        joined += [jnp.where(first, mine, other), jnp.where(first, other, mine)]
-    return jnp.concatenate(joined)
+    mine = top_of_four(around(0, parts))
+    mine = top_of_four(around(1, [mine] * SIDE))
+    got = around(0, [mine] * SIDE)
+    first = first_place()
+    quarters = []
+    for j in range(SIDE):
+        back = (first - j + SIDE) % SIDE
+        near = jnp.where(back == 0, got[0], got[1])
+        quarters.append(jnp.where(back < 2, near, jnp.where(back == 2, got[2], got[3])))
+    return jnp.concatenate(quarters)
 
 
 def bands_kernel(stratum, taps, v_ref, l_ref):
@@ -323,11 +324,8 @@
 
     @pl.when(plane == pl.num_programs(0) - 1)
     def _():
-        quarter = rows // 4
-        for piece, (keep, give) in enumerate(((o0, o1), (o2, o3))):
-            kept = side(piece)
-            keep[...] = top[rows_at(2 * piece + kept, quarter)]
-            give[...] = top[rows_at(2 * piece + 1 - kept, quarter)]
+        for k, out in enumerate((o0, o1, o2, o3)):
+            out[...] = top[rows_at(lax.rem(first_place() + k, SIDE), rows // SIDE)]
 
 
 def step(seams, ext, est, mea, above, above_across, above_beside, rim_across, rim_beside, v, l):
@@ -382,10 +380,10 @@
 
     above_across = lax.ppermute(rim_of(~first_core), "tile", across)
     above_beside = lax.ppermute(rim_of(first_core), "tile", beside)
-    updated, keep_a, give_a, keep_b, give_b = step(
+    updated, *tops = step(
         seam_flags, extinction, estimate, measured, above, above_across, above_beside, rim_across, rim_beside, v, l
     )
-    return updated, highest([(keep_a, give_a), (keep_b, give_b)])
+    return updated, highest(tops)
 
 
 def solution(mesh):

time: 114 us -> 115 us (level)
  the two profiles are of different devices: /device:TPU:0 before, /device:TPU:96 now
where the time goes in v6:
time: 115 us
  waiting for transfers between devices  55.9 us (49%)
  Pallas kernels  28.1 us (24%)
  starting transfers between devices  27.9 us (24%)
  other arithmetic  2.07 us (2%)
    ppermute x9, waiting for transfers between devices, around(): got[k] = lax.ppermute(parts[k], ('depth', 'tile'), shifts(stage, k, tiles))  29.4 us
    pallas_call x1, Pallas kernels, step(): pl.pallas_call(step_kernel, grid=(planes,), in_specs=[smem(), stack, stac...  14.8 us
    ppermute x9, starting transfers between devices, around(): got[k] = lax.ppermute(parts[k], ('depth', 'tile'), shifts(stage, k, tiles))  13.1 us
    all_to_all x1, waiting for transfers between devices, above_of(): parts = lax.all_to_all(parts, 'depth', 0, 0, tiled=True)  11.3 us
    all_to_all x1, waiting for transfers between devices, above_of(): lax.all_to_all(prefixes, 'depth', 0, 0, tiled=True).reshape(rows, cols)  9.54 us
    all_to_all x1, starting transfers between devices, above_of(): parts = lax.all_to_all(parts, 'depth', 0, 0, tiled=True)  7.05 us
    ppermute x1, waiting for transfers between devices, on_device(): above_across = lax.ppermute(rim_of(~first_core), 'tile', across)  5.65 us
    pallas_call x1, Pallas kernels, bands(): pl.pallas_call(bands_kernel, grid_spec=pltpu.PrefetchScalarGridSpec(num_s...  4.8 us
  transfers between devices with their start and end apart: 15, of which 8 were waited for; matrix products, arithmetic and copies ran while one was open for 1% of the time, Pallas kernels for 9%

profile of v6, /device:TPU:96, one launch (start us, length us, event | category | flops | bytes accessed | tf_op | source)
XLA Modules:
  0.0 115.0 jit_solution(901652543319359466)
XLA Ops:
  0.6 3.2 %shard_map.86 = f32[256,1024]{1,0:T(8,128)} custom-call(f32[4,256,1024]{2,1,0:T(8,128)} %ext.5), custom_call_target="tpu_custom_call" | custom-call | tf_op jit(solution)/shard_map/pallas_call | solution.py:78
  3.9 7.0 %all-to-all-start = ((f32[16,16,1024]{2,1,0:T(8,128)}), f32[16,16,1024]{2,1,0:T(8,128)S(1)}, u32[]{:S(2)}, u32[]{:S(2)}) async-start(f32[16,16,1024]{2,1,0:T(8,128)} %bitcast.8), calls=%async_computation | async-start | bytes 2097152 | tf_op jit(solution)/shard_map/all_to_all | solution.py:145
  10.9 4.2 %shard_map.89 = (f32[4,96,1024]{2,1,0:T(8,128)}, f32[4,96,1024]{2,1,0:T(8,128)}) custom-call(f32[4,256,1024]{2,1,0:T(8,128)} %ext.5, f32[4,256,1024]{2,1,0:T(8,128)} %est.3, f32[4,256,1024]{2,1,0:T(8,128)} %mea.3), custom_call_target="tpu_custom_call" | custom-call | flops 1048576 | bytes 8388608 | tf_op jit(solution)/shard_map/pallas_call | solution.py:117
  15.1 0.0 copy-start.2
  15.1 0.0 copy-start.1
  15.1 0.0 copy-start
  15.2 2.1 %collective-permute-start.2 = (f32[4,96,1024]{2,1,0:T(8,128)}, f32[4,96,1024]{2,1,0:T(8,128)S(1)}, u32[]{:S(2)}, u32[]{:S(2)}) collective-permute-start(f32[4,96,1024]{2,1,0:T(8,128)} %get-tuple-element.25), channel_id=1, source_target_pairs={{1,2},{2,1},{3,4},{4,3},{5,6},{6,5},{9,10},{10,9},{11,12},{12,11},... | collective-permute-start | bytes 4718600 | tf_op jit(solution)/shard_map/ppermute | solution.py:375
  17.2 0.1 collective-permute-start.3
  17.3 11.3 %all-to-all-done.parts = f32[16,16,1024]{2,1,0:T(8,128)S(1)} async-done(((f32[16,16,1024]{2,1,0:T(8,128)}), f32[16,16,1024]{2,1,0:T(8,128)S(1)}, u32[]{:S(2)}, u32[]{:S(2)}) %all-to-all-start) | async-done | bytes 1048608 | tf_op jit(solution)/shard_map/all_to_all | solution.py:145
  28.6 1.0 shard_map.87
  29.6 3.7 %all-to-all-start.1 = ((f32[16,16,1024]{2,1,0:T(8,128)}), f32[16,16,1024]{2,1,0:T(8,128)S(1)}, u32[]{:S(2)}, u32[]{:S(2)}) async-start(f32[16,16,1024]{2,1,0:T(8,128)} %shard_map.87), calls=%async_computation.1 | async-start | bytes 2097152 | tf_op jit(solution)/shard_map/all_to_all | solution.py:155
  33.3 0.0 copy-done.2
  33.3 0.1 rev.6
  33.4 0.0 copy-done.1
  33.4 0.1 rev.7
  33.5 0.7 select_maximum_fusion.taps
  34.2 4.8 %shard_map.88 = (bf16[4,2,2,192,256]{4,3,2,1,0:T(8,128)(2,1)}, bf16[4,2,768,256]{3,2,1,0:T(8,128)(2,1)}) custom-call(s32[4]{0:T(128)} %stratum, f32[16,4,256]{2,1,0:T(4,128)} %select_maximum_fusion.taps), custom_call_target="tpu_custom_call" | custom-call | flops 4194304 | bytes 6291456 | tf_op jit(solution)/shard_map/pallas_call | solution.py:205
  39.0 9.5 %all-to-all-done.1 = f32[16,16,1024]{2,1,0:T(8,128)S(1)} async-done(((f32[16,16,1024]{2,1,0:T(8,128)}), f32[16,16,1024]{2,1,0:T(8,128)S(1)}, u32[]{:S(2)}, u32[]{:S(2)}) %all-to-all-start.1) | async-done | bytes 1048608 | tf_op jit(solution)/shard_map/all_to_all | solution.py:155
  48.6 1.9 %collective-permute-start = (f32[64,1024]{1,0:T(8,128)S(1)}, f32[64,1024]{1,0:T(8,128)S(1)}, u32[]{:S(2)}, u32[]{:S(2)}) collective-permute-start(f32[64,1024]{1,0:T(8,128)S(1)} %get-tuple-element.39), channel_id=1, source_target_pairs={{1,2},{2,1},{3,4},{4,3},{5,6},{6,5},{9,10},{10,9},{11,12},{12,11},... | collective-permute-start | bytes 786440 | tf_op jit(solution)/shard_map/ppermute | solution.py:381
  50.5 0.1 collective-permute-start.1
  50.6 0.0 collective-permute-done.2.rim_across
  50.6 0.0 collective-permute-done.3.rim_beside
  50.6 5.6 %collective-permute-done.above_across = f32[64,1024]{1,0:T(8,128)S(1)} collective-permute-done((f32[64,1024]{1,0:T(8,128)S(1)}, f32[64,1024]{1,0:T(8,128)S(1)}, u32[]{:S(2)}, u32[]{:S(2)}) %collective-permute-start) | collective-permute-done | bytes 262176 | tf_op jit(solution)/shard_map/ppermute | solution.py:381
  56.3 0.0 collective-permute-done.1.above_beside
  56.3 0.0 copy-done
  56.3 14.8 %shard_map.90 = (f32[4,256,1024]{2,1,0:T(8,128)}, f32[64,1024]{1,0:T(8,128)S(1)}, f32[64,1024]{1,0:T(8,128)S(1)}, f32[64,1024]{1,0:T(8,128)S(1)}, f32[64,1024]{1,0:T(8,128)S(1)}) custom-call(s32[7]{0:T(128)S(1)} %copy-done, f32[4,256,1024]{2,1,0:T(8,128)} %ext.5, f32[4,256,1024]{2,1,0:T(8,128)} %est.3, f32[4,256,1024]{2,1,0:T(8,128)} %mea.3, ...), custom_call_target="tpu_custom_call" | custom-call | flops 12884901888 | bytes 25165824 | tf_op jit(solution)/shard_map/pallas_call | solution.py:337
  71.1 0.6 collective-permute-start.4
  71.7 1.9 %collective-permute-start.5 = (f32[64,1024]{1,0:T(8,128)S(1)}, f32[64,1024]{1,0:T(8,128)S(1)}, u32[]{:S(2)}, u32[]{:S(2)}) collective-permute-start(f32[64,1024]{1,0:T(8,128)S(1)} %get-tuple-element.32), channel_id=1, source_target_pairs={{0,16},{1,65},{2,18},{3,67},{4,20},{5,69},{6,22},{7,71},{8,24},{9,... | collective-permute-start | bytes 786440 | tf_op jit(solution)/shard_map/ppermute | solution.py:47
  73.6 1.1 collective-permute-start.6
  74.7 7.0 %collective-permute-done.4 = f32[64,1024]{1,0:T(8,128)S(1)} collective-permute-done((f32[64,1024]{1,0:T(8,128)S(1)}, f32[64,1024]{1,0:T(8,128)S(1)}, u32[]{:S(2)}, u32[]{:S(2)}) %collective-permute-start.4) | collective-permute-done | bytes 262176 | tf_op jit(solution)/shard_map/ppermute | solution.py:47
  81.7 0.0 collective-permute-done.5
  81.7 3.0 %collective-permute-done.6 = f32[64,1024]{1,0:T(8,128)S(1)} collective-permute-done((f32[64,1024]{1,0:T(8,128)S(1)}, f32[64,1024]{1,0:T(8,128)S(1)}, u32[]{:S(2)}, u32[]{:S(2)}) %collective-permute-start.6) | collective-permute-done | bytes 262176 | tf_op jit(solution)/shard_map/ppermute | solution.py:47
  84.7 0.1 maximum_maximum_fusion.1
  84.8 0.1 collective-permute-start.7
  84.9 0.4 collective-permute-start.8
  85.3 2.8 %collective-permute-start.9 = (f32[64,1024]{1,0:T(8,128)S(1)}, f32[64,1024]{1,0:T(8,128)S(1)}, u32[]{:S(2)}, u32[]{:S(2)}) collective-permute-start(f32[64,1024]{1,0:T(8,128)S(1)} %maximum_maximum_fusion.1), channel_id=1, source_target_pairs={{0,96},{1,25},{2,98},{3,27},{4,100},{5,29},{6,102},{7,31},{8,104},... | collective-permute-start | bytes 786440 | tf_op jit(solution)/shard_map/ppermute | solution.py:47
  88.1 12.2 %collective-permute-done.7 = f32[64,1024]{1,0:T(8,128)S(1)} collective-permute-done((f32[64,1024]{1,0:T(8,128)S(1)}, f32[64,1024]{1,0:T(8,128)S(1)}, u32[]{:S(2)}, u32[]{:S(2)}) %collective-permute-start.7) | collective-permute-done | bytes 262176 | tf_op jit(solution)/shard_map/ppermute | solution.py:47
  100.3 0.0 collective-permute-done.8
  100.3 0.0 collective-permute-done.9
  100.3 0.1 maximum_maximum_fusion
  100.4 0.1 collective-permute-start.10
  100.4 6.1 %collective-permute-start.11 = (f32[64,1024]{1,0:T(8,128)S(1)}, f32[64,1024]{1,0:T(8,128)S(1)}, u32[]{:S(2)}, u32[]{:S(2)}) collective-permute-start(f32[64,1024]{1,0:T(8,128)S(1)} %maximum_maximum_fusion), channel_id=1, source_target_pairs={{0,16},{1,65},{2,18},{3,67},{4,20},{5,69},{6,22},{7,71},{8,24},{9,... | collective-permute-start | bytes 786440 | tf_op jit(solution)/shard_map/ppermute | solution.py:47
  106.6 0.0 collective-permute-start.12
  106.6 2.9 %collective-permute-done.10 = f32[64,1024]{1,0:T(8,128)S(1)} collective-permute-done((f32[64,1024]{1,0:T(8,128)S(1)}, f32[64,1024]{1,0:T(8,128)S(1)}, u32[]{:S(2)}, u32[]{:S(2)}) %collective-permute-start.10) | collective-permute-done | bytes 262176 | tf_op jit(solution)/shard_map/ppermute | solution.py:47
  109.5 4.3 %collective-permute-done.11 = f32[64,1024]{1,0:T(8,128)S(1)} collective-permute-done((f32[64,1024]{1,0:T(8,128)S(1)}, f32[64,1024]{1,0:T(8,128)S(1)}, u32[]{:S(2)}, u32[]{:S(2)}) %collective-permute-start.11) | collective-permute-done | bytes 262176 | tf_op jit(solution)/shard_map/ppermute | solution.py:47
  113.7 0.0 collective-permute-done.12
  113.7 0.1 select_select_fusion.3
  113.9 1.1 pad_maximum_fusion
  (1 shorter events, 0.0 us)
Async XLA Ops:
  3.9 24.8 %all-to-all-start = ((f32[16,16,1024]{2,1,0:T(8,128)}), f32[16,16,1024]{2,1,0:T(8,128)S(1)}, u32[]{:S(2)}, u32[]{:S(2)}) async-start(f32[16,16,1024]{2,1,0:T(8,128)} %bitcast.8), calls=%async_computation | async-start | bytes 2097152 | tf_op jit(solution)/shard_map/all_to_all | solution.py:145
  15.1 18.2 %copy-start.2 = (f32[16,65]{1,0:T(8,128)S(1)}, f32[16,65]{1,0:T(8,128)}, u32[]{:S(2)}) copy-start(f32[16,65]{1,0:T(8,128)} %param.10) | copy-start | bytes 12484
  15.1 18.3 %copy-start.1 = (f32[16,65]{1,0:T(8,128)S(1)}, f32[16,65]{1,0:T(8,128)}, u32[]{:S(2)}) copy-start(f32[16,65]{1,0:T(8,128)} %param.11) | copy-start | bytes 12484
  15.1 41.1 %copy-start = (s32[7]{0:T(128)S(1)}, s32[7]{0:T(128)}, u32[]{:S(2)}) copy-start(s32[7]{0:T(128)} %seams.1) | copy-start | bytes 88
  15.2 35.4 %collective-permute-start.2 = (f32[4,96,1024]{2,1,0:T(8,128)}, f32[4,96,1024]{2,1,0:T(8,128)S(1)}, u32[]{:S(2)}, u32[]{:S(2)}) collective-permute-start(f32[4,96,1024]{2,1,0:T(8,128)} %get-tuple-element.25), channel_id=1, source_target_pairs={{1,2},{2,1},{3,4},{4,3},{5,6},{6,5},{9,10},{10,9},{11,12},{12,11},... | collective-permute-start | bytes 4718600 | tf_op jit(solution)/shard_map/ppermute | solution.py:375
  17.2 33.4 %collective-permute-start.3 = (f32[4,96,1024]{2,1,0:T(8,128)}, f32[4,96,1024]{2,1,0:T(8,128)}, u32[]{:S(2)}, u32[]{:S(2)}) collective-permute-start(f32[4,96,1024]{2,1,0:T(8,128)} %get-tuple-element.26), channel_id=1, source_target_pairs={{0,1},{1,0},{2,3},{3,2},{4,5},{5,4},{6,7},{7,6},{8,9},{9,8},{10,11... | collective-permute-start | bytes 4718600 | tf_op jit(solution)/shard_map/ppermute | solution.py:376
  29.6 18.9 %all-to-all-start.1 = ((f32[16,16,1024]{2,1,0:T(8,128)}), f32[16,16,1024]{2,1,0:T(8,128)S(1)}, u32[]{:S(2)}, u32[]{:S(2)}) async-start(f32[16,16,1024]{2,1,0:T(8,128)} %shard_map.87), calls=%async_computation.1 | async-start | bytes 2097152 | tf_op jit(solution)/shard_map/all_to_all | solution.py:155
  48.6 7.7 %collective-permute-start = (f32[64,1024]{1,0:T(8,128)S(1)}, f32[64,1024]{1,0:T(8,128)S(1)}, u32[]{:S(2)}, u32[]{:S(2)}) collective-permute-start(f32[64,1024]{1,0:T(8,128)S(1)} %get-tuple-element.39), channel_id=1, source_target_pairs={{1,2},{2,1},{3,4},{4,3},{5,6},{6,5},{9,10},{10,9},{11,12},{12,11},... | collective-permute-start | bytes 786440 | tf_op jit(solution)/shard_map/ppermute | solution.py:381
  50.5 5.8 %collective-permute-start.1 = (f32[64,1024]{1,0:T(8,128)S(1)}, f32[64,1024]{1,0:T(8,128)S(1)}, u32[]{:S(2)}, u32[]{:S(2)}) collective-permute-start(f32[64,1024]{1,0:T(8,128)S(1)} %get-tuple-element.38), channel_id=1, source_target_pairs={{0,1},{1,0},{2,3},{3,2},{4,5},{5,4},{6,7},{7,6},{8,9},{9,8},{10,11... | collective-permute-start | bytes 786440 | tf_op jit(solution)/shard_map/ppermute | solution.py:382
  71.1 10.6 %collective-permute-start.4 = (f32[64,1024]{1,0:T(8,128)S(1)}, f32[64,1024]{1,0:T(8,128)S(1)}, u32[]{:S(2)}, u32[]{:S(2)}) collective-permute-start(f32[64,1024]{1,0:T(8,128)S(1)} %get-tuple-element.31), channel_id=1, source_target_pairs={{0,8},{1,33},{2,10},{3,35},{4,12},{5,37},{6,14},{7,39},{8,16},{9,4... | collective-permute-start | bytes 786440 | tf_op jit(solution)/shard_map/ppermute | solution.py:47
  71.7 10.1 %collective-permute-start.5 = (f32[64,1024]{1,0:T(8,128)S(1)}, f32[64,1024]{1,0:T(8,128)S(1)}, u32[]{:S(2)}, u32[]{:S(2)}) collective-permute-start(f32[64,1024]{1,0:T(8,128)S(1)} %get-tuple-element.32), channel_id=1, source_target_pairs={{0,16},{1,65},{2,18},{3,67},{4,20},{5,69},{6,22},{7,71},{8,24},{9,... | collective-permute-start | bytes 786440 | tf_op jit(solution)/shard_map/ppermute | solution.py:47
  73.6 11.1 %collective-permute-start.6 = (f32[64,1024]{1,0:T(8,128)S(1)}, f32[64,1024]{1,0:T(8,128)S(1)}, u32[]{:S(2)}, u32[]{:S(2)}) collective-permute-start(f32[64,1024]{1,0:T(8,128)S(1)} %get-tuple-element.33), channel_id=1, source_target_pairs={{0,24},{1,97},{2,26},{3,99},{4,28},{5,101},{6,30},{7,103},{8,0},{9... | collective-permute-start | bytes 786440 | tf_op jit(solution)/shard_map/ppermute | solution.py:47
  84.8 15.5 %collective-permute-start.7 = (f32[64,1024]{1,0:T(8,128)S(1)}, f32[64,1024]{1,0:T(8,128)S(1)}, u32[]{:S(2)}, u32[]{:S(2)}) collective-permute-start(f32[64,1024]{1,0:T(8,128)S(1)} %maximum_maximum_fusion.1), channel_id=1, source_target_pairs={{0,32},{1,9},{2,34},{3,11},{4,36},{5,13},{6,38},{7,15},{8,40},{9,1... | collective-permute-start | bytes 786440 | tf_op jit(solution)/shard_map/ppermute | solution.py:47
  84.9 15.4 %collective-permute-start.8 = (f32[64,1024]{1,0:T(8,128)S(1)}, f32[64,1024]{1,0:T(8,128)S(1)}, u32[]{:S(2)}, u32[]{:S(2)}) collective-permute-start(f32[64,1024]{1,0:T(8,128)S(1)} %maximum_maximum_fusion.1), channel_id=1, source_target_pairs={{0,64},{1,17},{2,66},{3,19},{4,68},{5,21},{6,70},{7,23},{8,72},{9,... | collective-permute-start | bytes 786440 | tf_op jit(solution)/shard_map/ppermute | solution.py:47
  85.3 15.0 %collective-permute-start.9 = (f32[64,1024]{1,0:T(8,128)S(1)}, f32[64,1024]{1,0:T(8,128)S(1)}, u32[]{:S(2)}, u32[]{:S(2)}) collective-permute-start(f32[64,1024]{1,0:T(8,128)S(1)} %maximum_maximum_fusion.1), channel_id=1, source_target_pairs={{0,96},{1,25},{2,98},{3,27},{4,100},{5,29},{6,102},{7,31},{8,104},... | collective-permute-start | bytes 786440 | tf_op jit(solution)/shard_map/ppermute | solution.py:47
  100.4 9.1 %collective-permute-start.10 = (f32[64,1024]{1,0:T(8,128)S(1)}, f32[64,1024]{1,0:T(8,128)S(1)}, u32[]{:S(2)}, u32[]{:S(2)}) collective-permute-start(f32[64,1024]{1,0:T(8,128)S(1)} %maximum_maximum_fusion), channel_id=1, source_target_pairs={{0,8},{1,33},{2,10},{3,35},{4,12},{5,37},{6,14},{7,39},{8,16},{9,4... | collective-permute-start | bytes 786440 | tf_op jit(solution)/shard_map/ppermute | solution.py:47
  100.4 13.3 %collective-permute-start.11 = (f32[64,1024]{1,0:T(8,128)S(1)}, f32[64,1024]{1,0:T(8,128)S(1)}, u32[]{:S(2)}, u32[]{:S(2)}) collective-permute-start(f32[64,1024]{1,0:T(8,128)S(1)} %maximum_maximum_fusion), channel_id=1, source_target_pairs={{0,16},{1,65},{2,18},{3,67},{4,20},{5,69},{6,22},{7,71},{8,24},{9,... | collective-permute-start | bytes 786440 | tf_op jit(solution)/shard_map/ppermute | solution.py:47
  106.6 7.2 %collective-permute-start.12 = (f32[64,1024]{1,0:T(8,128)S(1)}, f32[64,1024]{1,0:T(8,128)S(1)}, u32[]{:S(2)}, u32[]{:S(2)}) collective-permute-start(f32[64,1024]{1,0:T(8,128)S(1)} %maximum_maximum_fusion), channel_id=1, source_target_pairs={{0,24},{1,97},{2,26},{3,99},{4,28},{5,101},{6,30},{7,103},{8,0},{9... | collective-permute-start | bytes 786440 | tf_op jit(solution)/shard_map/ppermute | solution.py:47
